TPU v7x, 128 devices: a whole 4x4x4 slice. The times are simulated.
128 devices in a mesh: outer: 16 (over z_hi, x, core), inner: 8 (over z_lo, y).
Axes of the slice: x: 4, y: 4, z: 4 (z_hi: 2, z_lo: 2; z = z_hi * 2 + z_lo), core: 2. Of those that a mesh axis runs over, the one named last changes fastest.
Arguments:
- tokens: bfloat16 [49152, 8192], P(('outer', 'inner')), may hold values from -6 to 6
- queries: bfloat16 [49152, 4096], P(('outer', 'inner')), may hold values from -6 to 6
- values: bfloat16 [49152, 512], P(('outer', 'inner')), may hold values from -6 to 6
- doc_ids: int32 [128, 384], P(('outer', 'inner')), may hold values from 0 to 3, never falling along the last dimension, each value on 1 to 192 neighbouring positions
- weight_codes: bfloat16 [8192, 512], P(('inner', 'outer')), may hold values from -15 to 15, as said below
- weight_scales: int32 [256, 512], P(('inner', 'outer')), may hold values from -11 to -8
- out_grad: bfloat16 [49152, 4096], P(('outer', 'inner')), may hold values from -6 to 6
Outputs:
- attn_out: bfloat16 [49152, 4096], P(('outer', 'inner'))
- grad_tokens: bfloat16 [49152, 8192], P(('outer', 'inner'))
- grad_weight: float32 [8192, 512], P(('inner', 'outer'))
Inputs may be any that keep to these rules, and one draw needn't show every extreme that they name: `weight_codes`: each entry is plus or minus (1 + m / 8) * 2 ** e with whole m of 0 to 7 and e of -2 to 3.
All inputs are finite; a program needn't handle non-finite values.
Results may differ from a plain program's by a relative error of at most 0.023.
Values may be sent and summed in bfloat16 or wider, within the bound.
No kernel may reach another device: no remote copies, remote signals or barrier semaphores. Data moves between devices by JAX's collectives and lax.ppermute only.
A program may use at most 192 MiB of HBM per device.

v0:
```python
import jax
import jax.numpy as jnp
from jax import lax
from jax.sharding import PartitionSpec as P

HD = 128


def dequantize(codes, scales):
    factor = jnp.exp2(scales.astype(jnp.float32))
    rows = codes.shape[0]
    expanded = (
        codes.astype(jnp.float32).reshape(rows // 32, 32, codes.shape[1]) * factor[:, None, :]
    )
    return expanded.reshape(rows, codes.shape[1]).astype(jnp.bfloat16)


def per_device(tokens, queries, values, doc_ids, weight_codes, weight_scales, out_grad):
    seq_len = tokens.shape[0]
    key_cols = weight_codes.shape[1]
    kv_heads = key_cols // HD
    group_size = queries.shape[1] // key_cols
    scale = HD ** (-0.5)
    tokens_full = tokens.astype(jnp.float32)
    inverse_rms = lax.rsqrt(jnp.mean(tokens_full * tokens_full, axis=-1, keepdims=True) + 1e-05)
    hat = tokens_full * inverse_rms
    normed = hat.astype(jnp.bfloat16)
    secondary = (
        lax.all_gather(weight_codes, "outer", axis=0, tiled=True),
        lax.all_gather(weight_scales, "outer", axis=0, tiled=True),
    )
    pieces = (
        lax.all_gather(secondary[0], "inner", axis=0, tiled=True),
        lax.all_gather(secondary[1], "inner", axis=0, tiled=True),
    )
    piece_weight = dequantize(pieces[0], pieces[1])
    columns = normed
    keys_full = jnp.dot(columns, piece_weight, preferred_element_type=jnp.float32)
    keys = keys_full.astype(jnp.bfloat16)
    query_heads = queries.reshape(seq_len, kv_heads, group_size, HD)
    key_heads = keys.reshape(seq_len, kv_heads, HD)
    value_heads = values.reshape(seq_len, kv_heads, HD)
    grad_heads = out_grad.reshape(seq_len, kv_heads, group_size, HD)
    doc_row = doc_ids.reshape(seq_len)
    positions = jnp.arange(seq_len)
    allowed = (doc_row[:, None] == doc_row[None, :]) & (positions[:, None] >= positions[None, :])
    scores = (
        jnp.einsum("tkgd,skd->kgts", query_heads, key_heads, preferred_element_type=jnp.float32)
        * scale
    )
    scores = jnp.where(allowed, scores, -1e30)
    row_max = jnp.max(scores, axis=-1, keepdims=True)
    unnormed = jnp.exp(scores - row_max)
    attn_probs = unnormed / jnp.sum(unnormed, axis=-1, keepdims=True)
    probs_low = attn_probs.astype(jnp.bfloat16)
    output = jnp.einsum(
        "kgts,skd->tkgd", probs_low, value_heads, preferred_element_type=jnp.float32
    )
    attn_out = output.reshape(seq_len, queries.shape[1]).astype(jnp.bfloat16)
    dprobs = jnp.einsum(
        "tkgd,skd->kgts", grad_heads, value_heads, preferred_element_type=jnp.float32
    )
    delta = jnp.sum(attn_probs * dprobs, axis=-1, keepdims=True)
    score_grad = (attn_probs * (dprobs - delta)).astype(jnp.bfloat16)
    key_grad = (
        jnp.einsum("kgts,tkgd->skd", score_grad, query_heads, preferred_element_type=jnp.float32)
        * scale
    )
    dkeys = key_grad.reshape(seq_len, key_cols).astype(jnp.bfloat16)
    columns = normed
    inner_share = lax.psum_scatter(
        lax.dot_general(
            columns, dkeys, (((0,), (0,)), ((), ())), preferred_element_type=jnp.float32
        ).astype(jnp.bfloat16),
        "inner",
        scatter_dimension=0,
        tiled=True,
    )
    grad_weight = lax.psum_scatter(inner_share, "outer", scatter_dimension=0, tiled=True).astype(
        jnp.float32
    )
    pieces = lax.all_gather((secondary[0], secondary[1]), "inner", axis=0, tiled=True)
    piece_weight = dequantize(pieces[0], pieces[1])
    dnormed = lax.dot_general(
        dkeys, piece_weight, (((1,), (1,)), ((), ())), preferred_element_type=jnp.float32
    )
    grad_tokens = (
        inverse_rms * (dnormed - hat * jnp.mean(dnormed * hat, axis=-1, keepdims=True))
    ).astype(jnp.bfloat16)
    return (attn_out, grad_tokens, grad_weight)


def solution(mesh):
    return jax.shard_map(
        per_device,
        mesh=mesh,
        in_specs=(
            P(("outer", "inner"), None),
            P(("outer", "inner"), None),
            P(("outer", "inner"), None),
            P(("outer", "inner"), None),
            P(("inner", "outer"), None),
            P(("inner", "outer"), None),
            P(("outer", "inner"), None),
        ),
        out_specs=(
            P(("outer", "inner"), None),
            P(("outer", "inner"), None),
            P(("inner", "outer"), None),
        ),
        check_vma=False,
    )
```

profile of v0, /device:TPU:1, one launch (start us, length us, event | category | flops | bytes accessed | tf_op | source)
XLA Modules:
  0.0 395.2 jit_solution(13303190276991439225)
XLA Ops:
  7.2 0.0 all-gather.4.cloned.1.call-start
  7.2 0.7 all-gather.4.cloned.1.call-update
  7.9 0.0 all-gather.6.cloned.1.call-start
  8.0 51.3 %all-gather.4.cloned.1.call-done = bf16[1024,512]{1,0:T(8,128)(2,1)} async-done(((bf16[64,512]{1,0:T(8,128)(2,1)}), bf16[1024,512]{1,0:T(8,128)(2,1)}) %all-gather.4.cloned.1.call-update) | async-done | bytes 1048592 | tf_op jit(solution)/shard_map/all_gather | solution.py:29
  59.2 0.0 all-gather.6.cloned.1.call-update
  59.3 0.0 reduce-scatter.3.cloned.1.call-start
  59.3 21.8 %all-gather = s32[16,2,512]{2,1,0:T(2,128)S(1)} all-gather(s32[1,2,512]{2,1,0:T(2,128)} %bitcast.69), channel_id=1, replica_groups=mesh['outer'=16,'inner'=8] {'outer'}, dimensions={0}, use_global_device_ids=true | all-gather | bytes 69632 | tf_op jit(solution)/shard_map/all_gather | solution.py:30
  81.1 0.7 reshape.49
  81.7 3.5 copy.40
  85.2 1.1 reshape.46
  86.3 4.5 %copy.41 = bf16[48,8,32,128]{3,2,1,0:T(8,128)(2,1)} copy(bf16[48,8,32,128]{3,1,2,0:T(8,128)(2,1)} %bitcast.59) | data formatting | bytes 6291456
  90.8 4.1 %fusion.13 = f32[384]{0:T(512)S(1)} fusion(bf16[384,8192]{1,0:T(8,128)(2,1)} %param.7), kind=kLoop, calls=%fused_computation.20 | loop fusion | flops 9436800 | bytes 6292992 | tf_op jit(solution)/shard_map/reduce_sum | solution.py:25
  94.9 0.8 fusion.44
  95.8 27.8 %all_gather.17 = s32[256,512]{1,0:T(8,128)S(1)} all-gather(s32[32,512]{1,0:T(8,128)} %reshape.49), channel_id=1, replica_groups=mesh['outer'=16,'inner'=8] {'inner'}, dimensions={0}, use_global_device_ids=true | all-gather | bytes 589824 | tf_op jit(solution)/shard_map/all_gather | solution.py:34
  123.5 0.9 multiply_exponential_fusion
  124.4 31.7 %all-gather.6.cloned.1.call-done = bf16[8192,512]{1,0:T(8,128)(2,1)} async-done(((bf16[1024,512]{1,0:T(8,128)(2,1)}), bf16[8192,512]{1,0:T(8,128)(2,1)}) %all-gather.6.cloned.1.call-update) | async-done | bytes 8388624 | tf_op jit(solution)/shard_map/all_gather | solution.py:33
  156.1 8.3 %fusion.4 = bf16[8192,512]{1,0:T(8,128)(2,1)} fusion(bf16[8192,512]{1,0:T(8,128)(2,1)} %all-gather.6.cloned.1.call-done, f32[256,512]{1,0:T(8,128)} %multiply_exponential_fusion), kind=kLoop, calls=%fused_computation.9 | loop fusion | flops 12582912 | bytes 17301504 | tf_op jit(solution)/shard_map/convert_element_type | solution.py:15
  164.4 9.4 %fusion.38 = bf16[384,512]{1,0:T(8,128)(2,1)} fusion(bf16[8192,512]{1,0:T(8,128)(2,1)} %fusion.4, bf16[384,8192]{1,0:T(8,128)(2,1)} %param.7, f32[384]{0:T(512)S(1)} %add_rsqrt_fusion), kind=kOutput, calls=%fused_computation.37 | convolution fusion | flops 3230859264 | bytes 15074816 | tf_op jit(solution)/shard_map/dot_general | solution.py:38
  173.8 1.8 reshape.44
  175.6 12.1 %fusion.56 = (f32[4,8,384]{2,1,0:T(8,128)}, f32[4,8,384,384]{2,3,1,0:T(8,128)}) fusion(pred[384,384]{0,1:T(8,128)(4,1)} %fusion.44, bf16[384,4,8,128]{0,3,2,1:T(8,128)(2,1)S(1)} %bitcast.60, bf16[384,4,128,1]{2,1,0,3:T(4,128)(2,1)} %bitcast.66), kind=kOutput, calls=%fused_computation.51 | convolution fusion | flops 1226834304 | bytes 22609920 | tf_op jit(solution)/shard_map/sub | solution.py:53
  187.7 15.5 %fusion.1 = (f32[4,8,384]{2,1,0:T(8,128)}, f32[4,384,384,8]{2,1,3,0:T(8,128)}) fusion(f32[4,8,384,384]{2,3,1,0:T(8,128)} %get-tuple-element.10, f32[4,8,384]{2,1,0:T(8,128)} %get-tuple-element.9, bf16[384,4,8,128]{3,2,1,0:T(8,128)(2,1)} %bitcast.62, bf16[384,4,128,1]{2,1,0,3:T(4,128)(2,1)S(1)} %bitcast.64), kind=kOutput, calls=%fused_computation.3 | convolution fusion | flops 1222103040 | bytes 41385984 | tf_op jit(solution)/shard_map/tkgd,skd->kgts/dot_general | solution.py:60
  203.2 14.1 %fusion.41 = bf16[4,384,128]{1,2,0:T(8,128)(2,1)} fusion(bf16[384,4,8,128]{0,3,2,1:T(8,128)(2,1)S(1)} %bitcast.61, f32[4,384,384,8]{2,1,3,0:T(8,128)} %get-tuple-element.12, f32[4,8,384]{2,1,0:T(8,128)} %get-tuple-element.11, f32[4,8,384,384]{2,3,1,0:T(8,128)} %get-tuple-element.10, f32[4,8,384]{2,1,0:T(8,128)} %get-tuple-element.9), kind=kOutput, calls=%fused_computation.38 | convolution fusion | flops 1227227136 | bytes 41385984 | tf_op jit(solution)/shard_map/kgts,tkgd->skd/dot_general | solution.py:66
  217.3 11.0 %convolution_convert_fusion = bf16[8192,512]{1,0:T(8,128)(2,1)} fusion(bf16[384,512]{0,1:T(8,128)(2,1)} %bitcast.67, bf16[384,8192]{1,0:T(8,128)(2,1)} %param.7, f32[384]{0:T(512)S(1)} %add_rsqrt_fusion), kind=kOutput, calls=%fused_computation.21 | convolution fusion | flops 3234856960 | bytes 15074816 | tf_op jit(solution)/shard_map/dot_general | solution.py:72
  228.3 0.0 reduce-scatter.3.cloned.1.call-update
  228.3 0.0 reduce-scatter.5.cloned.1.call-start
  228.4 8.4 %fusion.27 = bf16[4,8,384,128]{2,3,1,0:T(8,128)(2,1)S(1)} fusion(bf16[384,4,128,1]{2,1,0,3:T(4,128)(2,1)S(1)} %bitcast.65, f32[4,8,384,384]{2,3,1,0:T(8,128)} %get-tuple-element.10, f32[4,8,384]{2,1,0:T(8,128)} %get-tuple-element.9), kind=kOutput, calls=%fused_computation.33 | convolution fusion | flops 1218969600 | bytes 22462464 | tf_op jit(solution)/shard_map/kgts,skd->tkgd/dot_general | solution.py:56
  236.8 3.1 copy.27
  239.9 14.8 %fusion.9 = (f32[384]{0:T(512)S(1)}, f32[384,8192]{1,0:T(8,128)}) fusion(bf16[384,8192]{1,0:T(8,128)(2,1)} %param.7, f32[384]{0:T(512)S(1)} %add_rsqrt_fusion, bf16[384,512]{0,1:T(8,128)(2,1)} %bitcast.68, bf16[8192,512]{1,0:T(8,128)(2,1)} %fusion.4), kind=kOutput, calls=%fused_computation.16 | convolution fusion | flops 3233807872 | bytes 27659264 | tf_op jit(solution)/shard_map/dot_general | solution.py:84
  254.8 65.1 %reduce-scatter.3.cloned.1.call-done = bf16[1024,512]{1,0:T(8,128)(2,1)} async-done(((bf16[8192,512]{1,0:T(8,128)(2,1)}), bf16[1024,512]{1,0:T(8,128)(2,1)}) %reduce-scatter.3.cloned.1.call-update) | async-done | bytes 1048592 | tf_op jit(solution)/shard_map/reduce_scatter | solution.py:71
  319.9 10.5 %fusion.12 = bf16[384,8192]{1,0:T(8,128)(2,1)} fusion(f32[384,8192]{1,0:T(8,128)} %get-tuple-element.14, bf16[384,8192]{1,0:T(8,128)(2,1)} %param.7, f32[384]{0:T(512)S(1)} %broadcast_multiply_fusion, f32[384]{0:T(512)S(1)} %add_rsqrt_fusion), kind=kLoop, calls=%fused_computation.19 | loop fusion | flops 18874368 | bytes 25168896 | tf_op jit(solution)/shard_map/convert_element_type | solution.py:89
  330.4 56.8 %reduce-scatter.5.cloned.1.call-done = bf16[64,512]{1,0:T(8,128)(2,1)} async-done(((bf16[1024,512]{1,0:T(8,128)(2,1)}), bf16[64,512]{1,0:T(8,128)(2,1)}) %reduce-scatter.5.cloned.1.call-update) | async-done | bytes 65552 | tf_op jit(solution)/shard_map/reduce_scatter | solution.py:79
  387.2 1.5 convert_element_type.70
  (6 shorter events, 0.1 us)
Async XLA Ops:
  7.2 83.6 %copy-start = (s32[1,384]{1,0:T(1,128)S(1)}, s32[1,384]{1,0:T(1,128)}, u32[]{:S(2)}) copy-start(s32[1,384]{1,0:T(1,128)} %param.10) | copy-start | bytes 4612
  7.2 52.1 %all-gather.4.cloned.1.call-start = ((), (), s32[]{:S(2)}) async-start(), calls=%async_computation.2 | async-start | bytes 1114112 | tf_op jit(solution)/shard_map/all_gather | solution.py:29
  7.9 148.2 %all-gather.6.cloned.1.call-start = ((), (), s32[]{:S(2)}) async-start(), calls=%async_computation.3 | async-start | bytes 9437184 | tf_op jit(solution)/shard_map/all_gather | solution.py:33
  59.3 260.7 %reduce-scatter.3.cloned.1.call-start = ((), (), s32[]{:S(2)}) async-start(), calls=%async_computation.4 | async-start | bytes 9437184 | tf_op jit(solution)/shard_map/reduce_scatter | solution.py:71
  228.3 158.8 %reduce-scatter.5.cloned.1.call-start = ((), (), s32[]{:S(2)}) async-start(), calls=%async_computation.5 | async-start | bytes 1114112 | tf_op jit(solution)/shard_map/reduce_scatter | solution.py:79
Sparse Core Ops, SparseCore 0:
  10.5 48.7 all-gather.3
  60.9 95.1 all-gather.5
  228.5 91.4 reduce-scatter.2
  323.6 63.5 reduce-scatter.4
where the time goes:
time: 397 us; the launch traced here: 395 us
  waiting for transfers between devices  206 us (52%)
  matrix products  85.4 us (22%)
  blocking collectives  49.5 us (12%)
  other arithmetic  26.1 us (7%)
  local copies, waits for them, and re-layouts  14.6 us (4%)
  between operations  13.8 us (3%)
    reduce_scatter x1, waiting for transfers between devices, per_device(): lax.psum_scatter(lax.dot_general(columns, dkeys, (((0,), (0,)), ((), ()))...  65.1 us
    reduce_scatter x1, waiting for transfers between devices, per_device(): lax.psum_scatter(inner_share, 'outer', scatter_dimension=0, tiled=True)  56.8 us
    all_gather x1, waiting for transfers between devices, per_device(): lax.all_gather(weight_codes, 'outer', axis=0, tiled=True)  51.3 us
    all_gather x1, waiting for transfers between devices, per_device(): lax.all_gather(secondary[0], 'inner', axis=0, tiled=True)  31.7 us
    all_gather x1, blocking collectives, per_device(): lax.all_gather(secondary[1], 'inner', axis=0, tiled=True)  27.8 us
    all_gather x1, blocking collectives, per_device(): lax.all_gather(weight_scales, 'outer', axis=0, tiled=True)  21.8 us
    dot_general x1, matrix products, per_device(): jnp.einsum('tkgd,skd->kgts', grad_heads, value_heads, preferred_element_t...  15.5 us
    dot_general x1, matrix products, per_device(): lax.dot_general(dkeys, piece_weight, (((1,), (1,)), ((), ())), preferred_...  14.8 us
  transfers between devices with their start and end apart: 4, of which 4 were waited for; matrix products, arithmetic and copies ran while one was open for 13% of the time, Pallas kernels for 0%

commit v1 on v0

v1 whole, which is shorter than its diff:
```python
import math

import jax
import jax.numpy as jnp
import numpy as np
from jax import lax
from jax.experimental import pallas as pl
from jax.experimental.pallas import tpu as pltpu
from jax.sharding import PartitionSpec as P

HD = 128
GROUP = 8
BLK = 512
AXES = ("outer", "inner")
F32 = jnp.float32
BF16 = jnp.bfloat16
VMEM_LIMIT = 48 * 1024 * 1024

INDEX = np.arange(128).reshape(2, 4, 2, 2, 4)


def permutation(move):
    pairs = []
    for zh in range(2):
        for x in range(4):
            for c in range(2):
                for zl in range(2):
                    for y in range(4):
                        nx, ny, nz, nc = move(x, y, zh * 2 + zl, c)
                        nx, ny, nz = nx % 4, ny % 4, nz % 4
                        target = INDEX[nz // 2, nx, nc, nz % 2, ny]
                        pairs.append((int(INDEX[zh, x, c, zl, y]), int(target)))
    return pairs


SWAP = permutation(lambda x, y, z, c: (x, y, z, 1 - c))


def along_x(d):
    return permutation(lambda x, y, z, c: (x + d, y, z, c))


def along_u(d):
    return permutation(lambda x, y, z, c: (x, y + d * (1 - c), z + d * c, c))


def along_v(d):
    return permutation(lambda x, y, z, c: (x, y + d * c, z + d * (1 - c), c))


def permute(a, perm):
    return lax.ppermute(a, AXES, perm)


def collect(a, along):
    return [a, permute(a, along(-1)), permute(a, along(2)), permute(a, along(1))]


def distribute(parts, along):
    return [permute(parts[2], along(2)), permute(parts[1], along(1)), permute(parts[3], along(-1))]


def params(**kw):
    return pltpu.CompilerParams(vmem_limit_bytes=VMEM_LIMIT, **kw)


def keys_part(order, own, sib, w, acc, rv):
    rows = own.shape[0]
    cols = w.shape[-1]
    first = acc is None

    def kernel(order_ref, own_ref, sib_ref, w_ref, *rest):
        out_own, out_sib = rest[-2:]
        i = pl.program_id(0)
        a = jnp.dot(own_ref[...], w_ref[0], preferred_element_type=F32)
        b = jnp.dot(sib_ref[...], w_ref[0], preferred_element_type=F32)

        @pl.when(i == 0)
        def _():
            if first:
                out_own[...] = a
                out_sib[...] = b
            else:
                out_own[...] = rest[0][...] + a
                out_sib[...] = rest[1][...] + b

        @pl.when(i > 0)
        def _():
            out_own[...] += a
            out_sib[...] += b

    tok = pl.BlockSpec((rows, BLK), lambda i, o: (0, o[rv * 4 + i]))
    whole = pl.BlockSpec((rows, cols), lambda i, o: (0, 0))
    out = jax.ShapeDtypeStruct((rows, cols), F32)
    return pl.pallas_call(
        kernel,
        out_shape=(out, out),
        grid_spec=pltpu.PrefetchScalarGridSpec(
            num_scalar_prefetch=1,
            grid=(4,),
            in_specs=[tok, tok, pl.BlockSpec((1, BLK, cols), lambda i, o: (i, 0, 0))]
            + ([] if first else [whole, whole]),
            out_specs=(whole, whole),
        ),
        compiler_params=params(),
        cost_estimate=pl.CostEstimate(
            flops=4 * rows * cols * BLK * 4, bytes_accessed=rows * BLK * 16, transcendentals=0
        ),
        name="keys_part",
    )(order, own, sib, w, *(() if first else acc))


def attention(kv, queries, keys_raw, values, out_grad, inv, doc_row, doc_col, prev):
    rows = queries.shape[0]
    scale = HD ** (-0.5)
    first = prev is None
    pairs = GROUP // 2

    def kernel(kv_ref, q_ref, k_ref, v_ref, g_ref, inv_ref, row_ref, col_ref, *rest):
        if not first:
            rest = rest[1:]
        o_ref, dkb_ref, dkw_ref, ms_ref, acc, bias, kb, vt, msum = rest
        h, i = pl.program_id(0), pl.program_id(1)

        @pl.when((h == 0) & (i == 0))
        def _():
            s = lax.broadcasted_iota(jnp.int32, (rows, rows), 0)
            t = lax.broadcasted_iota(jnp.int32, (rows, rows), 1)
            ok = (s <= t) & (col_ref[...] == row_ref[...])
            bias[...] = jnp.where(ok, 0.0, -1e30).astype(F32)
            msum[...] = jnp.zeros_like(msum)

        @pl.when(i == 0)
        def _():
            kb[...] = (k_ref[...] * inv_ref[...] * (scale * math.log2(math.e))).astype(BF16)
            vt[...] = v_ref[...].astype(F32).T.astype(BF16)
            acc[...] = jnp.zeros_like(acc)

        for j in range(rows // HD):
            n = (j + 1) * HD
            ts = slice(j * HD, n)
            q = jnp.concatenate([q_ref[ts, :HD], q_ref[ts, HD:]], axis=0)
            g = jnp.concatenate([g_ref[ts, :HD], g_ref[ts, HD:]], axis=0)
            sc = lax.dot_general(kb[:n], q, (((1,), (1,)), ((), ())), preferred_element_type=F32)
            b = bias[:n, ts]
            sc = sc + jnp.concatenate([b, b], axis=1)
            top = jnp.max(sc, axis=0, keepdims=True)
            e = jnp.exp2(sc - top)
            p = e * (1.0 / jnp.sum(e, axis=0, keepdims=True))
            ot = jnp.dot(vt[:, :n], p.astype(BF16), preferred_element_type=F32)
            o = ot.T.astype(BF16)
            o_ref[ts, :HD] = o[:HD]
            o_ref[ts, HD:] = o[HD:]
            dp = lax.dot_general(
                v_ref[:n], g, (((1,), (1,)), ((), ())), preferred_element_type=F32
            )
            pd = p * dp
            ds = (pd - p * jnp.sum(pd, axis=0, keepdims=True)).astype(BF16)
            acc[:n] += jnp.dot(ds, q, preferred_element_type=F32)

        @pl.when(i == pairs - 1)
        def _():
            dk = acc[...] * scale
            dkb = dk.astype(BF16)
            dkb_ref[...] = dkb
            dkw_ref[...] = (dk * inv_ref[...]).astype(BF16)
            msum[...] += jnp.sum(
                dkb.astype(F32) * (k_ref[...] * inv_ref[...]), axis=1, keepdims=True
            )
            ms_ref[...] = msum[...]

    wide = pl.BlockSpec((rows, 2 * HD), lambda h, i, kv: (0, (kv[0] + h) * pairs + i))
    half = pl.BlockSpec((rows, HD), lambda h, i, kv: (0, h))
    one = pl.BlockSpec((rows, 1), lambda h, i, kv: (0, 0))
    cols = 2 * HD
    return pl.pallas_call(
        kernel,
        out_shape=(
            jax.ShapeDtypeStruct(queries.shape, BF16),
            jax.ShapeDtypeStruct((rows, cols), BF16),
            jax.ShapeDtypeStruct((rows, cols), BF16),
            jax.ShapeDtypeStruct((rows, 1), F32),
        ),
        grid_spec=pltpu.PrefetchScalarGridSpec(
            num_scalar_prefetch=1,
            grid=(2, pairs),
            in_specs=[
                wide,
                half,
                pl.BlockSpec((rows, HD), lambda h, i, kv: (0, kv[0] + h)),
                wide,
                one,
                pl.BlockSpec((1, rows), lambda h, i, kv: (0, 0)),
                one,
            ]
            + ([] if first else [pl.BlockSpec(memory_space=pl.ANY)]),
            out_specs=(wide, half, half, one),
            scratch_shapes=[
                pltpu.VMEM((rows, HD), F32),
                pltpu.VMEM((rows, rows), F32),
                pltpu.VMEM((rows, HD), BF16),
                pltpu.VMEM((HD, rows), BF16),
                pltpu.VMEM((rows, 1), F32),
            ],
        ),
        input_output_aliases={} if first else {8: 0},
        compiler_params=params(),
        cost_estimate=pl.CostEstimate(
            flops=8 * 16 * rows * rows * HD * 2 // 3,
            bytes_accessed=rows * 2048 * 6,
            transcendentals=16 * rows * rows * 2 // 3,
        ),
        name="attention",
    )(kv, queries, keys_raw, values, out_grad, inv, doc_row, doc_col, *(() if first else (prev,)))


def grad_part(order, own, sib, dk_own, dk_sib, rv):
    rows = own.shape[0]
    cols = dk_own.shape[1]

    def kernel(order_ref, own_ref, sib_ref, a_ref, b_ref, out, at, bt):
        @pl.when(pl.program_id(0) == 0)
        def _():
            at[...] = a_ref[...].astype(F32).T.astype(BF16)
            bt[...] = b_ref[...].astype(F32).T.astype(BF16)

        out[0] = (
            jnp.dot(at[...], own_ref[...], preferred_element_type=F32)
            + jnp.dot(bt[...], sib_ref[...], preferred_element_type=F32)
        ).astype(BF16)

    tok = pl.BlockSpec((rows, BLK), lambda i, o: (0, o[rv * 4 + i]))
    whole = pl.BlockSpec((rows, cols), lambda i, o: (0, 0))
    return pl.pallas_call(
        kernel,
        out_shape=jax.ShapeDtypeStruct((4, cols, BLK), BF16),
        grid_spec=pltpu.PrefetchScalarGridSpec(
            num_scalar_prefetch=1,
            grid=(4,),
            in_specs=[tok, tok, whole, whole],
            out_specs=pl.BlockSpec((1, cols, BLK), lambda i, o: (i, 0, 0)),
            scratch_shapes=[pltpu.VMEM((cols, rows), BF16), pltpu.VMEM((cols, rows), BF16)],
        ),
        compiler_params=params(),
        cost_estimate=pl.CostEstimate(
            flops=4 * rows * cols * BLK * 4, bytes_accessed=rows * BLK * 16, transcendentals=0
        ),
        name="grad_part",
    )(order, own, sib, dk_own, dk_sib)


def token_grad(order, tokens, dk_own, dk_oth, w_own, w_sib, inv, ms0, ms1):
    rows, width = tokens.shape
    cols = dk_own.shape[1]

    def kernel(order_ref, tok_ref, a_ref, b_ref, *rest):
        own, sib = rest[:4], rest[4:8]
        inv_ref, ms0_ref, ms1_ref, out, wo, ws = rest[8:]
        i = pl.program_id(0)
        for k in range(4):

            @pl.when(i // 4 == k)
            def _(k=k):
                wo[...] = own[k][0]

            @pl.when(i % 4 == k)
            def _(k=k):
                ws[...] = sib[k][0]

        nt = (((1,), (1,)), ((), ()))
        dn = lax.dot_general(a_ref[...], wo[...], nt, preferred_element_type=F32)
        dn = dn + lax.dot_general(b_ref[...], ws[...], nt, preferred_element_type=F32)
        r = inv_ref[...]
        mean = (ms0_ref[...] + ms1_ref[...]) * (1.0 / width)
        hat = tok_ref[...].astype(F32) * r
        out[...] = (r * (dn - hat * mean)).astype(BF16)

    tok = pl.BlockSpec((rows, BLK), lambda i, o: (0, o[i]))
    whole = pl.BlockSpec((rows, cols), lambda i, o: (0, 0))
    one = pl.BlockSpec((rows, 1), lambda i, o: (0, 0))
    own_specs = [
        pl.BlockSpec((1, BLK, cols), lambda i, o, k=k: (jnp.clip(i - 4 * k, 0, 3), 0, 0))
        for k in range(4)
    ]
    sib_specs = [pl.BlockSpec((1, BLK, cols), lambda i, o: (i // 4, 0, 0)) for _ in range(4)]
    return pl.pallas_call(
        kernel,
        out_shape=jax.ShapeDtypeStruct(tokens.shape, BF16),
        grid_spec=pltpu.PrefetchScalarGridSpec(
            num_scalar_prefetch=1,
            grid=(16,),
            in_specs=[tok, whole, whole] + own_specs + sib_specs + [one, one, one],
            out_specs=tok,
            scratch_shapes=[pltpu.VMEM((BLK, cols), BF16), pltpu.VMEM((BLK, cols), BF16)],
        ),
        compiler_params=params(),
        cost_estimate=pl.CostEstimate(
            flops=4 * rows * cols * width, bytes_accessed=rows * width * 5, transcendentals=0
        ),
        name="token_grad",
    )(order, tokens, dk_own, dk_oth, *w_own, *w_sib, inv, ms0, ms1)


def per_device(tokens, queries, values, doc_ids, weight_codes, weight_scales, out_grad):
    rows, width = tokens.shape
    outer, inner = lax.axis_index("outer"), lax.axis_index("inner")
    x, core, y = (outer // 2) % 4, outer % 2, inner % 4
    z = (outer // 8) * 2 + inner // 4
    u, v = jnp.where(core == 0, y, z), jnp.where(core == 0, z, y)
    bv = (v + jnp.arange(4, dtype=jnp.int32)[:, None]) % 4
    bu = (u + jnp.arange(4, dtype=jnp.int32)[None, :]) % 4
    by, bz = jnp.where(core == 0, bu, bv), jnp.where(core == 0, bv, bu)
    order = (((bz % 2) * 4 + by) * 2 + bz // 2).reshape(16).astype(jnp.int32)

    factor = jnp.exp2(weight_scales.astype(F32))
    wrows, wcols = weight_codes.shape
    weight = weight_codes.astype(F32).reshape(2, wrows // 2, wcols) * factor[:, None, :]
    weight = weight.reshape(wrows, wcols).astype(BF16)
    hc = wcols // 2
    keep = jnp.where(core == 0, weight[:, :hc], weight[:, hc:])
    send = jnp.where(core == 0, weight[:, hc:], weight[:, :hc])
    got = permute(send, SWAP)
    chip = jnp.where(
        core == 0, jnp.concatenate([keep, got], 0), jnp.concatenate([got, keep], 0)
    )
    ring = collect(chip, along_x)
    ordered = []
    for i in range(4):
        r = (i - x) % 4
        ordered.append(
            jnp.where(r == 0, ring[0], jnp.where(r == 1, ring[1], jnp.where(r == 2, ring[2], ring[3])))
        )
    block = jnp.concatenate(ordered, 0)
    plane = jnp.stack(collect(block, along_u))
    w_own = collect(plane, along_v)

    tokens_sib = permute(tokens, SWAP)
    full = tokens.astype(F32)
    inv = lax.rsqrt(jnp.mean(full * full, axis=-1, keepdims=True) + 1e-05)

    acc = None
    for rv in (0, 1, 3, 2):
        acc = keys_part(order, tokens, tokens_sib, w_own[rv], acc, rv)
    keys_own, keys_sib = acc
    keys_oth = permute(keys_sib, SWAP)
    w_sib = [permute(w, SWAP) for w in w_own]

    doc_row = doc_ids
    doc_col = doc_ids.reshape(rows, 1)
    kv_own = (core * 2).astype(jnp.int32).reshape(1)
    kv_oth = 2 - kv_own
    out, dkb_own, dkw_own, ms_own = attention(
        kv_own, queries, keys_own, values, out_grad, inv, doc_row, doc_col, None
    )
    out, dkb_oth, dkw_oth, ms_oth = attention(
        kv_oth, queries, keys_oth, values, out_grad, inv, doc_row, doc_col, out
    )
    dkw_sib = permute(dkw_oth, SWAP)

    parts = [None] * 4
    for rv in (2, 1, 3, 0):
        parts[rv] = grad_part(order, tokens, tokens_sib, dkw_own, dkw_sib, rv)
    arrived = distribute(parts, along_v)
    grad_tokens = token_grad(
        order, tokens, dkb_own, dkb_oth, w_own, w_sib, inv, ms_own, ms_oth
    )

    def total(own, others):
        s = own.astype(F32)
        for o in others:
            s = s + o.astype(F32)
        return s

    chunk = [total(parts[0][r], [a[r] for a in arrived]) for r in range(4)]
    arrived = distribute([c.astype(BF16) for c in chunk], along_u)
    line = total(chunk[0], arrived)
    by_x = [lax.dynamic_slice_in_dim(line, ((x + r) % 4) * HD, HD, 1) for r in range(4)]
    arrived = distribute([c.astype(BF16) for c in by_x], along_x)
    mine = total(by_x[0], arrived).T
    keep = lax.dynamic_slice_in_dim(mine, core * wrows, wrows, 0)
    got = permute(lax.dynamic_slice_in_dim(mine, (1 - core) * wrows, wrows, 0), SWAP)
    grad_weight = jnp.where(
        core == 0, jnp.concatenate([keep, got], 1), jnp.concatenate([got, keep], 1)
    )
    return (out, grad_tokens, grad_weight)


def solution(mesh):
    return jax.shard_map(
        per_device,
        mesh=mesh,
        in_specs=(
            P(("outer", "inner"), None),
            P(("outer", "inner"), None),
            P(("outer", "inner"), None),
            P(("outer", "inner"), None),
            P(("inner", "outer"), None),
            P(("inner", "outer"), None),
            P(("outer", "inner"), None),
        ),
        out_specs=(
            P(("outer", "inner"), None),
            P(("outer", "inner"), None),
            P(("inner", "outer"), None),
        ),
        check_vma=False,
    )
```

time: 397 us -> 206 us (0.52)
  waiting for transfers between devices: 206 us -> 63.7 us
  matrix products: 85.4 us -> 0 us
  Pallas kernels: 0 us -> 85.1 us
  blocking collectives: 49.5 us -> 0 us
  starting transfers between devices: 0.16 us -> 37.1 us
  other arithmetic: 26.1 us -> 7.33 us
  between operations: 13.8 us -> 1.04 us
    reduce_scatter x2 -> x0, waiting for transfers between devices: 122 us -> none  [the longest x1 65.1 us: per_device(): lax.psum_scatter(lax.dot_general(columns, dkeys, (((0,), (0,)), ((), ()))...]
    pallas_call x0 -> x11, Pallas kernels: none -> 85.1 us  [the longest x2 32.8 us: attention(): pl.pallas_call(kernel, out_shape=(jax.ShapeDtypeStruct(queries.shape, BF1...]
    all_gather x2 -> x0, waiting for transfers between devices: 83 us -> none  [the longest x1 51.3 us: per_device(): lax.all_gather(weight_codes, 'outer', axis=0, tiled=True)]
    dot_general x6 -> x0, matrix products: 73.3 us -> none  [the longest x1 15.5 us: per_device(): jnp.einsum('tkgd,skd->kgts', grad_heads, value_heads, preferred_element_t...]
    ppermute x0 -> x27, waiting for transfers between devices: none -> 63.7 us  [permute(): return lax.ppermute(a, AXES, perm)]
    all_gather x2 -> x0, blocking collectives: 49.5 us -> none  [the longest x1 27.8 us: per_device(): lax.all_gather(secondary[1], 'inner', axis=0, tiled=True)]
    ppermute x0 -> x27, starting transfers between devices: none -> 37.1 us  [permute(): return lax.ppermute(a, AXES, perm)]
    convert_element_type x3 -> x1, other arithmetic: 20.2 us -> 0.86 us  [per_device(): weight = weight.reshape(wrows, wcols).astype(BF16)]
  transfers between devices with their start and end apart: 4 -> 27, of which waited for: 4 -> 14; matrix products, arithmetic and copies ran while one was open for 13% -> 3% of each run, Pallas kernels for 0% -> 29%
where the time goes in v1:
time: 206 us; the launch traced here: 205 us
  Pallas kernels  85.1 us (41%)
  waiting for transfers between devices  63.7 us (31%)
  starting transfers between devices  37.1 us (18%)
  local copies, waits for them, and re-layouts  11.1 us (5%)
  other arithmetic  7.33 us (4%)
    ppermute x27, waiting for transfers between devices, permute(): return lax.ppermute(a, AXES, perm)  63.7 us
    ppermute x27, starting transfers between devices, permute(): return lax.ppermute(a, AXES, perm)  37.1 us
    pallas_call x2, Pallas kernels, attention(): pl.pallas_call(kernel, out_shape=(jax.ShapeDtypeStruct(queries.shape, BF1...  32.8 us
    pallas_call x4, Pallas kernels, keys_part(): pl.pallas_call(kernel, out_shape=(out, out), grid_spec=pltpu.PrefetchScal...  18.6 us
    pallas_call x4, Pallas kernels, grad_part(): pl.pallas_call(kernel, out_shape=jax.ShapeDtypeStruct((4, cols, BLK), BF1...  17.5 us
    pallas_call x1, Pallas kernels, token_grad(): pl.pallas_call(kernel, out_shape=jax.ShapeDtypeStruct(tokens.shape, BF16)...  16.2 us
    unnamed x59, local copies, waits for them, and re-layouts  9.87 us
  transfers between devices with their start and end apart: 27, of which 14 were waited for; matrix products, arithmetic and copies ran while one was open for 3% of the time, Pallas kernels for 29%

profile of v1, /device:TPU:1, one launch (start us, length us, event | category | flops | bytes accessed | tf_op | source)
XLA Modules:
  0.0 205.3 jit_solution(11266651694624905026)
XLA Ops:
  3.8 8.1 %collective-permute-done.1 = bf16[64,256]{1,0:T(8,128)(2,1)S(1)} collective-permute-done((bf16[64,256]{1,0:T(8,128)(2,1)S(1)}, bf16[64,256]{1,0:T(8,128)(2,1)S(1)}, u32[]{:S(2)}, u32[]{:S(2)}) %collective-permute-start.1) | collective-permute-done | bytes 32800 | tf_op jit(solution)/shard_map/ppermute | solution.py:52
  12.0 2.6 %collective-permute-start.2 = (bf16[128,256]{1,0:T(8,128)(2,1)S(1)}, bf16[128,256]{1,0:T(8,128)(2,1)S(1)}, u32[]{:S(2)}, u32[]{:S(2)}) collective-permute-start(bf16[128,256]{1,0:T(8,128)(2,1)S(1)} %maximum_select_fusion.1), channel_id=1, source_target_pairs={{0,48},{1,49},{2,50},{3,51},{4,52},{5,53},{6,54},{7,55},{8,56},{9,... | collective-permute-start | bytes 196616 | tf_op jit(solution)/shard_map/ppermute | solution.py:52
  15.9 3.3 %collective-permute-done.3 = bf16[128,256]{1,0:T(8,128)(2,1)S(1)} collective-permute-done((bf16[128,256]{1,0:T(8,128)(2,1)S(1)}, bf16[128,256]{1,0:T(8,128)(2,1)S(1)}, u32[]{:S(2)}, u32[]{:S(2)}) %collective-permute-start.3) | collective-permute-done | bytes 65568 | tf_op jit(solution)/shard_map/ppermute | solution.py:52
  20.6 3.8 %collective-permute-start.5 = (bf16[512,256]{1,0:T(8,128)(2,1)S(1)}, bf16[512,256]{1,0:T(8,128)(2,1)S(1)}, u32[]{:S(2)}, u32[]{:S(2)}) collective-permute-start(bf16[512,256]{1,0:T(8,128)(2,1)S(1)} %get-tuple-element.48), channel_id=1, source_target_pairs={{0,3},{1,0},{2,1},{3,2},{4,7},{5,4},{6,5},{7,6},{8,76},{9,77},{10,... | collective-permute-start | bytes 786440 | tf_op jit(solution)/shard_map/ppermute | solution.py:52
  25.1 5.4 %collective-permute-done.5 = bf16[512,256]{1,0:T(8,128)(2,1)S(1)} collective-permute-done((bf16[512,256]{1,0:T(8,128)(2,1)S(1)}, bf16[512,256]{1,0:T(8,128)(2,1)S(1)}, u32[]{:S(2)}, u32[]{:S(2)}) %collective-permute-start.5) | collective-permute-done | bytes 262176 | tf_op jit(solution)/shard_map/ppermute | solution.py:52
  31.5 2.5 %collective-permute-done.7 = bf16[512,256]{1,0:T(8,128)(2,1)S(1)} collective-permute-done((bf16[512,256]{1,0:T(8,128)(2,1)S(1)}, bf16[512,256]{1,0:T(8,128)(2,1)S(1)}, u32[]{:S(2)}, u32[]{:S(2)}) %collective-permute-start.7) | collective-permute-done | bytes 262176 | tf_op jit(solution)/shard_map/ppermute | solution.py:52
  34.1 2.5 %collective-permute-start.10 = (bf16[4,512,256]{2,1,0:T(8,128)(2,1)S(1)}, bf16[4,512,256]{2,1,0:T(8,128)(2,1)S(1)}, u32[]{:S(2)}, u32[]{:S(2)}) collective-permute-start(bf16[4,512,256]{2,1,0:T(8,128)(2,1)S(1)} %pad_maximum_fusion.w_ref.rest_0_), channel_id=1, source_target_pairs={{0,68},{1,69},{2,70},{3,71},{4,0},{5,1},{6,2},{7,3},{8,11},{9,8},{... | collective-permute-start | bytes 3145736 | tf_op jit(solution)/shard_map/ppermute | solution.py:52
  36.6 1.6 collective-permute-start.8
  38.5 4.2 %keys_part.4 = (f32[384,256]{1,0:T(8,128)S(1)}, f32[384,256]{1,0:T(8,128)S(1)}) custom-call(s32[16]{0:T(128)S(1)} %multiply_add_fusion.order_ref, bf16[384,8192]{1,0:T(8,128)(2,1)} %own_ref.15, bf16[384,8192]{1,0:T(8,128)(2,1)} %collective-permute-done.sib_ref, bf16[4,512,256]{2,1,0:T(8,128)(2,1)S(1)} %pad_maximum_fusion.w_ref.rest_0_), custom_call_target="tpu_custom_call" | custom-call | flops 805306368 | bytes 3145728 | tf_op jit(solution)/shard_map/keys_part/pallas_call | solution.py:95
  42.8 16.8 %collective-permute-done.10.w_ref.rest_1_ = bf16[4,512,256]{2,1,0:T(8,128)(2,1)S(1)} collective-permute-done((bf16[4,512,256]{2,1,0:T(8,128)(2,1)S(1)}, bf16[4,512,256]{2,1,0:T(8,128)(2,1)S(1)}, u32[]{:S(2)}, u32[]{:S(2)}) %collective-permute-start.10) | collective-permute-done | bytes 1048608 | tf_op jit(solution)/shard_map/ppermute | solution.py:52
  59.6 4.2 %keys_part.5 = (f32[384,256]{1,0:T(8,128)S(1)}, f32[384,256]{1,0:T(8,128)S(1)}) custom-call(s32[16]{0:T(128)S(1)} %multiply_add_fusion.order_ref, bf16[384,8192]{1,0:T(8,128)(2,1)} %own_ref.15, bf16[384,8192]{1,0:T(8,128)(2,1)} %collective-permute-done.sib_ref, bf16[4,512,256]{2,1,0:T(8,128)(2,1)S(1)} %collective-permute-done.10.w_ref.rest_1_, ...), custom_call_target="tpu_custom_call" | custom-call | flops 805306368 | bytes 3145728 | tf_op jit(solution)/shard_map/keys_part/pallas_call | solution.py:95
  63.9 4.9 %keys_part.6 = (f32[384,256]{1,0:T(8,128)S(1)}, f32[384,256]{1,0:T(8,128)S(1)}) custom-call(s32[16]{0:T(128)S(1)} %multiply_add_fusion.order_ref, bf16[384,8192]{1,0:T(8,128)(2,1)} %own_ref.15, bf16[384,8192]{1,0:T(8,128)(2,1)} %collective-permute-done.sib_ref, bf16[4,512,256]{2,1,0:T(8,128)(2,1)S(1)} %collective-permute-done.9.w_ref.rest_3_, ...), custom_call_target="tpu_custom_call" | custom-call | flops 805306368 | bytes 3145728 | tf_op jit(solution)/shard_map/keys_part/pallas_call | solution.py:95
  68.9 5.2 %keys_part.7 = (f32[384,256]{1,0:T(8,128)S(1)}, f32[384,256]{1,0:T(8,128)}) custom-call(s32[16]{0:T(128)S(1)} %multiply_add_fusion.order_ref, bf16[384,8192]{1,0:T(8,128)(2,1)} %own_ref.15, bf16[384,8192]{1,0:T(8,128)(2,1)} %collective-permute-done.sib_ref, bf16[4,512,256]{2,1,0:T(8,128)(2,1)} %collective-permute-done.8.w_ref.rest_2_, ...), custom_call_target="tpu_custom_call" | custom-call | flops 805306368 | bytes 3145728 | tf_op jit(solution)/shard_map/keys_part/pallas_call | solution.py:95
  74.8 4.1 %collective-permute-start.11 = (f32[384,256]{1,0:T(8,128)}, f32[384,256]{1,0:T(8,128)}, u32[]{:S(2)}, u32[]{:S(2)}) collective-permute-start(f32[384,256]{1,0:T(8,128)} %get-tuple-element.25), channel_id=1, source_target_pairs={{0,8},{1,9},{2,10},{3,11},{4,12},{5,13},{6,14},{7,15},{8,0},{9,1},... | collective-permute-start | bytes 1179656 | tf_op jit(solution)/shard_map/ppermute | solution.py:52
  82.5 16.4 %attention.2 = (bf16[384,4096]{1,0:T(8,128)(2,1)}, bf16[384,256]{1,0:T(8,128)(2,1)S(1)}, bf16[384,256]{1,0:T(8,128)(2,1)S(1)}, f32[384,1]{1,0:T(8,128)S(1)}) custom-call(s32[1]{0:T(128)} %bitcast.kv_ref, bf16[384,4096]{1,0:T(8,128)(2,1)S(1)} %copy-done, f32[384,256]{1,0:T(8,128)S(1)} %copy-done.11, bf16[384,512]{1,0:T(8,128)(2,1)S(1)} %copy-done.8, ...), custom_call_target="tpu_custom_call" | custom-call | flops 1610612736 | bytes 4718592 | tf_op jit(solution)/shard_map/attention/pallas_call | solution.py:176
  100.3 16.4 %attention.3 = (bf16[384,4096]{1,0:T(8,128)(2,1)}, bf16[384,256]{1,0:T(8,128)(2,1)S(1)}, bf16[384,256]{1,0:T(8,128)(2,1)S(1)}, f32[384,1]{1,0:T(8,128)S(1)}) custom-call(s32[1]{0:T(128)S(6)} %sub.32.kv_ref, bf16[384,4096]{1,0:T(8,128)(2,1)S(1)} %copy-done, f32[384,256]{1,0:T(8,128)} %collective-permute-done.11.k_ref, ...), custom_call_target="tpu_custom_call", output_to_operand_aliasing={{0}: (8, {})} | custom-call | flops 1610612736 | bytes 4718592 | tf_op jit(solution)/shard_map/attention/pallas_call | solution.py:176
  118.8 4.4 %grad_part.5 = bf16[4,256,512]{2,1,0:T(8,128)(2,1)S(1)} custom-call(s32[16]{0:T(128)S(1)} %multiply_add_fusion.order_ref, bf16[384,8192]{1,0:T(8,128)(2,1)} %own_ref.15, bf16[384,8192]{1,0:T(8,128)(2,1)} %collective-permute-done.sib_ref, bf16[384,256]{1,0:T(8,128)(2,1)S(1)} %get-tuple-element.33.a_ref, bf16[384,256]{1,0:T(8,128)(2,1)S(1)} %collective-permute-done.16.b_ref), custom_call_target="tpu_custom_call" | custom-call | flops 805306368 | bytes 3145728 | tf_op jit(solution)/shard_map/grad_part/pallas_call | solution.py:234
  123.8 4.4 %grad_part.6 = bf16[4,256,512]{2,1,0:T(8,128)(2,1)S(1)} custom-call(s32[16]{0:T(128)S(1)} %multiply_add_fusion.order_ref, bf16[384,8192]{1,0:T(8,128)(2,1)} %own_ref.15, bf16[384,8192]{1,0:T(8,128)(2,1)} %collective-permute-done.sib_ref, bf16[384,256]{1,0:T(8,128)(2,1)S(1)} %get-tuple-element.33.a_ref, bf16[384,256]{1,0:T(8,128)(2,1)S(1)} %collective-permute-done.16.b_ref), custom_call_target="tpu_custom_call" | custom-call | flops 805306368 | bytes 3145728 | tf_op jit(solution)/shard_map/grad_part/pallas_call | solution.py:234
  128.8 4.4 %grad_part.7 = bf16[4,256,512]{2,1,0:T(8,128)(2,1)S(1)} custom-call(s32[16]{0:T(128)S(1)} %multiply_add_fusion.order_ref, bf16[384,8192]{1,0:T(8,128)(2,1)} %own_ref.15, bf16[384,8192]{1,0:T(8,128)(2,1)} %collective-permute-done.sib_ref, bf16[384,256]{1,0:T(8,128)(2,1)S(1)} %get-tuple-element.33.a_ref, bf16[384,256]{1,0:T(8,128)(2,1)S(1)} %collective-permute-done.16.b_ref), custom_call_target="tpu_custom_call" | custom-call | flops 805306368 | bytes 3145728 | tf_op jit(solution)/shard_map/grad_part/pallas_call | solution.py:234
  133.2 2.2 %collective-permute-start.19 = (bf16[4,256,512]{2,1,0:T(8,128)(2,1)S(1)}, bf16[4,256,512]{2,1,0:T(8,128)(2,1)S(1)}, u32[]{:S(2)}, u32[]{:S(2)}) collective-permute-start(bf16[4,256,512]{2,1,0:T(8,128)(2,1)S(1)} %grad_part.7), channel_id=1, source_target_pairs={{0,68},{1,69},{2,70},{3,71},{4,0},{5,1},{6,2},{7,3},{8,11},{9,8},{... | collective-permute-start | bytes 3145736 | tf_op jit(solution)/shard_map/ppermute | solution.py:52
  135.4 4.4 %grad_part.4 = bf16[4,256,512]{2,1,0:T(8,128)(2,1)S(1)} custom-call(s32[16]{0:T(128)S(1)} %multiply_add_fusion.order_ref, bf16[384,8192]{1,0:T(8,128)(2,1)} %own_ref.15, bf16[384,8192]{1,0:T(8,128)(2,1)} %collective-permute-done.sib_ref, bf16[384,256]{1,0:T(8,128)(2,1)S(1)} %get-tuple-element.33.a_ref, bf16[384,256]{1,0:T(8,128)(2,1)S(1)} %collective-permute-done.16.b_ref), custom_call_target="tpu_custom_call" | custom-call | flops 805306368 | bytes 3145728 | tf_op jit(solution)/shard_map/grad_part/pallas_call | solution.py:234
  139.9 10.3 %collective-permute-done.18 = bf16[4,256,512]{2,1,0:T(8,128)(2,1)S(1)} collective-permute-done((bf16[4,256,512]{2,1,0:T(8,128)(2,1)S(1)}, bf16[4,256,512]{2,1,0:T(8,128)(2,1)S(1)}, u32[]{:S(2)}, u32[]{:S(2)}) %collective-permute-start.18) | collective-permute-done | bytes 1048608 | tf_op jit(solution)/shard_map/ppermute | solution.py:52
  151.6 4.0 %collective-permute-start.21 = (bf16[256,512]{1,0:T(8,128)(2,1)S(1)}, bf16[256,512]{1,0:T(8,128)(2,1)S(1)}, u32[]{:S(2)}, u32[]{:S(2)}) collective-permute-start(bf16[256,512]{1,0:T(8,128)(2,1)S(1)} %get-tuple-element.43), channel_id=1, source_target_pairs={{0,1},{1,2},{2,3},{3,0},{4,5},{5,6},{6,7},{7,4},{8,12},{9,13},{10,... | collective-permute-start | bytes 786440 | tf_op jit(solution)/shard_map/ppermute | solution.py:52
  155.6 1.8 collective-permute-start.12
  158.6 2.8 %collective-permute-start.14 = (bf16[4,512,256]{2,1,0:T(8,128)(2,1)}, bf16[4,512,256]{2,1,0:T(8,128)(2,1)}, u32[]{:S(2)}, u32[]{:S(2)}) collective-permute-start(bf16[4,512,256]{2,1,0:T(8,128)(2,1)} %collective-permute-done.8.w_ref.rest_2_), channel_id=1, source_target_pairs={{0,8},{1,9},{2,10},{3,11},{4,12},{5,13},{6,14},{7,15},{8,0},{9,1},... | collective-permute-start | bytes 3145736 | tf_op jit(solution)/shard_map/ppermute | solution.py:52
  162.2 2.7 %collective-permute-start.15 = (bf16[4,512,256]{2,1,0:T(8,128)(2,1)S(1)}, bf16[4,512,256]{2,1,0:T(8,128)(2,1)}, u32[]{:S(2)}, u32[]{:S(2)}) collective-permute-start(bf16[4,512,256]{2,1,0:T(8,128)(2,1)S(1)} %copy-done.6), channel_id=1, source_target_pairs={{0,8},{1,9},{2,10},{3,11},{4,12},{5,13},{6,14},{7,15},{8,0},{9,1},... | collective-permute-start | bytes 3145736 | tf_op jit(solution)/shard_map/ppermute | solution.py:52
  164.9 1.7 fusion.1
  168.8 4.6 %collective-permute-done.23 = bf16[256,128]{1,0:T(8,128)(2,1)} collective-permute-done((bf16[256,128]{1,0:T(8,128)(2,1)S(1)}, bf16[256,128]{1,0:T(8,128)(2,1)}, u32[]{:S(2)}, u32[]{:S(2)}) %collective-permute-start.23) | collective-permute-done | bytes 65568 | tf_op jit(solution)/shard_map/ppermute | solution.py:52
  173.3 4.4 %collective-permute-done.24 = bf16[256,128]{1,0:T(8,128)(2,1)} collective-permute-done((bf16[256,128]{1,0:T(8,128)(2,1)S(1)}, bf16[256,128]{1,0:T(8,128)(2,1)}, u32[]{:S(2)}, u32[]{:S(2)}) %collective-permute-start.24) | collective-permute-done | bytes 65568 | tf_op jit(solution)/shard_map/ppermute | solution.py:52
  177.8 3.4 %collective-permute-done.25 = bf16[256,128]{1,0:T(8,128)(2,1)} collective-permute-done((bf16[256,128]{1,0:T(8,128)(2,1)}, bf16[256,128]{1,0:T(8,128)(2,1)}, u32[]{:S(2)}, u32[]{:S(2)}) %collective-permute-start.25) | collective-permute-done | bytes 65568 | tf_op jit(solution)/shard_map/ppermute | solution.py:52
  182.4 3.2 %collective-permute-start.26 = (f32[64,256]{0,1:T(8,128)S(1)}, f32[64,256]{0,1:T(8,128)S(1)}, u32[]{:S(2)}, u32[]{:S(2)}) collective-permute-start(f32[64,256]{0,1:T(8,128)S(1)} %get-tuple-element.54), channel_id=1, source_target_pairs={{0,8},{1,9},{2,10},{3,11},{4,12},{5,13},{6,14},{7,15},{8,0},{9,1},... | collective-permute-start | bytes 196616 | tf_op jit(solution)/shard_map/ppermute | solution.py:52
  188.4 16.2 %token_grad.1 = bf16[384,8192]{1,0:T(8,128)(2,1)} custom-call(s32[16]{0:T(128)S(1)} %multiply_add_fusion.order_ref, bf16[384,8192]{1,0:T(8,128)(2,1)} %own_ref.15, bf16[384,256]{1,0:T(8,128)(2,1)S(1)} %copy-done.13, bf16[384,256]{1,0:T(8,128)(2,1)S(1)} %copy-done.17, bf16[4,512,256]{2,1,0:T(8,128)(2,1)S(1)} %copy-done.2, bf16[4,512,256]{2,1,0:T(8,128)(2,1)S(1)} %copy-done.4, ...), custom_call_target="tpu_custom_call" | custom-call | flops 3221225472 | bytes 15728640 | tf_op jit(solution)/shard_map/token_grad/pallas_call | solution.py:286
  (115 shorter events, 27.4 us)
Async XLA Ops:
  0.6 37.9 %collective-permute-start = (bf16[384,8192]{1,0:T(8,128)(2,1)}, bf16[384,8192]{1,0:T(8,128)(2,1)}, u32[]{:S(2)}, u32[]{:S(2)}) collective-permute-start(bf16[384,8192]{1,0:T(8,128)(2,1)} %own_ref.15), channel_id=1, source_target_pairs={{0,8},{1,9},{2,10},{3,11},{4,12},{5,13},{6,14},{7,15},{8,0},{9,1},... | collective-permute-start | bytes 18874376 | tf_op jit(solution)/shard_map/ppermute | solution.py:52
  3.7 8.3 %collective-permute-start.1 = (bf16[64,256]{1,0:T(8,128)(2,1)S(1)}, bf16[64,256]{1,0:T(8,128)(2,1)S(1)}, u32[]{:S(2)}, u32[]{:S(2)}) collective-permute-start(bf16[64,256]{1,0:T(8,128)(2,1)S(1)} %get-tuple-element.56), channel_id=1, source_target_pairs={{0,8},{1,9},{2,10},{3,11},{4,12},{5,13},{6,14},{7,15},{8,0},{9,1},... | collective-permute-start | bytes 98312 | tf_op jit(solution)/shard_map/ppermute | solution.py:52
  12.0 4.0 %collective-permute-start.2 = (bf16[128,256]{1,0:T(8,128)(2,1)S(1)}, bf16[128,256]{1,0:T(8,128)(2,1)S(1)}, u32[]{:S(2)}, u32[]{:S(2)}) collective-permute-start(bf16[128,256]{1,0:T(8,128)(2,1)S(1)} %maximum_select_fusion.1), channel_id=1, source_target_pairs={{0,48},{1,49},{2,50},{3,51},{4,52},{5,53},{6,54},{7,55},{8,56},{9,... | collective-permute-start | bytes 196616 | tf_op jit(solution)/shard_map/ppermute | solution.py:52
  14.6 4.7 %collective-permute-start.3 = (bf16[128,256]{1,0:T(8,128)(2,1)S(1)}, bf16[128,256]{1,0:T(8,128)(2,1)S(1)}, u32[]{:S(2)}, u32[]{:S(2)}) collective-permute-start(bf16[128,256]{1,0:T(8,128)(2,1)S(1)} %maximum_select_fusion.1), channel_id=1, source_target_pairs={{0,32},{1,33},{2,34},{3,35},{4,36},{5,37},{6,38},{7,39},{8,40},{9,... | collective-permute-start | bytes 196616 | tf_op jit(solution)/shard_map/ppermute | solution.py:52
  15.1 5.4 %collective-permute-start.4 = (bf16[128,256]{1,0:T(8,128)(2,1)S(1)}, bf16[128,256]{1,0:T(8,128)(2,1)S(1)}, u32[]{:S(2)}, u32[]{:S(2)}) collective-permute-start(bf16[128,256]{1,0:T(8,128)(2,1)S(1)} %maximum_select_fusion.1), channel_id=1, source_target_pairs={{0,16},{1,17},{2,18},{3,19},{4,20},{5,21},{6,22},{7,23},{8,24},{9,... | collective-permute-start | bytes 196616 | tf_op jit(solution)/shard_map/ppermute | solution.py:52
  20.6 10.0 %collective-permute-start.5 = (bf16[512,256]{1,0:T(8,128)(2,1)S(1)}, bf16[512,256]{1,0:T(8,128)(2,1)S(1)}, u32[]{:S(2)}, u32[]{:S(2)}) collective-permute-start(bf16[512,256]{1,0:T(8,128)(2,1)S(1)} %get-tuple-element.48), channel_id=1, source_target_pairs={{0,3},{1,0},{2,1},{3,2},{4,7},{5,4},{6,5},{7,6},{8,76},{9,77},{10,... | collective-permute-start | bytes 786440 | tf_op jit(solution)/shard_map/ppermute | solution.py:52
  24.4 7.1 %collective-permute-start.6 = (bf16[512,256]{1,0:T(8,128)(2,1)S(1)}, bf16[512,256]{1,0:T(8,128)(2,1)S(1)}, u32[]{:S(2)}, u32[]{:S(2)}) collective-permute-start(bf16[512,256]{1,0:T(8,128)(2,1)S(1)} %get-tuple-element.48), channel_id=1, source_target_pairs={{0,2},{1,3},{2,0},{3,1},{4,6},{5,7},{6,4},{7,5},{8,72},{9,73},{10,... | collective-permute-start | bytes 786440 | tf_op jit(solution)/shard_map/ppermute | solution.py:52
  24.4 9.5 %collective-permute-start.7 = (bf16[512,256]{1,0:T(8,128)(2,1)S(1)}, bf16[512,256]{1,0:T(8,128)(2,1)S(1)}, u32[]{:S(2)}, u32[]{:S(2)}) collective-permute-start(bf16[512,256]{1,0:T(8,128)(2,1)S(1)} %get-tuple-element.48), channel_id=1, source_target_pairs={{0,1},{1,2},{2,3},{3,0},{4,5},{5,6},{6,7},{7,4},{8,12},{9,13},{10,... | collective-permute-start | bytes 786440 | tf_op jit(solution)/shard_map/ppermute | solution.py:52
  34.1 25.5 %collective-permute-start.10 = (bf16[4,512,256]{2,1,0:T(8,128)(2,1)S(1)}, bf16[4,512,256]{2,1,0:T(8,128)(2,1)S(1)}, u32[]{:S(2)}, u32[]{:S(2)}) collective-permute-start(bf16[4,512,256]{2,1,0:T(8,128)(2,1)S(1)} %pad_maximum_fusion.w_ref.rest_0_), channel_id=1, source_target_pairs={{0,68},{1,69},{2,70},{3,71},{4,0},{5,1},{6,2},{7,3},{8,11},{9,8},{... | collective-permute-start | bytes 3145736 | tf_op jit(solution)/shard_map/ppermute | solution.py:52
  36.6 27.3 %collective-permute-start.9 = (bf16[4,512,256]{2,1,0:T(8,128)(2,1)S(1)}, bf16[4,512,256]{2,1,0:T(8,128)(2,1)S(1)}, u32[]{:S(2)}, u32[]{:S(2)}) collective-permute-start(bf16[4,512,256]{2,1,0:T(8,128)(2,1)S(1)} %pad_maximum_fusion.w_ref.rest_0_), channel_id=1, source_target_pairs={{0,4},{1,5},{2,6},{3,7},{4,64},{5,65},{6,66},{7,67},{8,9},{9,10},{... | collective-permute-start | bytes 3145736 | tf_op jit(solution)/shard_map/ppermute | solution.py:52
  36.6 32.2 %collective-permute-start.8 = (bf16[4,512,256]{2,1,0:T(8,128)(2,1)S(1)}, bf16[4,512,256]{2,1,0:T(8,128)(2,1)}, u32[]{:S(2)}, u32[]{:S(2)}) collective-permute-start(bf16[4,512,256]{2,1,0:T(8,128)(2,1)S(1)} %pad_maximum_fusion.w_ref.rest_0_), channel_id=1, source_target_pairs={{0,64},{1,65},{2,66},{3,67},{4,68},{5,69},{6,70},{7,71},{8,10},{9,... | collective-permute-start | bytes 3145736 | tf_op jit(solution)/shard_map/ppermute | solution.py:52
  74.8 25.4 %collective-permute-start.11 = (f32[384,256]{1,0:T(8,128)}, f32[384,256]{1,0:T(8,128)}, u32[]{:S(2)}, u32[]{:S(2)}) collective-permute-start(f32[384,256]{1,0:T(8,128)} %get-tuple-element.25), channel_id=1, source_target_pairs={{0,8},{1,9},{2,10},{3,11},{4,12},{5,13},{6,14},{7,15},{8,0},{9,1},... | collective-permute-start | bytes 1179656 | tf_op jit(solution)/shard_map/ppermute | solution.py:52
  117.4 1.4 collective-permute-start.16
  123.2 16.6 %collective-permute-start.17 = (bf16[4,256,512]{2,1,0:T(8,128)(2,1)S(1)}, bf16[4,256,512]{2,1,0:T(8,128)(2,1)S(1)}, u32[]{:S(2)}, u32[]{:S(2)}) collective-permute-start(bf16[4,256,512]{2,1,0:T(8,128)(2,1)S(1)} %grad_part.5), channel_id=1, source_target_pairs={{0,64},{1,65},{2,66},{3,67},{4,68},{5,69},{6,70},{7,71},{8,10},{9,... | collective-permute-start | bytes 3145736 | tf_op jit(solution)/shard_map/ppermute | solution.py:52
  128.2 21.9 %collective-permute-start.18 = (bf16[4,256,512]{2,1,0:T(8,128)(2,1)S(1)}, bf16[4,256,512]{2,1,0:T(8,128)(2,1)S(1)}, u32[]{:S(2)}, u32[]{:S(2)}) collective-permute-start(bf16[4,256,512]{2,1,0:T(8,128)(2,1)S(1)} %grad_part.6), channel_id=1, source_target_pairs={{0,4},{1,5},{2,6},{3,7},{4,64},{5,65},{6,66},{7,67},{8,9},{9,10},{... | collective-permute-start | bytes 3145736 | tf_op jit(solution)/shard_map/ppermute | solution.py:52
  133.2 22.3 %copy-start.2 = (bf16[4,512,256]{2,1,0:T(8,128)(2,1)S(1)}, bf16[4,512,256]{2,1,0:T(8,128)(2,1)}, u32[]{:S(2)}) copy-start(bf16[4,512,256]{2,1,0:T(8,128)(2,1)} %copy-done.1) | copy-start | bytes 3145732
  133.2 24.1 %copy-start.4 = (bf16[4,512,256]{2,1,0:T(8,128)(2,1)S(1)}, bf16[4,512,256]{2,1,0:T(8,128)(2,1)}, u32[]{:S(2)}) copy-start(bf16[4,512,256]{2,1,0:T(8,128)(2,1)} %copy-done.3) | copy-start | bytes 3145732
  133.2 28.9 %copy-start.6 = (bf16[4,512,256]{2,1,0:T(8,128)(2,1)S(1)}, bf16[4,512,256]{2,1,0:T(8,128)(2,1)}, u32[]{:S(2)}) copy-start(bf16[4,512,256]{2,1,0:T(8,128)(2,1)} %copy-done.5) | copy-start | bytes 3145732
  133.2 16.9 %collective-permute-start.19 = (bf16[4,256,512]{2,1,0:T(8,128)(2,1)S(1)}, bf16[4,256,512]{2,1,0:T(8,128)(2,1)S(1)}, u32[]{:S(2)}, u32[]{:S(2)}) collective-permute-start(bf16[4,256,512]{2,1,0:T(8,128)(2,1)S(1)} %grad_part.7), channel_id=1, source_target_pairs={{0,68},{1,69},{2,70},{3,71},{4,0},{5,1},{6,2},{7,3},{8,11},{9,8},{... | collective-permute-start | bytes 3145736 | tf_op jit(solution)/shard_map/ppermute | solution.py:52
  139.8 21.6 %copy-start.7 = (bf16[4,256,512]{2,1,0:T(8,128)(2,1)}, bf16[4,256,512]{2,1,0:T(8,128)(2,1)S(1)}, u32[]{:S(2)}) copy-start(bf16[4,256,512]{2,1,0:T(8,128)(2,1)S(1)} %grad_part.4) | copy-start | bytes 3145732
  139.8 45.7 %copy-start.13 = (bf16[384,256]{1,0:T(8,128)(2,1)S(1)}, bf16[384,256]{1,0:T(8,128)(2,1)}, u32[]{:S(2)}) copy-start(bf16[384,256]{1,0:T(8,128)(2,1)} %copy-done.12) | copy-start | bytes 589828
  151.6 7.1 %collective-permute-start.20 = (bf16[256,512]{1,0:T(8,128)(2,1)S(1)}, bf16[256,512]{1,0:T(8,128)(2,1)S(1)}, u32[]{:S(2)}, u32[]{:S(2)}) collective-permute-start(bf16[256,512]{1,0:T(8,128)(2,1)S(1)} %get-tuple-element.41), channel_id=1, source_target_pairs={{0,2},{1,3},{2,0},{3,1},{4,6},{5,7},{6,4},{7,5},{8,72},{9,73},{10,... | collective-permute-start | bytes 786440 | tf_op jit(solution)/shard_map/ppermute | solution.py:52
  151.6 9.9 %collective-permute-start.21 = (bf16[256,512]{1,0:T(8,128)(2,1)S(1)}, bf16[256,512]{1,0:T(8,128)(2,1)S(1)}, u32[]{:S(2)}, u32[]{:S(2)}) collective-permute-start(bf16[256,512]{1,0:T(8,128)(2,1)S(1)} %get-tuple-element.43), channel_id=1, source_target_pairs={{0,1},{1,2},{2,3},{3,0},{4,5},{5,6},{6,7},{7,4},{8,12},{9,13},{10,... | collective-permute-start | bytes 786440 | tf_op jit(solution)/shard_map/ppermute | solution.py:52
  155.6 9.3 %collective-permute-start.22 = (bf16[256,512]{1,0:T(8,128)(2,1)}, bf16[256,512]{1,0:T(8,128)(2,1)}, u32[]{:S(2)}, u32[]{:S(2)}) collective-permute-start(bf16[256,512]{1,0:T(8,128)(2,1)} %get-tuple-element.42), channel_id=1, source_target_pairs={{0,3},{1,0},{2,1},{3,2},{4,7},{5,4},{6,5},{7,6},{8,76},{9,77},{10,... | collective-permute-start | bytes 786440 | tf_op jit(solution)/shard_map/ppermute | solution.py:52
  155.6 30.0 %collective-permute-start.12 = (bf16[4,512,256]{2,1,0:T(8,128)(2,1)S(1)}, bf16[4,512,256]{2,1,0:T(8,128)(2,1)}, u32[]{:S(2)}, u32[]{:S(2)}) collective-permute-start(bf16[4,512,256]{2,1,0:T(8,128)(2,1)S(1)} %copy-done.2), channel_id=1, source_target_pairs={{0,8},{1,9},{2,10},{3,11},{4,12},{5,13},{6,14},{7,15},{8,0},{9,1},... | collective-permute-start | bytes 3145736 | tf_op jit(solution)/shard_map/ppermute | solution.py:52
  157.3 28.2 %collective-permute-start.13 = (bf16[4,512,256]{2,1,0:T(8,128)(2,1)S(1)}, bf16[4,512,256]{2,1,0:T(8,128)(2,1)}, u32[]{:S(2)}, u32[]{:S(2)}) collective-permute-start(bf16[4,512,256]{2,1,0:T(8,128)(2,1)S(1)} %copy-done.4), channel_id=1, source_target_pairs={{0,8},{1,9},{2,10},{3,11},{4,12},{5,13},{6,14},{7,15},{8,0},{9,1},... | collective-permute-start | bytes 3145736 | tf_op jit(solution)/shard_map/ppermute | solution.py:52
  158.6 26.9 %collective-permute-start.14 = (bf16[4,512,256]{2,1,0:T(8,128)(2,1)}, bf16[4,512,256]{2,1,0:T(8,128)(2,1)}, u32[]{:S(2)}, u32[]{:S(2)}) collective-permute-start(bf16[4,512,256]{2,1,0:T(8,128)(2,1)} %collective-permute-done.8.w_ref.rest_2_), channel_id=1, source_target_pairs={{0,8},{1,9},{2,10},{3,11},{4,12},{5,13},{6,14},{7,15},{8,0},{9,1},... | collective-permute-start | bytes 3145736 | tf_op jit(solution)/shard_map/ppermute | solution.py:52
  162.2 23.4 %collective-permute-start.15 = (bf16[4,512,256]{2,1,0:T(8,128)(2,1)S(1)}, bf16[4,512,256]{2,1,0:T(8,128)(2,1)}, u32[]{:S(2)}, u32[]{:S(2)}) collective-permute-start(bf16[4,512,256]{2,1,0:T(8,128)(2,1)S(1)} %copy-done.6), channel_id=1, source_target_pairs={{0,8},{1,9},{2,10},{3,11},{4,12},{5,13},{6,14},{7,15},{8,0},{9,1},... | collective-permute-start | bytes 3145736 | tf_op jit(solution)/shard_map/ppermute | solution.py:52
  168.0 5.3 %collective-permute-start.23 = (bf16[256,128]{1,0:T(8,128)(2,1)S(1)}, bf16[256,128]{1,0:T(8,128)(2,1)}, u32[]{:S(2)}, u32[]{:S(2)}) collective-permute-start(bf16[256,128]{1,0:T(8,128)(2,1)S(1)} %get-tuple-element.44), channel_id=1, source_target_pairs={{0,32},{1,33},{2,34},{3,35},{4,36},{5,37},{6,38},{7,39},{8,40},{9,... | collective-permute-start | bytes 196616 | tf_op jit(solution)/shard_map/ppermute | solution.py:52
  173.3 4.4 %collective-permute-start.24 = (bf16[256,128]{1,0:T(8,128)(2,1)S(1)}, bf16[256,128]{1,0:T(8,128)(2,1)}, u32[]{:S(2)}, u32[]{:S(2)}) collective-permute-start(bf16[256,128]{1,0:T(8,128)(2,1)S(1)} %get-tuple-element.46), channel_id=1, source_target_pairs={{0,16},{1,17},{2,18},{3,19},{4,20},{5,21},{6,22},{7,23},{8,24},{9,... | collective-permute-start | bytes 196616 | tf_op jit(solution)/shard_map/ppermute | solution.py:52
  177.8 3.4 %collective-permute-start.25 = (bf16[256,128]{1,0:T(8,128)(2,1)}, bf16[256,128]{1,0:T(8,128)(2,1)}, u32[]{:S(2)}, u32[]{:S(2)}) collective-permute-start(bf16[256,128]{1,0:T(8,128)(2,1)} %get-tuple-element.45), channel_id=1, source_target_pairs={{0,48},{1,49},{2,50},{3,51},{4,52},{5,53},{6,54},{7,55},{8,56},{9,... | collective-permute-start | bytes 196616 | tf_op jit(solution)/shard_map/ppermute | solution.py:52
  182.4 22.2 %collective-permute-start.26 = (f32[64,256]{0,1:T(8,128)S(1)}, f32[64,256]{0,1:T(8,128)S(1)}, u32[]{:S(2)}, u32[]{:S(2)}) collective-permute-start(f32[64,256]{0,1:T(8,128)S(1)} %get-tuple-element.54), channel_id=1, source_target_pairs={{0,8},{1,9},{2,10},{3,11},{4,12},{5,13},{6,14},{7,15},{8,0},{9,1},... | collective-permute-start | bytes 196616 | tf_op jit(solution)/shard_map/ppermute | solution.py:52
  (24 other events, 133.9 us)

commit v2 on v1

v2 whole, which is shorter than its diff:
```python
import math

import jax
import jax.numpy as jnp
import numpy as np
from jax import lax
from jax.experimental import pallas as pl
from jax.experimental.pallas import tpu as pltpu
from jax.sharding import PartitionSpec as P

HD = 128
GROUP = 8
BLK = 512
AXES = ("outer", "inner")
F32 = jnp.float32
BF16 = jnp.bfloat16
VMEM_LIMIT = 48 * 1024 * 1024
ATTENTION_LIMIT = 56 * 1024 * 1024

INDEX = np.arange(128).reshape(2, 4, 2, 2, 4)


def permutation(move):
    pairs = []
    for zh in range(2):
        for x in range(4):
            for c in range(2):
                for zl in range(2):
                    for y in range(4):
                        nx, ny, nz, nc = move(x, y, zh * 2 + zl, c)
                        nx, ny, nz = nx % 4, ny % 4, nz % 4
                        target = INDEX[nz // 2, nx, nc, nz % 2, ny]
                        pairs.append((int(INDEX[zh, x, c, zl, y]), int(target)))
    return pairs


SWAP = permutation(lambda x, y, z, c: (x, y, z, 1 - c))


def along_x(d):
    return permutation(lambda x, y, z, c: (x + d, y, z, c))


def along_u(d):
    return permutation(lambda x, y, z, c: (x, y + d * (1 - c), z + d * c, c))


def along_v(d):
    return permutation(lambda x, y, z, c: (x, y + d * c, z + d * (1 - c), c))


def permute(a, perm):
    return lax.ppermute(a, AXES, perm)


def collect(a, along):
    return [a, permute(a, along(-1)), permute(a, along(2)), permute(a, along(1))]


def distribute(parts, along):
    return [permute(parts[2], along(2)), permute(parts[1], along(1)), permute(parts[3], along(-1))]


def params(**kw):
    return pltpu.CompilerParams(vmem_limit_bytes=VMEM_LIMIT, **kw)


def prepare(tokens, doc_ids):
    rows, width = tokens.shape
    steps = 4

    def kernel(tok_ref, doc_ref, inv_ref, bias_ref):
        i = pl.program_id(0)
        a = tok_ref[...].astype(F32)
        part = jnp.sum(a * a, axis=1, keepdims=True)

        @pl.when(i == 0)
        def _():
            row = jnp.broadcast_to(doc_ref[...].astype(F32), (rows, rows))
            s = lax.broadcasted_iota(jnp.int32, (rows, rows), 0)
            t = lax.broadcasted_iota(jnp.int32, (rows, rows), 1)
            bias_ref[...] = jnp.where((s <= t) & (row == row.T), 0.0, -1e30).astype(F32)
            inv_ref[...] = part

        @pl.when(i > 0)
        def _():
            inv_ref[...] += part

        @pl.when(i == steps - 1)
        def _():
            inv_ref[...] = lax.rsqrt(inv_ref[...] * (1.0 / width) + 1e-05)

    return pl.pallas_call(
        kernel,
        out_shape=(
            jax.ShapeDtypeStruct((rows, 1), F32),
            jax.ShapeDtypeStruct((rows, rows), F32),
        ),
        grid=(steps,),
        in_specs=[
            pl.BlockSpec((rows, width // steps), lambda i: (0, i)),
            pl.BlockSpec((1, rows), lambda i: (0, 0)),
        ],
        out_specs=(
            pl.BlockSpec((rows, 1), lambda i: (0, 0)),
            pl.BlockSpec((rows, rows), lambda i: (0, 0)),
        ),
        compiler_params=params(),
        cost_estimate=pl.CostEstimate(
            flops=rows * width * 3, bytes_accessed=rows * width * 2, transcendentals=0
        ),
        name="prepare",
    )(tokens, doc_ids)


def keys_part(order, own, sib, ws, acc, base):
    rows = own.shape[0]
    cols = ws[0].shape[-1]
    first = acc is None
    n = len(ws)

    def kernel(order_ref, *refs):
        tok_refs, w_refs = refs[:8], refs[8 : 8 + n]
        rest = refs[8 + n :]
        out_own, out_sib = rest[-2:]
        i = pl.program_id(0)
        x = jnp.concatenate(
            [jnp.concatenate([tok_refs[4 * s + k][...] for k in range(4)], 1) for s in range(2)], 0
        )

        def add(w, start):
            p = jnp.dot(x, w.reshape(4 * BLK, cols), preferred_element_type=F32)
            if start and first:
                out_own[...] = p[:rows]
                out_sib[...] = p[rows:]
            elif start:
                out_own[...] = rest[0][...] + p[:rows]
                out_sib[...] = rest[1][...] + p[rows:]
            else:
                out_own[...] += p[:rows]
                out_sib[...] += p[rows:]

        for k in range(n):

            @pl.when(i == k)
            def _(k=k):
                add(w_refs[k][...], k == 0)

    tok = [
        pl.BlockSpec((rows, BLK), lambda i, o, k=k: (0, o[(base + i) * 4 + k])) for k in range(4)
    ]
    whole = pl.BlockSpec((rows, cols), lambda i, o: (0, 0))
    wspec = pl.BlockSpec((4, BLK, cols), lambda i, o: (0, 0, 0))
    out = jax.ShapeDtypeStruct((rows, cols), F32)
    return pl.pallas_call(
        kernel,
        out_shape=(out, out),
        grid_spec=pltpu.PrefetchScalarGridSpec(
            num_scalar_prefetch=1,
            grid=(n,),
            in_specs=tok + tok + [wspec] * n + ([] if first else [whole, whole]),
            out_specs=(whole, whole),
        ),
        compiler_params=params(),
        cost_estimate=pl.CostEstimate(
            flops=4 * n * rows * cols * BLK * 4,
            bytes_accessed=n * rows * BLK * 16,
            transcendentals=0,
        ),
        name="keys_part",
    )(order, *[own] * 4, *[sib] * 4, *ws, *(() if first else acc))


def attention(queries, keys_own, keys_oth, values, out_grad, inv, bias):
    rows = queries.shape[0]
    scale = HD ** (-0.5)
    cols = keys_own.shape[1]

    def kernel(q_ref, ko_ref, kt_ref, v_ref, g_ref, inv_ref, bias, *rest):
        o_ref, dk_ref, dwo_ref, dwt_ref, ms_ref, acc, kf = rest
        h = pl.program_id(0)
        core = lax.axis_index("outer") % 2
        is_own = h // 2 == core
        at = pl.ds(pl.multiple_of((h % 2) * HD, HD), HD)

        @pl.when(h == 0)
        def _():
            ms_ref[...] = jnp.zeros_like(ms_ref)

        @pl.when(is_own)
        def _():
            kf[...] = ko_ref[:, at] * inv_ref[...]

        @pl.when(jnp.logical_not(is_own))
        def _():
            kf[...] = kt_ref[:, at] * inv_ref[...]

        kb = (kf[...] * (scale * math.log2(math.e))).astype(BF16)
        vb = v_ref[...]
        vt = vb.astype(F32).T.astype(BF16)
        acc[...] = jnp.zeros_like(acc)
        for j in range(rows // HD):
            n = (j + 1) * HD
            ts = slice(j * HD, n)
            cut = [slice(a * HD, (a + 1) * HD) for a in range(GROUP)]
            q = jnp.concatenate([q_ref[ts, c] for c in cut], axis=0)
            g = jnp.concatenate([g_ref[ts, c] for c in cut], axis=0)
            sc = lax.dot_general(kb[:n], q, (((1,), (1,)), ((), ())), preferred_element_type=F32)
            sc = sc + jnp.concatenate([bias[:n, ts]] * GROUP, axis=1)
            top = jnp.max(sc, axis=0, keepdims=True)
            e = jnp.exp2(sc - top)
            p = e * (1.0 / jnp.sum(e, axis=0, keepdims=True))
            ot = jnp.dot(vt[:, :n], p.astype(BF16), preferred_element_type=F32)
            o = ot.T.astype(BF16)
            for c in cut:
                o_ref[ts, c] = o[c]
            dp = lax.dot_general(vb[:n], g, (((1,), (1,)), ((), ())), preferred_element_type=F32)
            pd = p * dp
            ds = (pd - p * jnp.sum(pd, axis=0, keepdims=True)).astype(BF16)
            acc[:n] += jnp.dot(ds, q, preferred_element_type=F32)
        dk = acc[...] * scale
        dkb = dk.astype(BF16)
        dkw = (dk * inv_ref[...]).T.astype(BF16)
        ms_ref[...] += jnp.sum(dkb.astype(F32) * kf[...], axis=1, keepdims=True)

        @pl.when(is_own)
        def _():
            dk_ref[:, at] = dkb
            dwo_ref[at, :] = dkw

        @pl.when(jnp.logical_not(is_own))
        def _():
            dk_ref[:, pl.ds(pl.multiple_of((h % 2) * HD + cols, HD), HD)] = dkb
            dwt_ref[at, :] = dkw

    wide = pl.BlockSpec((rows, GROUP * HD), lambda h: (0, h))
    head = pl.BlockSpec((rows, HD), lambda h: (0, h))

    def whole(*shape):
        return pl.BlockSpec(shape, lambda h: (0, 0))

    half = whole(rows, cols)
    halft = whole(cols, rows)
    one = whole(rows, 1)
    return pl.pallas_call(
        kernel,
        out_shape=(
            jax.ShapeDtypeStruct(queries.shape, BF16),
            jax.ShapeDtypeStruct((rows, 2 * cols), BF16),
            jax.ShapeDtypeStruct((cols, rows), BF16),
            jax.ShapeDtypeStruct((cols, rows), BF16),
            jax.ShapeDtypeStruct((rows, 1), F32),
        ),
        grid=(4,),
        in_specs=[wide, half, half, head, wide, one, whole(rows, rows)],
        out_specs=(wide, whole(rows, 2 * cols), halft, halft, one),
        scratch_shapes=[pltpu.VMEM((rows, HD), F32), pltpu.VMEM((rows, HD), F32)],
        compiler_params=pltpu.CompilerParams(vmem_limit_bytes=ATTENTION_LIMIT),
        cost_estimate=pl.CostEstimate(
            flops=8 * 32 * rows * rows * HD * 2 // 3,
            bytes_accessed=rows * 4096 * 6,
            transcendentals=32 * rows * rows * 2 // 3,
        ),
        name="attention",
    )(queries, keys_own, keys_oth, values, out_grad, inv, bias)


def grad_part(order, own, sib, dk_own, dk_sib, rvs):
    cols, rows = dk_own.shape
    n = len(rvs)

    def kernel(order_ref, *refs):
        own_refs, sib_refs = refs[:4], refs[4:8]
        a_ref, b_ref, *outs = refs[8:]
        dk = jnp.concatenate([a_ref[...], b_ref[...]], 1)
        i = pl.program_id(0)
        for k in range(4):
            x = jnp.concatenate([own_refs[k][...], sib_refs[k][...]], 0)
            p = jnp.dot(dk, x, preferred_element_type=F32).astype(BF16)
            for m in range(n):

                @pl.when(i == m)
                def _(m=m):
                    outs[m][k] = p

    base = rvs[0]
    by = rvs[1] - rvs[0] if n > 1 else 0
    tok = [
        pl.BlockSpec((rows, BLK), lambda i, o, k=k: (0, o[(base + by * i) * 4 + k]))
        for k in range(4)
    ]
    half = pl.BlockSpec((cols, rows), lambda i, o: (0, 0))
    return pl.pallas_call(
        kernel,
        out_shape=tuple(jax.ShapeDtypeStruct((4, cols, BLK), BF16) for _ in rvs),
        grid_spec=pltpu.PrefetchScalarGridSpec(
            num_scalar_prefetch=1,
            grid=(n,),
            in_specs=tok + tok + [half, half],
            out_specs=tuple(pl.BlockSpec((4, cols, BLK), lambda i, o: (0, 0, 0)) for _ in rvs),
        ),
        compiler_params=params(),
        cost_estimate=pl.CostEstimate(
            flops=4 * n * rows * cols * BLK * 4,
            bytes_accessed=n * rows * BLK * 16,
            transcendentals=0,
        ),
        name="grad_part",
    )(order, *[own] * 4, *[sib] * 4, dk_own, dk_sib)


def token_grad(place, tokens, dk, w_own, w_sib, inv, ms):
    rows, width = tokens.shape
    cols = w_own[0].shape[-1]
    step = 2

    def kernel(place_ref, tok_ref, dk_ref, *rest):
        own, sib = rest[:4], rest[4:8]
        inv_ref, ms_ref, out, w = rest[8:]
        i = pl.program_id(0)

        @pl.when(i == 0)
        def _():
            for k in range(4):
                w[4 * k : 4 * k + 4, :, :cols] = own[k][...]
            for k in range(4):
                for m in range(4):
                    w[4 * m + k, :, cols:] = sib[k][m]

        r = inv_ref[...]
        mean = ms_ref[...] * (r * r * (1.0 / width))
        for k in range(step):
            dn = lax.dot_general(
                dk_ref[...],
                w[place_ref[i * step + k]],
                (((1,), (1,)), ((), ())),
                preferred_element_type=F32,
            )
            c = slice(k * BLK, (k + 1) * BLK)
            out[:, c] = (r * dn - tok_ref[:, c].astype(F32) * mean).astype(BF16)

    tok = pl.BlockSpec((rows, BLK * step), lambda i, o: (0, i))
    one = pl.BlockSpec((rows, 1), lambda i, o: (0, 0))
    wspec = pl.BlockSpec((4, BLK, cols), lambda i, o: (0, 0, 0))
    return pl.pallas_call(
        kernel,
        out_shape=jax.ShapeDtypeStruct(tokens.shape, BF16),
        grid_spec=pltpu.PrefetchScalarGridSpec(
            num_scalar_prefetch=1,
            grid=(16 // step,),
            in_specs=[tok, pl.BlockSpec((rows, 2 * cols), lambda i, o: (0, 0))]
            + [wspec] * 8
            + [one, one],
            out_specs=tok,
            scratch_shapes=[pltpu.VMEM((16, BLK, 2 * cols), BF16)],
        ),
        compiler_params=params(),
        cost_estimate=pl.CostEstimate(
            flops=4 * rows * cols * width, bytes_accessed=rows * width * 5, transcendentals=0
        ),
        name="token_grad",
    )(place, tokens, dk, *w_own, *w_sib, inv, ms)


def per_device(tokens, queries, values, doc_ids, weight_codes, weight_scales, out_grad):
    rows, width = tokens.shape
    outer, inner = lax.axis_index("outer"), lax.axis_index("inner")
    x, core, y = (outer // 2) % 4, outer % 2, inner % 4
    z = (outer // 8) * 2 + inner // 4
    u, v = jnp.where(core == 0, y, z), jnp.where(core == 0, z, y)
    ring4 = jnp.arange(4, dtype=jnp.int32)
    bv, bu = (v + ring4[:, None]) % 4, (u + ring4[None, :]) % 4
    by, bz = jnp.where(core == 0, bu, bv), jnp.where(core == 0, bv, bu)
    order = (((bz % 2) * 4 + by) * 2 + bz // 2).reshape(16).astype(jnp.int32)
    q = jnp.arange(16, dtype=jnp.int32)
    ry, rz = (q // 2 - y) % 4, ((q % 2) * 2 + q // 8 - z) % 4
    rv, ru = jnp.where(core == 0, rz, ry), jnp.where(core == 0, ry, rz)
    place = (rv * 4 + ru).astype(jnp.int32)

    factor = jnp.exp2(weight_scales.astype(F32))
    wrows, wcols = weight_codes.shape
    weight = weight_codes.astype(F32).reshape(2, wrows // 2, wcols) * factor[:, None, :]
    weight = weight.reshape(wrows, wcols).astype(BF16)
    hc = wcols // 2
    keep = jnp.where(core == 0, weight[:, :hc], weight[:, hc:])
    send = jnp.where(core == 0, weight[:, hc:], weight[:, :hc])
    got = permute(send, SWAP)
    chip = jnp.where(
        core == 0, jnp.concatenate([keep, got], 0), jnp.concatenate([got, keep], 0)
    )
    ring = collect(chip, along_x)
    ordered = []
    for i in range(4):
        r = (i - x) % 4
        ordered.append(
            jnp.where(r == 0, ring[0], jnp.where(r == 1, ring[1], jnp.where(r == 2, ring[2], ring[3])))
        )
    block = jnp.concatenate(ordered, 0)
    tokens_later, block = lax.optimization_barrier((tokens, block))
    tokens_sib = permute(tokens_later, SWAP)
    inv, bias = prepare(tokens, doc_ids)
    plane = jnp.stack(collect(block, along_u))
    plane, inv, bias, tokens_sib, order, place = lax.optimization_barrier(
        (plane, inv, bias, tokens_sib, order, place)
    )
    w_own = collect(plane, along_v)

    acc = keys_part(order, tokens, tokens_sib, w_own[:1], None, 0)
    w_own[1], w_own[2], w_own[3], *acc = lax.optimization_barrier(
        (w_own[1], w_own[2], w_own[3], *acc)
    )
    keys_own, keys_sib = keys_part(order, tokens, tokens_sib, w_own[1:], acc, 1)
    keys_oth = permute(keys_sib, SWAP)
    w_sib = [permute(w, SWAP) for w in w_own]

    out, dk, dkw_own, dkw_oth, ms = attention(
        queries, keys_own, keys_oth, values, out_grad, inv, bias
    )
    dkw_oth, *w_sib = lax.optimization_barrier((dkw_oth, *w_sib))
    dkw_sib = permute(dkw_oth, SWAP)

    parts = [None] * 4
    for rvs in ((2,), (1, 3), (0,)):
        for r, part in zip(rvs, grad_part(order, tokens, tokens_sib, dkw_own, dkw_sib, rvs)):
            parts[r] = part
    arrived = distribute(parts, along_v)
    grad_tokens = token_grad(place, tokens, dk, w_own, w_sib, inv, ms)
    grad_tokens, parts[0], *arrived = lax.optimization_barrier((grad_tokens, parts[0], *arrived))

    def total(own, others):
        s = own.astype(F32)
        for o in others:
            s = s + o.astype(F32)
        return s

    chunk = [total(parts[0][r], [a[r] for a in arrived]) for r in range(4)]
    arrived = distribute([c.astype(BF16) for c in chunk], along_u)
    line = total(chunk[0], arrived)
    by_x = [lax.dynamic_slice_in_dim(line, ((x + r) % 4) * HD, HD, 1) for r in range(4)]
    arrived = distribute([c.astype(BF16) for c in by_x], along_x)
    mine = total(by_x[0], arrived).T
    keep = lax.dynamic_slice_in_dim(mine, core * wrows, wrows, 0)
    got = permute(lax.dynamic_slice_in_dim(mine, (1 - core) * wrows, wrows, 0), SWAP)
    grad_weight = jnp.where(
        core == 0, jnp.concatenate([keep, got], 1), jnp.concatenate([got, keep], 1)
    )
    return (out, grad_tokens, grad_weight)


def solution(mesh):
    return jax.shard_map(
        per_device,
        mesh=mesh,
        in_specs=(
            P(("outer", "inner"), None),
            P(("outer", "inner"), None),
            P(("outer", "inner"), None),
            P(("outer", "inner"), None),
            P(("inner", "outer"), None),
            P(("inner", "outer"), None),
            P(("outer", "inner"), None),
        ),
        out_specs=(
            P(("outer", "inner"), None),
            P(("outer", "inner"), None),
            P(("inner", "outer"), None),
        ),
        check_vma=False,
    )
```

time: 206 us -> 145 us (0.70)
  Pallas kernels: 85.1 us -> 55.8 us
  waiting for transfers between devices: 63.7 us -> 44.6 us
  local copies, waits for them, and re-layouts: 11.1 us -> 5.31 us
  starting transfers between devices: 37.1 us -> 33.5 us
  other arithmetic: 7.33 us -> 4.35 us
    ppermute x27, waiting for transfers between devices: 63.7 us -> 44.6 us  [permute(): return lax.ppermute(a, AXES, perm)]
    pallas_call x2 -> x1, Pallas kernels: 32.8 us -> 16.9 us  [attention(): pl.pallas_call(kernel, out_shape=(jax.ShapeDtypeStruct(queries.shape, BF1...]
    pallas_call x4 -> x2, Pallas kernels: 18.6 us -> 10.2 us  [keys_part(): pl.pallas_call(kernel, out_shape=(out, out), grid_spec=pltpu.PrefetchScal...]
    unnamed x59 -> x27, local copies, waits for them, and re-layouts: 9.87 us -> 4.96 us
    pallas_call x1, Pallas kernels: 16.2 us -> 11.9 us  [token_grad(): pl.pallas_call(kernel, out_shape=jax.ShapeDtypeStruct(tokens.shape, BF16)...]
    ppermute x27, starting transfers between devices: 37.1 us -> 33.5 us  [permute(): return lax.ppermute(a, AXES, perm)]
  transfers between devices with their start and end apart: 27 -> 27, of which waited for: 14 -> 18; matrix products, arithmetic and copies ran while one was open for 3% -> 0% of each run, Pallas kernels for 29% -> 35%
where the time goes in v2:
time: 145 us; the launch traced here: 144 us
  Pallas kernels  55.8 us (38%)
  waiting for transfers between devices  44.6 us (31%)
  starting transfers between devices  33.5 us (23%)
  local copies, waits for them, and re-layouts  5.31 us (4%)
  other arithmetic  4.35 us (3%)
    ppermute x27, waiting for transfers between devices, permute(): return lax.ppermute(a, AXES, perm)  44.6 us
    ppermute x27, starting transfers between devices, permute(): return lax.ppermute(a, AXES, perm)  33.5 us
    pallas_call x1, Pallas kernels, attention(): pl.pallas_call(kernel, out_shape=(jax.ShapeDtypeStruct(queries.shape, BF1...  16.9 us
    pallas_call x3, Pallas kernels, grad_part(): pl.pallas_call(kernel, out_shape=tuple((jax.ShapeDtypeStruct((4, cols, BL...  12.5 us
    pallas_call x1, Pallas kernels, token_grad(): pl.pallas_call(kernel, out_shape=jax.ShapeDtypeStruct(tokens.shape, BF16)...  11.9 us
    pallas_call x2, Pallas kernels, keys_part(): pl.pallas_call(kernel, out_shape=(out, out), grid_spec=pltpu.PrefetchScal...  10.2 us
    unnamed x27, local copies, waits for them, and re-layouts  4.96 us
    pallas_call x1, Pallas kernels, prepare(): pl.pallas_call(kernel, out_shape=(jax.ShapeDtypeStruct((rows, 1), F32), j...  4.32 us
  transfers between devices with their start and end apart: 27, of which 18 were waited for; matrix products, arithmetic and copies ran while one was open for 0% of the time, Pallas kernels for 35%

profile of v2, /device:TPU:1, one launch (start us, length us, event | category | flops | bytes accessed | tf_op | source)
XLA Modules:
  0.0 144.5 jit_solution(15517314946869157468)
XLA Ops:
  2.2 1.5 %collective-permute-start = (bf16[64,256]{1,0:T(8,128)(2,1)S(1)}, bf16[64,256]{1,0:T(8,128)(2,1)S(1)}, u32[]{:S(2)}, u32[]{:S(2)}) collective-permute-start(bf16[64,256]{1,0:T(8,128)(2,1)S(1)} %get-tuple-element.91), channel_id=1, source_target_pairs={{0,8},{1,9},{2,10},{3,11},{4,12},{5,13},{6,14},{7,15},{8,0},{9,1},... | collective-permute-start | bytes 98312 | tf_op jit(solution)/shard_map/ppermute | solution.py:53
  4.6 2.6 %collective-permute-start.1 = (bf16[128,256]{1,0:T(8,128)(2,1)S(1)}, bf16[128,256]{1,0:T(8,128)(2,1)S(1)}, u32[]{:S(2)}, u32[]{:S(2)}) collective-permute-start(bf16[128,256]{1,0:T(8,128)(2,1)S(1)} %maximum_select_fusion.1), channel_id=1, source_target_pairs={{0,48},{1,49},{2,50},{3,51},{4,52},{5,53},{6,54},{7,55},{8,56},{9,... | collective-permute-start | bytes 196616 | tf_op jit(solution)/shard_map/ppermute | solution.py:53
  8.6 3.3 %collective-permute-done.2 = bf16[128,256]{1,0:T(8,128)(2,1)S(1)} collective-permute-done((bf16[128,256]{1,0:T(8,128)(2,1)S(1)}, bf16[128,256]{1,0:T(8,128)(2,1)S(1)}, u32[]{:S(2)}, u32[]{:S(2)}) %collective-permute-start.2) | collective-permute-done | bytes 65568 | tf_op jit(solution)/shard_map/ppermute | solution.py:53
  11.9 1.3 collective-permute-done.3
  13.3 1.5 %collective-permute-start.7 = (bf16[384,8192]{1,0:T(8,128)(2,1)}, bf16[384,8192]{1,0:T(8,128)(2,1)}, u32[]{:S(2)}, u32[]{:S(2)}) collective-permute-start(bf16[384,8192]{1,0:T(8,128)(2,1)} %refs_3_.9), channel_id=1, source_target_pairs={{0,8},{1,9},{2,10},{3,11},{4,12},{5,13},{6,14},{7,15},{8,0},{9,1},... | collective-permute-start | bytes 18874376 | tf_op jit(solution)/shard_map/ppermute | solution.py:53
  14.9 3.8 %collective-permute-start.4 = (bf16[512,256]{1,0:T(8,128)(2,1)S(1)}, bf16[512,256]{1,0:T(8,128)(2,1)S(1)}, u32[]{:S(2)}, u32[]{:S(2)}) collective-permute-start(bf16[512,256]{1,0:T(8,128)(2,1)S(1)} %pad_maximum_fusion.1), channel_id=1, source_target_pairs={{0,3},{1,0},{2,1},{3,2},{4,7},{5,4},{6,5},{7,6},{8,76},{9,77},{10,... | collective-permute-start | bytes 786440 | tf_op jit(solution)/shard_map/ppermute | solution.py:53
  20.2 4.3 %prepare.1 = (f32[384,1]{1,0:T(8,128)S(1)}, f32[384,384]{1,0:T(8,128)S(1)}) custom-call(bf16[384,8192]{1,0:T(8,128)(2,1)} %refs_3_.9, s32[1,384]{1,0:T(1,128)S(1)} %copy-done.5), custom_call_target="tpu_custom_call" | custom-call | flops 9437184 | bytes 6291456 | tf_op jit(solution)/shard_map/prepare/pallas_call | solution.py:93
  25.5 2.7 %collective-permute-done.6 = bf16[512,256]{1,0:T(8,128)(2,1)S(1)} collective-permute-done((bf16[512,256]{1,0:T(8,128)(2,1)S(1)}, bf16[512,256]{1,0:T(8,128)(2,1)S(1)}, u32[]{:S(2)}, u32[]{:S(2)}) %collective-permute-start.6) | collective-permute-done | bytes 262176 | tf_op jit(solution)/shard_map/ppermute | solution.py:53
  29.4 1.7 %collective-permute-start.8 = (bf16[4,512,256]{2,1,0:T(8,128)(2,1)S(1)}, bf16[4,512,256]{2,1,0:T(8,128)(2,1)S(1)}, u32[]{:S(2)}, u32[]{:S(2)}) collective-permute-start(bf16[4,512,256]{2,1,0:T(8,128)(2,1)S(1)} %pad_maximum_fusion.refs_8_.rest_0_), channel_id=1, source_target_pairs={{0,68},{1,69},{2,70},{3,71},{4,0},{5,1},{6,2},{7,3},{8,11},{9,8},{... | collective-permute-start | bytes 3145736 | tf_op jit(solution)/shard_map/ppermute | solution.py:53
  31.1 1.4 collective-permute-start.9
  32.5 2.3 %collective-permute-start.12 = (bf16[4,512,256]{2,1,0:T(8,128)(2,1)S(1)}, bf16[4,512,256]{2,1,0:T(8,128)(2,1)S(1)}, u32[]{:S(2)}, u32[]{:S(2)}) collective-permute-start(bf16[4,512,256]{2,1,0:T(8,128)(2,1)S(1)} %pad_maximum_fusion.refs_8_.rest_0_), channel_id=1, source_target_pairs={{0,8},{1,9},{2,10},{3,11},{4,12},{5,13},{6,14},{7,15},{8,0},{9,1},... | collective-permute-start | bytes 3145736 | tf_op jit(solution)/shard_map/ppermute | solution.py:53
  34.8 3.4 %keys_part.2 = (f32[384,256]{1,0:T(8,128)S(1)}, f32[384,256]{1,0:T(8,128)S(1)}) custom-call(s32[16]{0:T(128)S(1)} %multiply_add_fusion.order_ref, bf16[384,8192]{1,0:T(8,128)(2,1)} %refs_3_.9, bf16[384,8192]{1,0:T(8,128)(2,1)} %refs_3_.9, bf16[384,8192]{1,0:T(8,128)(2,1)} %refs_3_.9, bf16[384,8192]{1,0:T(8,128)(2,1)} %refs_3_.9, ...), custom_call_target="tpu_custom_call" | custom-call | flops 805306368 | bytes 3145728 | tf_op jit(solution)/shard_map/keys_part/pallas_call | solution.py:155
  38.2 5.4 %collective-permute-done.10.refs_10_.rest_3_ = bf16[4,512,256]{2,1,0:T(8,128)(2,1)S(1)} collective-permute-done((bf16[4,512,256]{2,1,0:T(8,128)(2,1)S(1)}, bf16[4,512,256]{2,1,0:T(8,128)(2,1)S(1)}, u32[]{:S(2)}, u32[]{:S(2)}) %collective-permute-start.10) | collective-permute-done | bytes 1048608 | tf_op jit(solution)/shard_map/ppermute | solution.py:53
  43.6 10.5 %collective-permute-done.8.refs_8_.rest_1_ = bf16[4,512,256]{2,1,0:T(8,128)(2,1)S(1)} collective-permute-done((bf16[4,512,256]{2,1,0:T(8,128)(2,1)S(1)}, bf16[4,512,256]{2,1,0:T(8,128)(2,1)S(1)}, u32[]{:S(2)}, u32[]{:S(2)}) %collective-permute-start.8) | collective-permute-done | bytes 1048608 | tf_op jit(solution)/shard_map/ppermute | solution.py:53
  54.1 1.7 %collective-permute-done.9.refs_9_.rest_2_ = bf16[4,512,256]{2,1,0:T(8,128)(2,1)S(1)} collective-permute-done((bf16[4,512,256]{2,1,0:T(8,128)(2,1)S(1)}, bf16[4,512,256]{2,1,0:T(8,128)(2,1)S(1)}, u32[]{:S(2)}, u32[]{:S(2)}) %collective-permute-start.9) | collective-permute-done | bytes 1048608 | tf_op jit(solution)/shard_map/ppermute | solution.py:53
  55.7 2.6 %collective-permute-start.13 = (bf16[4,512,256]{2,1,0:T(8,128)(2,1)S(1)}, bf16[4,512,256]{2,1,0:T(8,128)(2,1)S(1)}, u32[]{:S(2)}, u32[]{:S(2)}) collective-permute-start(bf16[4,512,256]{2,1,0:T(8,128)(2,1)S(1)} %collective-permute-done.8.refs_8_.rest_1_), channel_id=1, source_target_pairs={{0,8},{1,9},{2,10},{3,11},{4,12},{5,13},{6,14},{7,15},{8,0},{9,1},... | collective-permute-start | bytes 3145736 | tf_op jit(solution)/shard_map/ppermute | solution.py:53
  58.9 6.8 %keys_part.3 = (f32[384,256]{1,0:T(8,128)S(1)}, f32[384,256]{1,0:T(8,128)S(1)}) custom-call(s32[16]{0:T(128)S(1)} %multiply_add_fusion.order_ref, bf16[384,8192]{1,0:T(8,128)(2,1)} %refs_3_.9, bf16[384,8192]{1,0:T(8,128)(2,1)} %refs_3_.9, bf16[384,8192]{1,0:T(8,128)(2,1)} %refs_3_.9, bf16[384,8192]{1,0:T(8,128)(2,1)} %refs_3_.9, ...), custom_call_target="tpu_custom_call" | custom-call | flops 2415919104 | bytes 9437184 | tf_op jit(solution)/shard_map/keys_part/pallas_call | solution.py:155
  66.5 1.7 %collective-permute-done.11.kt_ref = f32[384,256]{1,0:T(8,128)S(1)} collective-permute-done((f32[384,256]{1,0:T(8,128)S(1)}, f32[384,256]{1,0:T(8,128)S(1)}, u32[]{:S(2)}, u32[]{:S(2)}) %collective-permute-start.11) | collective-permute-done | bytes 393248 | tf_op jit(solution)/shard_map/ppermute | solution.py:53
  69.0 16.9 %attention.1 = (bf16[384,4096]{1,0:T(8,128)(2,1)}, bf16[384,512]{1,0:T(8,128)(2,1)}, bf16[256,384]{1,0:T(8,128)(2,1)}, bf16[256,384]{1,0:T(8,128)(2,1)}, f32[384,1]{1,0:T(8,128)}) custom-call(bf16[384,4096]{1,0:T(8,128)(2,1)} %q_ref.1, f32[384,256]{1,0:T(8,128)} %copy-done.7, f32[384,256]{1,0:T(8,128)} %copy-done.12, bf16[384,512]{1,0:T(8,128)(2,1)} %v_ref.1, ...), custom_call_target="tpu_custom_call" | custom-call | flops 3221225472 | bytes 9437184 | tf_op jit(solution)/shard_map/attention/pallas_call | solution.py:245
  86.1 1.5 %collective-permute-done.16.refs_9_ = bf16[256,384]{1,0:T(8,128)(2,1)S(1)} collective-permute-done((bf16[256,384]{1,0:T(8,128)(2,1)}, bf16[256,384]{1,0:T(8,128)(2,1)S(1)}, u32[]{:S(2)}, u32[]{:S(2)}) %collective-permute-start.16) | collective-permute-done | bytes 196640 | tf_op jit(solution)/shard_map/ppermute | solution.py:53
  88.6 5.8 %grad_part.5 = (bf16[4,256,512]{2,1,0:T(8,128)(2,1)S(1)}, bf16[4,256,512]{2,1,0:T(8,128)(2,1)S(1)}) custom-call(s32[16]{0:T(128)S(1)} %multiply_add_fusion.order_ref, bf16[384,8192]{1,0:T(8,128)(2,1)} %refs_3_.9, bf16[384,8192]{1,0:T(8,128)(2,1)} %refs_3_.9, bf16[384,8192]{1,0:T(8,128)(2,1)} %refs_3_.9, bf16[384,8192]{1,0:T(8,128)(2,1)} %refs_3_.9, ...), custom_call_target="tpu_custom_call" | custom-call | flops 1610612736 | bytes 6291456 | tf_op jit(solution)/shard_map/grad_part/pallas_call | solution.py:293
  94.5 2.6 %collective-permute-start.19 = (bf16[4,256,512]{2,1,0:T(8,128)(2,1)S(1)}, bf16[4,256,512]{2,1,0:T(8,128)(2,1)S(1)}, u32[]{:S(2)}, u32[]{:S(2)}) collective-permute-start(bf16[4,256,512]{2,1,0:T(8,128)(2,1)S(1)} %get-tuple-element.69), channel_id=1, source_target_pairs={{0,68},{1,69},{2,70},{3,71},{4,0},{5,1},{6,2},{7,3},{8,11},{9,8},{... | collective-permute-start | bytes 3145736 | tf_op jit(solution)/shard_map/ppermute | solution.py:53
  97.1 3.4 %grad_part.4 = bf16[4,256,512]{2,1,0:T(8,128)(2,1)S(1)} custom-call(s32[16]{0:T(128)S(1)} %multiply_add_fusion.order_ref, bf16[384,8192]{1,0:T(8,128)(2,1)} %refs_3_.9, bf16[384,8192]{1,0:T(8,128)(2,1)} %refs_3_.9, bf16[384,8192]{1,0:T(8,128)(2,1)} %refs_3_.9, bf16[384,8192]{1,0:T(8,128)(2,1)} %refs_3_.9, ...), custom_call_target="tpu_custom_call" | custom-call | flops 805306368 | bytes 3145728 | tf_op jit(solution)/shard_map/grad_part/pallas_call | solution.py:293
  100.6 11.9 %token_grad.1 = bf16[384,8192]{1,0:T(8,128)(2,1)} custom-call(s32[16]{0:T(128)S(1)} %fusion.10.place_ref, bf16[384,8192]{1,0:T(8,128)(2,1)} %refs_3_.9, bf16[384,512]{1,0:T(8,128)(2,1)S(1)} %copy-done.1, bf16[4,512,256]{2,1,0:T(8,128)(2,1)S(1)} %pad_maximum_fusion.refs_8_.rest_0_, bf16[4,512,256]{2,1,0:T(8,128)(2,1)S(1)} %collective-permute-done.8.refs_8_.rest_1_, ...), custom_call_target="tpu_custom_call" | custom-call | flops 3221225472 | bytes 15728640 | tf_op jit(solution)/shard_map/token_grad/pallas_call | solution.py:345
  112.5 3.4 %grad_part.3 = bf16[4,256,512]{2,1,0:T(8,128)(2,1)S(1)} custom-call(s32[16]{0:T(128)S(1)} %multiply_add_fusion.order_ref, bf16[384,8192]{1,0:T(8,128)(2,1)} %refs_3_.9, bf16[384,8192]{1,0:T(8,128)(2,1)} %refs_3_.9, bf16[384,8192]{1,0:T(8,128)(2,1)} %refs_3_.9, bf16[384,8192]{1,0:T(8,128)(2,1)} %refs_3_.9, ...), custom_call_target="tpu_custom_call" | custom-call | flops 805306368 | bytes 3145728 | tf_op jit(solution)/shard_map/grad_part/pallas_call | solution.py:293
  115.9 5.0 %collective-permute-done.18 = bf16[4,256,512]{2,1,0:T(8,128)(2,1)S(1)} collective-permute-done((bf16[4,256,512]{2,1,0:T(8,128)(2,1)S(1)}, bf16[4,256,512]{2,1,0:T(8,128)(2,1)S(1)}, u32[]{:S(2)}, u32[]{:S(2)}) %collective-permute-start.18) | collective-permute-done | bytes 1048608 | tf_op jit(solution)/shard_map/ppermute | solution.py:53
  123.0 2.2 %collective-permute-start.21 = (bf16[256,512]{1,0:T(8,128)(2,1)S(1)}, bf16[256,512]{1,0:T(8,128)(2,1)S(1)}, u32[]{:S(2)}, u32[]{:S(2)}) collective-permute-start(bf16[256,512]{1,0:T(8,128)(2,1)S(1)} %get-tuple-element.80), channel_id=1, source_target_pairs={{0,1},{1,2},{2,3},{3,0},{4,5},{5,6},{6,7},{7,4},{8,12},{9,13},{10,... | collective-permute-start | bytes 786440 | tf_op jit(solution)/shard_map/ppermute | solution.py:53
  126.4 3.9 %collective-permute-done.20 = bf16[256,512]{1,0:T(8,128)(2,1)S(1)} collective-permute-done((bf16[256,512]{1,0:T(8,128)(2,1)}, bf16[256,512]{1,0:T(8,128)(2,1)S(1)}, u32[]{:S(2)}, u32[]{:S(2)}) %collective-permute-start.20) | collective-permute-done | bytes 262176 | tf_op jit(solution)/shard_map/ppermute | solution.py:53
  130.3 2.8 %collective-permute-done.21 = bf16[256,512]{1,0:T(8,128)(2,1)S(1)} collective-permute-done((bf16[256,512]{1,0:T(8,128)(2,1)S(1)}, bf16[256,512]{1,0:T(8,128)(2,1)S(1)}, u32[]{:S(2)}, u32[]{:S(2)}) %collective-permute-start.21) | collective-permute-done | bytes 262176 | tf_op jit(solution)/shard_map/ppermute | solution.py:53
  133.0 1.3 fusion.1
  135.3 2.6 %collective-permute-start.25 = (bf16[256,128]{1,0:T(8,128)(2,1)S(1)}, bf16[256,128]{1,0:T(8,128)(2,1)S(1)}, u32[]{:S(2)}, u32[]{:S(2)}) collective-permute-start(bf16[256,128]{1,0:T(8,128)(2,1)S(1)} %get-tuple-element.82), channel_id=1, source_target_pairs={{0,48},{1,49},{2,50},{3,51},{4,52},{5,53},{6,54},{7,55},{8,56},{9,... | collective-permute-start | bytes 196616 | tf_op jit(solution)/shard_map/ppermute | solution.py:53
  140.0 2.7 %collective-permute-start.26 = (f32[64,256]{0,1:T(8,128)S(1)}, f32[64,256]{0,1:T(8,128)S(1)}, u32[]{:S(2)}, u32[]{:S(2)}) collective-permute-start(f32[64,256]{0,1:T(8,128)S(1)} %get-tuple-element.89), channel_id=1, source_target_pairs={{0,8},{1,9},{2,10},{3,11},{4,12},{5,13},{6,14},{7,15},{8,0},{9,1},... | collective-permute-start | bytes 196616 | tf_op jit(solution)/shard_map/ppermute | solution.py:53
  (76 shorter events, 19.2 us)
Async XLA Ops:
  2.2 2.4 %collective-permute-start = (bf16[64,256]{1,0:T(8,128)(2,1)S(1)}, bf16[64,256]{1,0:T(8,128)(2,1)S(1)}, u32[]{:S(2)}, u32[]{:S(2)}) collective-permute-start(bf16[64,256]{1,0:T(8,128)(2,1)S(1)} %get-tuple-element.91), channel_id=1, source_target_pairs={{0,8},{1,9},{2,10},{3,11},{4,12},{5,13},{6,14},{7,15},{8,0},{9,1},... | collective-permute-start | bytes 98312 | tf_op jit(solution)/shard_map/ppermute | solution.py:53
  4.6 4.0 %collective-permute-start.1 = (bf16[128,256]{1,0:T(8,128)(2,1)S(1)}, bf16[128,256]{1,0:T(8,128)(2,1)S(1)}, u32[]{:S(2)}, u32[]{:S(2)}) collective-permute-start(bf16[128,256]{1,0:T(8,128)(2,1)S(1)} %maximum_select_fusion.1), channel_id=1, source_target_pairs={{0,48},{1,49},{2,50},{3,51},{4,52},{5,53},{6,54},{7,55},{8,56},{9,... | collective-permute-start | bytes 196616 | tf_op jit(solution)/shard_map/ppermute | solution.py:53
  7.2 4.7 %collective-permute-start.2 = (bf16[128,256]{1,0:T(8,128)(2,1)S(1)}, bf16[128,256]{1,0:T(8,128)(2,1)S(1)}, u32[]{:S(2)}, u32[]{:S(2)}) collective-permute-start(bf16[128,256]{1,0:T(8,128)(2,1)S(1)} %maximum_select_fusion.1), channel_id=1, source_target_pairs={{0,32},{1,33},{2,34},{3,35},{4,36},{5,37},{6,38},{7,39},{8,40},{9,... | collective-permute-start | bytes 196616 | tf_op jit(solution)/shard_map/ppermute | solution.py:53
  7.8 5.5 %collective-permute-start.3 = (bf16[128,256]{1,0:T(8,128)(2,1)S(1)}, bf16[128,256]{1,0:T(8,128)(2,1)S(1)}, u32[]{:S(2)}, u32[]{:S(2)}) collective-permute-start(bf16[128,256]{1,0:T(8,128)(2,1)S(1)} %maximum_select_fusion.1), channel_id=1, source_target_pairs={{0,16},{1,17},{2,18},{3,19},{4,20},{5,21},{6,22},{7,23},{8,24},{9,... | collective-permute-start | bytes 196616 | tf_op jit(solution)/shard_map/ppermute | solution.py:53
  13.3 15.1 %collective-permute-start.7 = (bf16[384,8192]{1,0:T(8,128)(2,1)}, bf16[384,8192]{1,0:T(8,128)(2,1)}, u32[]{:S(2)}, u32[]{:S(2)}) collective-permute-start(bf16[384,8192]{1,0:T(8,128)(2,1)} %refs_3_.9), channel_id=1, source_target_pairs={{0,8},{1,9},{2,10},{3,11},{4,12},{5,13},{6,14},{7,15},{8,0},{9,1},... | collective-permute-start | bytes 18874376 | tf_op jit(solution)/shard_map/ppermute | solution.py:53
  14.9 9.9 %collective-permute-start.4 = (bf16[512,256]{1,0:T(8,128)(2,1)S(1)}, bf16[512,256]{1,0:T(8,128)(2,1)S(1)}, u32[]{:S(2)}, u32[]{:S(2)}) collective-permute-start(bf16[512,256]{1,0:T(8,128)(2,1)S(1)} %pad_maximum_fusion.1), channel_id=1, source_target_pairs={{0,3},{1,0},{2,1},{3,2},{4,7},{5,4},{6,5},{7,6},{8,76},{9,77},{10,... | collective-permute-start | bytes 786440 | tf_op jit(solution)/shard_map/ppermute | solution.py:53
  18.6 6.8 %collective-permute-start.5 = (bf16[512,256]{1,0:T(8,128)(2,1)S(1)}, bf16[512,256]{1,0:T(8,128)(2,1)S(1)}, u32[]{:S(2)}, u32[]{:S(2)}) collective-permute-start(bf16[512,256]{1,0:T(8,128)(2,1)S(1)} %pad_maximum_fusion.1), channel_id=1, source_target_pairs={{0,2},{1,3},{2,0},{3,1},{4,6},{5,7},{6,4},{7,5},{8,72},{9,73},{10,... | collective-permute-start | bytes 786440 | tf_op jit(solution)/shard_map/ppermute | solution.py:53
  18.7 9.5 %collective-permute-start.6 = (bf16[512,256]{1,0:T(8,128)(2,1)S(1)}, bf16[512,256]{1,0:T(8,128)(2,1)S(1)}, u32[]{:S(2)}, u32[]{:S(2)}) collective-permute-start(bf16[512,256]{1,0:T(8,128)(2,1)S(1)} %pad_maximum_fusion.1), channel_id=1, source_target_pairs={{0,1},{1,2},{2,3},{3,0},{4,5},{5,6},{6,7},{7,4},{8,12},{9,13},{10,... | collective-permute-start | bytes 786440 | tf_op jit(solution)/shard_map/ppermute | solution.py:53
  24.5 7.9 %copy-start.2 = (f32[384,1]{1,0:T(8,128)}, f32[384,1]{1,0:T(8,128)S(1)}, u32[]{:S(2)}) copy-start(f32[384,1]{1,0:T(8,128)S(1)} %get-tuple-element.55.inv_ref.rest_8_) | copy-start | bytes 4612
  24.6 7.9 %copy-start.6 = (f32[384,384]{1,0:T(8,128)}, f32[384,384]{1,0:T(8,128)S(1)}, u32[]{:S(2)}) copy-start(f32[384,384]{1,0:T(8,128)S(1)} %get-tuple-element.56.bias) | copy-start | bytes 1769476
  28.3 15.2 %collective-permute-start.10 = (bf16[4,512,256]{2,1,0:T(8,128)(2,1)S(1)}, bf16[4,512,256]{2,1,0:T(8,128)(2,1)S(1)}, u32[]{:S(2)}, u32[]{:S(2)}) collective-permute-start(bf16[4,512,256]{2,1,0:T(8,128)(2,1)S(1)} %pad_maximum_fusion.refs_8_.rest_0_), channel_id=1, source_target_pairs={{0,4},{1,5},{2,6},{3,7},{4,64},{5,65},{6,66},{7,67},{8,9},{9,10},{... | collective-permute-start | bytes 3145736 | tf_op jit(solution)/shard_map/ppermute | solution.py:53
  29.4 24.7 %collective-permute-start.8 = (bf16[4,512,256]{2,1,0:T(8,128)(2,1)S(1)}, bf16[4,512,256]{2,1,0:T(8,128)(2,1)S(1)}, u32[]{:S(2)}, u32[]{:S(2)}) collective-permute-start(bf16[4,512,256]{2,1,0:T(8,128)(2,1)S(1)} %pad_maximum_fusion.refs_8_.rest_0_), channel_id=1, source_target_pairs={{0,68},{1,69},{2,70},{3,71},{4,0},{5,1},{6,2},{7,3},{8,11},{9,8},{... | collective-permute-start | bytes 3145736 | tf_op jit(solution)/shard_map/ppermute | solution.py:53
  31.1 24.7 %collective-permute-start.9 = (bf16[4,512,256]{2,1,0:T(8,128)(2,1)S(1)}, bf16[4,512,256]{2,1,0:T(8,128)(2,1)S(1)}, u32[]{:S(2)}, u32[]{:S(2)}) collective-permute-start(bf16[4,512,256]{2,1,0:T(8,128)(2,1)S(1)} %pad_maximum_fusion.refs_8_.rest_0_), channel_id=1, source_target_pairs={{0,64},{1,65},{2,66},{3,67},{4,68},{5,69},{6,70},{7,71},{8,10},{9,... | collective-permute-start | bytes 3145736 | tf_op jit(solution)/shard_map/ppermute | solution.py:53
  32.5 53.4 %collective-permute-start.12 = (bf16[4,512,256]{2,1,0:T(8,128)(2,1)S(1)}, bf16[4,512,256]{2,1,0:T(8,128)(2,1)S(1)}, u32[]{:S(2)}, u32[]{:S(2)}) collective-permute-start(bf16[4,512,256]{2,1,0:T(8,128)(2,1)S(1)} %pad_maximum_fusion.refs_8_.rest_0_), channel_id=1, source_target_pairs={{0,8},{1,9},{2,10},{3,11},{4,12},{5,13},{6,14},{7,15},{8,0},{9,1},... | collective-permute-start | bytes 3145736 | tf_op jit(solution)/shard_map/ppermute | solution.py:53
  55.7 30.1 %collective-permute-start.13 = (bf16[4,512,256]{2,1,0:T(8,128)(2,1)S(1)}, bf16[4,512,256]{2,1,0:T(8,128)(2,1)S(1)}, u32[]{:S(2)}, u32[]{:S(2)}) collective-permute-start(bf16[4,512,256]{2,1,0:T(8,128)(2,1)S(1)} %collective-permute-done.8.refs_8_.rest_1_), channel_id=1, source_target_pairs={{0,8},{1,9},{2,10},{3,11},{4,12},{5,13},{6,14},{7,15},{8,0},{9,1},... | collective-permute-start | bytes 3145736 | tf_op jit(solution)/shard_map/ppermute | solution.py:53
  58.4 27.5 %collective-permute-start.14 = (bf16[4,512,256]{2,1,0:T(8,128)(2,1)S(1)}, bf16[4,512,256]{2,1,0:T(8,128)(2,1)S(1)}, u32[]{:S(2)}, u32[]{:S(2)}) collective-permute-start(bf16[4,512,256]{2,1,0:T(8,128)(2,1)S(1)} %collective-permute-done.9.refs_9_.rest_2_), channel_id=1, source_target_pairs={{0,8},{1,9},{2,10},{3,11},{4,12},{5,13},{6,14},{7,15},{8,0},{9,1},... | collective-permute-start | bytes 3145736 | tf_op jit(solution)/shard_map/ppermute | solution.py:53
  58.4 27.5 %collective-permute-start.15 = (bf16[4,512,256]{2,1,0:T(8,128)(2,1)S(1)}, bf16[4,512,256]{2,1,0:T(8,128)(2,1)}, u32[]{:S(2)}, u32[]{:S(2)}) collective-permute-start(bf16[4,512,256]{2,1,0:T(8,128)(2,1)S(1)} %collective-permute-done.10.refs_10_.rest_3_), channel_id=1, source_target_pairs={{0,8},{1,9},{2,10},{3,11},{4,12},{5,13},{6,14},{7,15},{8,0},{9,1},... | collective-permute-start | bytes 3145736 | tf_op jit(solution)/shard_map/ppermute | solution.py:53
  66.5 1.7 %collective-permute-start.11 = (f32[384,256]{1,0:T(8,128)S(1)}, f32[384,256]{1,0:T(8,128)S(1)}, u32[]{:S(2)}, u32[]{:S(2)}) collective-permute-start(f32[384,256]{1,0:T(8,128)S(1)} %get-tuple-element.54), channel_id=1, source_target_pairs={{0,8},{1,9},{2,10},{3,11},{4,12},{5,13},{6,14},{7,15},{8,0},{9,1},... | collective-permute-start | bytes 1179656 | tf_op jit(solution)/shard_map/ppermute | solution.py:53
  85.9 8.5 %copy-start.8 = (bf16[4,512,256]{2,1,0:T(8,128)(2,1)}, bf16[4,512,256]{2,1,0:T(8,128)(2,1)S(1)}, u32[]{:S(2)}) copy-start(bf16[4,512,256]{2,1,0:T(8,128)(2,1)S(1)} %collective-permute-done.13.rest_5_) | copy-start | bytes 3145732
  85.9 8.5 %copy-start.9 = (bf16[4,512,256]{2,1,0:T(8,128)(2,1)}, bf16[4,512,256]{2,1,0:T(8,128)(2,1)S(1)}, u32[]{:S(2)}) copy-start(bf16[4,512,256]{2,1,0:T(8,128)(2,1)S(1)} %collective-permute-done.14.rest_6_) | copy-start | bytes 3145732
  85.9 1.7 %collective-permute-start.16 = (bf16[256,384]{1,0:T(8,128)(2,1)}, bf16[256,384]{1,0:T(8,128)(2,1)S(1)}, u32[]{:S(2)}, u32[]{:S(2)}) collective-permute-start(bf16[256,384]{1,0:T(8,128)(2,1)} %get-tuple-element.67), channel_id=1, source_target_pairs={{0,8},{1,9},{2,10},{3,11},{4,12},{5,13},{6,14},{7,15},{8,0},{9,1},... | collective-permute-start | bytes 589832 | tf_op jit(solution)/shard_map/ppermute | solution.py:53
  94.4 26.5 %collective-permute-start.18 = (bf16[4,256,512]{2,1,0:T(8,128)(2,1)S(1)}, bf16[4,256,512]{2,1,0:T(8,128)(2,1)S(1)}, u32[]{:S(2)}, u32[]{:S(2)}) collective-permute-start(bf16[4,256,512]{2,1,0:T(8,128)(2,1)S(1)} %get-tuple-element.68), channel_id=1, source_target_pairs={{0,4},{1,5},{2,6},{3,7},{4,64},{5,65},{6,66},{7,67},{8,9},{9,10},{... | collective-permute-start | bytes 3145736 | tf_op jit(solution)/shard_map/ppermute | solution.py:53
  94.5 6.1 %copy-start.1 = (bf16[384,512]{1,0:T(8,128)(2,1)S(1)}, bf16[384,512]{1,0:T(8,128)(2,1)}, u32[]{:S(2)}) copy-start(bf16[384,512]{1,0:T(8,128)(2,1)} %get-tuple-element.59.dk_ref) | copy-start | bytes 1179652
  94.5 26.3 %collective-permute-start.19 = (bf16[4,256,512]{2,1,0:T(8,128)(2,1)S(1)}, bf16[4,256,512]{2,1,0:T(8,128)(2,1)S(1)}, u32[]{:S(2)}, u32[]{:S(2)}) collective-permute-start(bf16[4,256,512]{2,1,0:T(8,128)(2,1)S(1)} %get-tuple-element.69), channel_id=1, source_target_pairs={{0,68},{1,69},{2,70},{3,71},{4,0},{5,1},{6,2},{7,3},{8,11},{9,8},{... | collective-permute-start | bytes 3145736 | tf_op jit(solution)/shard_map/ppermute | solution.py:53
  100.5 20.3 %collective-permute-start.17 = (bf16[4,256,512]{2,1,0:T(8,128)(2,1)S(1)}, bf16[4,256,512]{2,1,0:T(8,128)(2,1)S(1)}, u32[]{:S(2)}, u32[]{:S(2)}) collective-permute-start(bf16[4,256,512]{2,1,0:T(8,128)(2,1)S(1)} %grad_part.4), channel_id=1, source_target_pairs={{0,64},{1,65},{2,66},{3,67},{4,68},{5,69},{6,70},{7,71},{8,10},{9,... | collective-permute-start | bytes 3145736 | tf_op jit(solution)/shard_map/ppermute | solution.py:53
  123.0 7.3 %collective-permute-start.20 = (bf16[256,512]{1,0:T(8,128)(2,1)}, bf16[256,512]{1,0:T(8,128)(2,1)S(1)}, u32[]{:S(2)}, u32[]{:S(2)}) collective-permute-start(bf16[256,512]{1,0:T(8,128)(2,1)} %get-tuple-element.78), channel_id=1, source_target_pairs={{0,2},{1,3},{2,0},{3,1},{4,6},{5,7},{6,4},{7,5},{8,72},{9,73},{10,... | collective-permute-start | bytes 786440 | tf_op jit(solution)/shard_map/ppermute | solution.py:53
  123.0 10.0 %collective-permute-start.21 = (bf16[256,512]{1,0:T(8,128)(2,1)S(1)}, bf16[256,512]{1,0:T(8,128)(2,1)S(1)}, u32[]{:S(2)}, u32[]{:S(2)}) collective-permute-start(bf16[256,512]{1,0:T(8,128)(2,1)S(1)} %get-tuple-element.80), channel_id=1, source_target_pairs={{0,1},{1,2},{2,3},{3,0},{4,5},{5,6},{6,7},{7,4},{8,12},{9,13},{10,... | collective-permute-start | bytes 786440 | tf_op jit(solution)/shard_map/ppermute | solution.py:53
  125.2 7.9 %collective-permute-start.22 = (bf16[256,512]{1,0:T(8,128)(2,1)S(1)}, bf16[256,512]{1,0:T(8,128)(2,1)S(1)}, u32[]{:S(2)}, u32[]{:S(2)}) collective-permute-start(bf16[256,512]{1,0:T(8,128)(2,1)S(1)} %get-tuple-element.79), channel_id=1, source_target_pairs={{0,3},{1,0},{2,1},{3,2},{4,7},{5,4},{6,5},{7,6},{8,76},{9,77},{10,... | collective-permute-start | bytes 786440 | tf_op jit(solution)/shard_map/ppermute | solution.py:53
  134.4 4.7 %collective-permute-start.23 = (bf16[256,128]{1,0:T(8,128)(2,1)S(1)}, bf16[256,128]{1,0:T(8,128)(2,1)S(1)}, u32[]{:S(2)}, u32[]{:S(2)}) collective-permute-start(bf16[256,128]{1,0:T(8,128)(2,1)S(1)} %get-tuple-element.81), channel_id=1, source_target_pairs={{0,32},{1,33},{2,34},{3,35},{4,36},{5,37},{6,38},{7,39},{8,40},{9,... | collective-permute-start | bytes 196616 | tf_op jit(solution)/shard_map/ppermute | solution.py:53
  135.2 4.6 %collective-permute-start.24 = (bf16[256,128]{1,0:T(8,128)(2,1)S(1)}, bf16[256,128]{1,0:T(8,128)(2,1)S(1)}, u32[]{:S(2)}, u32[]{:S(2)}) collective-permute-start(bf16[256,128]{1,0:T(8,128)(2,1)S(1)} %get-tuple-element.83), channel_id=1, source_target_pairs={{0,16},{1,17},{2,18},{3,19},{4,20},{5,21},{6,22},{7,23},{8,24},{9,... | collective-permute-start | bytes 196616 | tf_op jit(solution)/shard_map/ppermute | solution.py:53
  135.3 4.5 %collective-permute-start.25 = (bf16[256,128]{1,0:T(8,128)(2,1)S(1)}, bf16[256,128]{1,0:T(8,128)(2,1)S(1)}, u32[]{:S(2)}, u32[]{:S(2)}) collective-permute-start(bf16[256,128]{1,0:T(8,128)(2,1)S(1)} %get-tuple-element.82), channel_id=1, source_target_pairs={{0,48},{1,49},{2,50},{3,51},{4,52},{5,53},{6,54},{7,55},{8,56},{9,... | collective-permute-start | bytes 196616 | tf_op jit(solution)/shard_map/ppermute | solution.py:53
  140.0 3.7 %collective-permute-start.26 = (f32[64,256]{0,1:T(8,128)S(1)}, f32[64,256]{0,1:T(8,128)S(1)}, u32[]{:S(2)}, u32[]{:S(2)}) collective-permute-start(f32[64,256]{0,1:T(8,128)S(1)} %get-tuple-element.89), channel_id=1, source_target_pairs={{0,8},{1,9},{2,10},{3,11},{4,12},{5,13},{6,14},{7,15},{8,0},{9,1},... | collective-permute-start | bytes 196616 | tf_op jit(solution)/shard_map/ppermute | solution.py:53
  (8 other events, 17.6 us)

commit v3 on v2

--- a/solution.py
+++ b/solution.py
@@ -13,9 +13,10 @@
 BLK = 512
 AXES = ("outer", "inner")
 F32 = jnp.float32
+NT = (((1,), (1,)), ((), ()))
 BF16 = jnp.bfloat16
 VMEM_LIMIT = 48 * 1024 * 1024
-ATTENTION_LIMIT = 56 * 1024 * 1024
+ATTENTION_LIMIT = 40 * 1024 * 1024
 
 INDEX = np.arange(128).reshape(2, 4, 2, 2, 4)
 
@@ -54,7 +55,8 @@
 
 
 def collect(a, along):
-    return [a, permute(a, along(-1)), permute(a, along(2)), permute(a, along(1))]
+    two, right, left = (permute(a, along(d)) for d in (2, 1, -1))
+    return [a, left, two, right]
 
 
 def distribute(parts, along):
@@ -113,7 +115,7 @@
     )(tokens, doc_ids)
 
 
-def keys_part(order, own, sib, ws, acc, base):
+def keys_part(order, own, sib, ws, acc, rvs):
     rows = own.shape[0]
     cols = ws[0].shape[-1]
     first = acc is None
@@ -147,7 +149,7 @@
                 add(w_refs[k][...], k == 0)
 
     tok = [
-        pl.BlockSpec((rows, BLK), lambda i, o, k=k: (0, o[(base + i) * 4 + k])) for k in range(4)
+        pl.BlockSpec((rows, BLK), lambda i, o, k=k: (0, o[(rvs[0] + i) * 4 + k])) for k in range(4)
     ]
     whole = pl.BlockSpec((rows, cols), lambda i, o: (0, 0))
     wspec = pl.BlockSpec((4, BLK, cols), lambda i, o: (0, 0, 0))
@@ -199,25 +201,46 @@
         vb = v_ref[...]
         vt = vb.astype(F32).T.astype(BF16)
         acc[...] = jnp.zeros_like(acc)
-        for j in range(rows // HD):
+
+        def scores(j, part):
             n = (j + 1) * HD
             ts = slice(j * HD, n)
-            cut = [slice(a * HD, (a + 1) * HD) for a in range(GROUP)]
+            cut = [slice(a * HD, (a + 1) * HD) for a in part]
             q = jnp.concatenate([q_ref[ts, c] for c in cut], axis=0)
             g = jnp.concatenate([g_ref[ts, c] for c in cut], axis=0)
-            sc = lax.dot_general(kb[:n], q, (((1,), (1,)), ((), ())), preferred_element_type=F32)
-            sc = sc + jnp.concatenate([bias[:n, ts]] * GROUP, axis=1)
+            sc = lax.dot_general(kb[:n], q, NT, preferred_element_type=F32)
+            return q, sc, lax.dot_general(vb[:n], g, NT, preferred_element_type=F32)
+
+        def soften(j, part, sc, dp):
+            n = (j + 1) * HD
+            sc = sc + jnp.concatenate([bias[:n, j * HD : n]] * len(part), axis=1)
             top = jnp.max(sc, axis=0, keepdims=True)
             e = jnp.exp2(sc - top)
             p = e * (1.0 / jnp.sum(e, axis=0, keepdims=True))
-            ot = jnp.dot(vt[:, :n], p.astype(BF16), preferred_element_type=F32)
-            o = ot.T.astype(BF16)
-            for c in cut:
-                o_ref[ts, c] = o[c]
-            dp = lax.dot_general(vb[:n], g, (((1,), (1,)), ((), ())), preferred_element_type=F32)
             pd = p * dp
             ds = (pd - p * jnp.sum(pd, axis=0, keepdims=True)).astype(BF16)
+            return p.astype(BF16), ds
+
+        def finish(j, part, q, pb, ds):
+            n = (j + 1) * HD
+            ot = jnp.dot(vt[:, :n], pb, preferred_element_type=F32)
+            o = ot.T.astype(BF16)
+            for k, a in enumerate(part):
+                o_ref[j * HD : n, a * HD : (a + 1) * HD] = o[k * HD : (k + 1) * HD]
             acc[:n] += jnp.dot(ds, q, preferred_element_type=F32)
+
+        tiles = [(j, range(a, a + 4)) for j in (2, 1, 0) for a in (0, 4)]
+        now = scores(*tiles[0])
+        before = None
+        for i, tile in enumerate(tiles):
+            later = scores(*tiles[i + 1]) if i + 1 < len(tiles) else None
+            q, sc, dp = now
+            soft = soften(*tile, sc, dp)
+            if before is not None:
+                finish(*before)
+            before = (*tile, q, *soft)
+            now = later
+        finish(*before)
         dk = acc[...] * scale
         dkb = dk.astype(BF16)
         dkw = (dk * inv_ref[...]).T.astype(BF16)
@@ -265,48 +288,35 @@
     )(queries, keys_own, keys_oth, values, out_grad, inv, bias)
 
 
-def grad_part(order, own, sib, dk_own, dk_sib, rvs):
+def grad_part(order, own, sib, dk_own, dk_sib, rv):
     cols, rows = dk_own.shape
-    n = len(rvs)
 
     def kernel(order_ref, *refs):
-        own_refs, sib_refs = refs[:4], refs[4:8]
-        a_ref, b_ref, *outs = refs[8:]
+        a_ref, b_ref, out = refs[4:]
         dk = jnp.concatenate([a_ref[...], b_ref[...]], 1)
-        i = pl.program_id(0)
-        for k in range(4):
-            x = jnp.concatenate([own_refs[k][...], sib_refs[k][...]], 0)
-            p = jnp.dot(dk, x, preferred_element_type=F32).astype(BF16)
-            for m in range(n):
-
-                @pl.when(i == m)
-                def _(m=m):
-                    outs[m][k] = p
-
-    base = rvs[0]
-    by = rvs[1] - rvs[0] if n > 1 else 0
+        for k in range(2):
+            x = jnp.concatenate([refs[k][...], refs[2 + k][...]], 0)
+            out[k] = jnp.dot(dk, x, preferred_element_type=F32).astype(BF16)
+
     tok = [
-        pl.BlockSpec((rows, BLK), lambda i, o, k=k: (0, o[(base + by * i) * 4 + k]))
-        for k in range(4)
+        pl.BlockSpec((rows, BLK), lambda i, o, k=k: (0, o[rv * 4 + 2 * i + k])) for k in range(2)
     ]
     half = pl.BlockSpec((cols, rows), lambda i, o: (0, 0))
     return pl.pallas_call(
         kernel,
-        out_shape=tuple(jax.ShapeDtypeStruct((4, cols, BLK), BF16) for _ in rvs),
+        out_shape=jax.ShapeDtypeStruct((4, cols, BLK), BF16),
         grid_spec=pltpu.PrefetchScalarGridSpec(
             num_scalar_prefetch=1,
-            grid=(n,),
+            grid=(2,),
             in_specs=tok + tok + [half, half],
-            out_specs=tuple(pl.BlockSpec((4, cols, BLK), lambda i, o: (0, 0, 0)) for _ in rvs),
+            out_specs=pl.BlockSpec((2, cols, BLK), lambda i, o: (i, 0, 0)),
         ),
         compiler_params=params(),
         cost_estimate=pl.CostEstimate(
-            flops=4 * n * rows * cols * BLK * 4,
-            bytes_accessed=n * rows * BLK * 16,
-            transcendentals=0,
+            flops=4 * rows * cols * BLK * 4, bytes_accessed=rows * BLK * 16, transcendentals=0
         ),
         name="grad_part",
-    )(order, *[own] * 4, *[sib] * 4, dk_own, dk_sib)
+    )(order, *[own] * 2, *[sib] * 2, dk_own, dk_sib)
 
 
 def token_grad(place, tokens, dk, w_own, w_sib, inv, ms):
@@ -333,7 +343,7 @@
             dn = lax.dot_general(
                 dk_ref[...],
                 w[place_ref[i * step + k]],
-                (((1,), (1,)), ((), ())),
+                NT,
                 preferred_element_type=F32,
             )
             c = slice(k * BLK, (k + 1) * BLK)
@@ -388,6 +398,8 @@
     chip = jnp.where(
         core == 0, jnp.concatenate([keep, got], 0), jnp.concatenate([got, keep], 0)
     )
+    tokens_later, chip = lax.optimization_barrier((tokens, chip))
+    tokens_sib = permute(tokens_later, SWAP)
     ring = collect(chip, along_x)
     ordered = []
     for i in range(4):
@@ -396,20 +408,18 @@
             jnp.where(r == 0, ring[0], jnp.where(r == 1, ring[1], jnp.where(r == 2, ring[2], ring[3])))
         )
     block = jnp.concatenate(ordered, 0)
-    tokens_later, block = lax.optimization_barrier((tokens, block))
-    tokens_sib = permute(tokens_later, SWAP)
-    inv, bias = prepare(tokens, doc_ids)
     plane = jnp.stack(collect(block, along_u))
-    plane, inv, bias, tokens_sib, order, place = lax.optimization_barrier(
-        (plane, inv, bias, tokens_sib, order, place)
+    plane, tokens_now, tokens_sib, order, place = lax.optimization_barrier(
+        (plane, tokens, tokens_sib, order, place)
     )
     w_own = collect(plane, along_v)
 
-    acc = keys_part(order, tokens, tokens_sib, w_own[:1], None, 0)
-    w_own[1], w_own[2], w_own[3], *acc = lax.optimization_barrier(
-        (w_own[1], w_own[2], w_own[3], *acc)
-    )
-    keys_own, keys_sib = keys_part(order, tokens, tokens_sib, w_own[1:], acc, 1)
+    acc = keys_part(order, tokens, tokens_sib, w_own[:1], None, (0,))
+    inv, bias = prepare(tokens_now, doc_ids)
+    w_own[3], inv, bias, *acc = lax.optimization_barrier((w_own[3], inv, bias, *acc))
+    acc = keys_part(order, tokens, tokens_sib, w_own[3:], acc, (3,))
+    w_own[1], w_own[2], *acc = lax.optimization_barrier((w_own[1], w_own[2], *acc))
+    keys_own, keys_sib = keys_part(order, tokens, tokens_sib, w_own[1:3], acc, (1, 2))
     keys_oth = permute(keys_sib, SWAP)
     w_sib = [permute(w, SWAP) for w in w_own]
 
@@ -420,9 +430,8 @@
     dkw_sib = permute(dkw_oth, SWAP)
 
     parts = [None] * 4
-    for rvs in ((2,), (1, 3), (0,)):
-        for r, part in zip(rvs, grad_part(order, tokens, tokens_sib, dkw_own, dkw_sib, rvs)):
-            parts[r] = part
+    for r in (2, 1, 3, 0):
+        parts[r] = grad_part(order, tokens, tokens_sib, dkw_own, dkw_sib, r)
     arrived = distribute(parts, along_v)
     grad_tokens = token_grad(place, tokens, dk, w_own, w_sib, inv, ms)
     grad_tokens, parts[0], *arrived = lax.optimization_barrier((grad_tokens, parts[0], *arrived))

time: 145 us -> 142 us (0.979)
  waiting for transfers between devices: 44.6 us -> 39.7 us
  starting transfers between devices: 33.5 us -> 38 us
  Pallas kernels: 55.8 us -> 54.2 us
    ppermute x27, waiting for transfers between devices: 44.6 us -> 39.7 us  [permute(): return lax.ppermute(a, AXES, perm)]
    ppermute x27, starting transfers between devices: 33.5 us -> 38 us  [permute(): return lax.ppermute(a, AXES, perm)]
    pallas_call x1, Pallas kernels: 16.9 us -> 13.4 us  [attention(): pl.pallas_call(kernel, out_shape=(jax.ShapeDtypeStruct(queries.shape, BF1...]
    pallas_call x2 -> x3, Pallas kernels: 10.2 us -> 11.8 us  [keys_part(): pl.pallas_call(kernel, out_shape=(out, out), grid_spec=pltpu.PrefetchScal...]
    unnamed x27 -> x19, local copies, waits for them, and re-layouts: 4.96 us -> 4.37 us
    pallas_call x3 -> x4, Pallas kernels: 12.5 us -> 12.8 us  [grad_part(): pl.pallas_call(kernel, out_shape=jax.ShapeDtypeStruct((4, cols, BLK), BF1...]
  transfers between devices with their start and end apart: 27 -> 27, of which waited for: 18 -> 17; matrix products, arithmetic and copies ran while one was open for 0% -> 0% of each run, Pallas kernels for 35% -> 36%
where the time goes in v3:
time: 142 us
  Pallas kernels  54.2 us (38%)
  waiting for transfers between devices  39.7 us (28%)
  starting transfers between devices  38 us (27%)
  local copies, waits for them, and re-layouts  4.72 us (3%)
  other arithmetic  4.37 us (3%)
    ppermute x27, waiting for transfers between devices, permute(): return lax.ppermute(a, AXES, perm)  39.7 us
    ppermute x27, starting transfers between devices, permute(): return lax.ppermute(a, AXES, perm)  38 us
    pallas_call x1, Pallas kernels, attention(): pl.pallas_call(kernel, out_shape=(jax.ShapeDtypeStruct(queries.shape, BF1...  13.4 us
    pallas_call x4, Pallas kernels, grad_part(): pl.pallas_call(kernel, out_shape=jax.ShapeDtypeStruct((4, cols, BLK), BF1...  12.8 us
    pallas_call x1, Pallas kernels, token_grad(): pl.pallas_call(kernel, out_shape=jax.ShapeDtypeStruct(tokens.shape, BF16)...  11.9 us
    pallas_call x3, Pallas kernels, keys_part(): pl.pallas_call(kernel, out_shape=(out, out), grid_spec=pltpu.PrefetchScal...  11.8 us
    unnamed x19, local copies, waits for them, and re-layouts  4.37 us
    pallas_call x1, Pallas kernels, prepare(): pl.pallas_call(kernel, out_shape=(jax.ShapeDtypeStruct((rows, 1), F32), j...  4.32 us
  transfers between devices with their start and end apart: 27, of which 17 were waited for; matrix products, arithmetic and copies ran while one was open for 0% of the time, Pallas kernels for 36%

profile of v3, /device:TPU:1, one launch (start us, length us, event | category | flops | bytes accessed | tf_op | source)
XLA Modules:
  0.0 141.8 jit_solution(3457588078056004428)
XLA Ops:
  2.2 1.5 %collective-permute-start = (bf16[64,256]{1,0:T(8,128)(2,1)S(1)}, bf16[64,256]{1,0:T(8,128)(2,1)S(1)}, u32[]{:S(2)}, u32[]{:S(2)}) collective-permute-start(bf16[64,256]{1,0:T(8,128)(2,1)S(1)} %get-tuple-element.99), channel_id=1, source_target_pairs={{0,8},{1,9},{2,10},{3,11},{4,12},{5,13},{6,14},{7,15},{8,0},{9,1},... | collective-permute-start | bytes 98312 | tf_op jit(solution)/shard_map/ppermute | solution.py:54
  5.0 2.6 %collective-permute-start.1 = (bf16[128,256]{1,0:T(8,128)(2,1)S(1)}, bf16[128,256]{1,0:T(8,128)(2,1)S(1)}, u32[]{:S(2)}, u32[]{:S(2)}) collective-permute-start(bf16[128,256]{1,0:T(8,128)(2,1)S(1)} %maximum_select_fusion.1), channel_id=1, source_target_pairs={{0,48},{1,49},{2,50},{3,51},{4,52},{5,53},{6,54},{7,55},{8,56},{9,... | collective-permute-start | bytes 196616 | tf_op jit(solution)/shard_map/ppermute | solution.py:54
  9.0 3.3 %collective-permute-done.2 = bf16[128,256]{1,0:T(8,128)(2,1)S(1)} collective-permute-done((bf16[128,256]{1,0:T(8,128)(2,1)S(1)}, bf16[128,256]{1,0:T(8,128)(2,1)S(1)}, u32[]{:S(2)}, u32[]{:S(2)}) %collective-permute-start.2) | collective-permute-done | bytes 65568 | tf_op jit(solution)/shard_map/ppermute | solution.py:54
  12.3 1.9 %collective-permute-done.3 = bf16[128,256]{1,0:T(8,128)(2,1)S(1)} collective-permute-done((bf16[128,256]{1,0:T(8,128)(2,1)S(1)}, bf16[128,256]{1,0:T(8,128)(2,1)S(1)}, u32[]{:S(2)}, u32[]{:S(2)}) %collective-permute-start.3) | collective-permute-done | bytes 65568 | tf_op jit(solution)/shard_map/ppermute | solution.py:54
  14.3 3.8 %collective-permute-start.4 = (bf16[512,256]{1,0:T(8,128)(2,1)S(1)}, bf16[512,256]{1,0:T(8,128)(2,1)S(1)}, u32[]{:S(2)}, u32[]{:S(2)}) collective-permute-start(bf16[512,256]{1,0:T(8,128)(2,1)S(1)} %get-tuple-element.91), channel_id=1, source_target_pairs={{0,3},{1,0},{2,1},{3,2},{4,7},{5,4},{6,5},{7,6},{8,76},{9,77},{10,... | collective-permute-start | bytes 786440 | tf_op jit(solution)/shard_map/ppermute | solution.py:54
  19.0 5.2 %collective-permute-done.4 = bf16[512,256]{1,0:T(8,128)(2,1)S(1)} collective-permute-done((bf16[512,256]{1,0:T(8,128)(2,1)S(1)}, bf16[512,256]{1,0:T(8,128)(2,1)S(1)}, u32[]{:S(2)}, u32[]{:S(2)}) %collective-permute-start.4) | collective-permute-done | bytes 262176 | tf_op jit(solution)/shard_map/ppermute | solution.py:54
  25.2 2.5 %collective-permute-done.6 = bf16[512,256]{1,0:T(8,128)(2,1)S(1)} collective-permute-done((bf16[512,256]{1,0:T(8,128)(2,1)S(1)}, bf16[512,256]{1,0:T(8,128)(2,1)S(1)}, u32[]{:S(2)}, u32[]{:S(2)}) %collective-permute-start.6) | collective-permute-done | bytes 262176 | tf_op jit(solution)/shard_map/ppermute | solution.py:54
  28.9 1.7 %collective-permute-start.8 = (bf16[4,512,256]{2,1,0:T(8,128)(2,1)S(1)}, bf16[4,512,256]{2,1,0:T(8,128)(2,1)S(1)}, u32[]{:S(2)}, u32[]{:S(2)}) collective-permute-start(bf16[4,512,256]{2,1,0:T(8,128)(2,1)S(1)} %pad_maximum_fusion.refs_8_.rest_0_), channel_id=1, source_target_pairs={{0,68},{1,69},{2,70},{3,71},{4,0},{5,1},{6,2},{7,3},{8,11},{9,8},{... | collective-permute-start | bytes 3145736 | tf_op jit(solution)/shard_map/ppermute | solution.py:54
  30.6 1.4 collective-permute-start.9
  32.0 3.1 %collective-permute-start.12 = (bf16[4,512,256]{2,1,0:T(8,128)(2,1)S(1)}, bf16[4,512,256]{2,1,0:T(8,128)(2,1)S(1)}, u32[]{:S(2)}, u32[]{:S(2)}) collective-permute-start(bf16[4,512,256]{2,1,0:T(8,128)(2,1)S(1)} %pad_maximum_fusion.refs_8_.rest_0_), channel_id=1, source_target_pairs={{0,8},{1,9},{2,10},{3,11},{4,12},{5,13},{6,14},{7,15},{8,0},{9,1},... | collective-permute-start | bytes 3145736 | tf_op jit(solution)/shard_map/ppermute | solution.py:54
  35.7 4.3 %prepare.1 = (f32[384,1]{1,0:T(8,128)S(1)}, f32[384,384]{1,0:T(8,128)S(1)}) custom-call(bf16[384,8192]{1,0:T(8,128)(2,1)} %refs_1_.13, s32[1,384]{1,0:T(1,128)S(1)} %copy-done), custom_call_target="tpu_custom_call" | custom-call | flops 9437184 | bytes 6291456 | tf_op jit(solution)/shard_map/prepare/pallas_call | solution.py:95
  40.1 3.4 %keys_part.3 = (f32[384,256]{1,0:T(8,128)S(1)}, f32[384,256]{1,0:T(8,128)S(1)}) custom-call(s32[16]{0:T(128)S(1)} %multiply_add_fusion.order_ref, bf16[384,8192]{1,0:T(8,128)(2,1)} %refs_1_.13, bf16[384,8192]{1,0:T(8,128)(2,1)} %refs_1_.13, bf16[384,8192]{1,0:T(8,128)(2,1)} %refs_1_.13, bf16[384,8192]{1,0:T(8,128)(2,1)} %refs_1_.13, ...), custom_call_target="tpu_custom_call" | custom-call | flops 805306368 | bytes 3145728 | tf_op jit(solution)/shard_map/keys_part/pallas_call | solution.py:157
  43.5 3.4 %keys_part.4 = (f32[384,256]{1,0:T(8,128)S(1)}, f32[384,256]{1,0:T(8,128)S(1)}) custom-call(s32[16]{0:T(128)S(1)} %multiply_add_fusion.order_ref, bf16[384,8192]{1,0:T(8,128)(2,1)} %refs_1_.13, bf16[384,8192]{1,0:T(8,128)(2,1)} %refs_1_.13, bf16[384,8192]{1,0:T(8,128)(2,1)} %refs_1_.13, bf16[384,8192]{1,0:T(8,128)(2,1)} %refs_1_.13, ...), custom_call_target="tpu_custom_call" | custom-call | flops 805306368 | bytes 3145728 | tf_op jit(solution)/shard_map/keys_part/pallas_call | solution.py:157
  46.8 6.7 %collective-permute-done.8.refs_8_.rest_1_ = bf16[4,512,256]{2,1,0:T(8,128)(2,1)S(1)} collective-permute-done((bf16[4,512,256]{2,1,0:T(8,128)(2,1)S(1)}, bf16[4,512,256]{2,1,0:T(8,128)(2,1)S(1)}, u32[]{:S(2)}, u32[]{:S(2)}) %collective-permute-start.8) | collective-permute-done | bytes 1048608 | tf_op jit(solution)/shard_map/ppermute | solution.py:54
  53.6 1.7 %collective-permute-done.9.refs_9_.rest_2_ = bf16[4,512,256]{2,1,0:T(8,128)(2,1)S(1)} collective-permute-done((bf16[4,512,256]{2,1,0:T(8,128)(2,1)S(1)}, bf16[4,512,256]{2,1,0:T(8,128)(2,1)S(1)}, u32[]{:S(2)}, u32[]{:S(2)}) %collective-permute-start.9) | collective-permute-done | bytes 1048608 | tf_op jit(solution)/shard_map/ppermute | solution.py:54
  55.2 3.4 %collective-permute-start.13 = (bf16[4,512,256]{2,1,0:T(8,128)(2,1)S(1)}, bf16[4,512,256]{2,1,0:T(8,128)(2,1)S(1)}, u32[]{:S(2)}, u32[]{:S(2)}) collective-permute-start(bf16[4,512,256]{2,1,0:T(8,128)(2,1)S(1)} %collective-permute-done.8.refs_8_.rest_1_), channel_id=1, source_target_pairs={{0,8},{1,9},{2,10},{3,11},{4,12},{5,13},{6,14},{7,15},{8,0},{9,1},... | collective-permute-start | bytes 3145736 | tf_op jit(solution)/shard_map/ppermute | solution.py:54
  59.2 5.0 %keys_part.5 = (f32[384,256]{1,0:T(8,128)S(1)}, f32[384,256]{1,0:T(8,128)S(1)}) custom-call(s32[16]{0:T(128)S(1)} %multiply_add_fusion.order_ref, bf16[384,8192]{1,0:T(8,128)(2,1)} %refs_1_.13, bf16[384,8192]{1,0:T(8,128)(2,1)} %refs_1_.13, bf16[384,8192]{1,0:T(8,128)(2,1)} %refs_1_.13, bf16[384,8192]{1,0:T(8,128)(2,1)} %refs_1_.13, ...), custom_call_target="tpu_custom_call" | custom-call | flops 1610612736 | bytes 6291456 | tf_op jit(solution)/shard_map/keys_part/pallas_call | solution.py:157
  64.6 1.6 %collective-permute-done.11.kt_ref = f32[384,256]{1,0:T(8,128)S(1)} collective-permute-done((f32[384,256]{1,0:T(8,128)S(1)}, f32[384,256]{1,0:T(8,128)S(1)}, u32[]{:S(2)}, u32[]{:S(2)}) %collective-permute-start.11) | collective-permute-done | bytes 393248 | tf_op jit(solution)/shard_map/ppermute | solution.py:54
  66.2 1.9 %copy-done.2 = bf16[384,4096]{1,0:T(8,128)(2,1)S(1)} copy-done((bf16[384,4096]{1,0:T(8,128)(2,1)S(1)}, bf16[384,4096]{1,0:T(8,128)(2,1)}, u32[]{:S(2)}) %copy-start.2) | copy-done | bytes 3145752
  68.1 13.4 %attention.1 = (bf16[384,4096]{1,0:T(8,128)(2,1)}, bf16[384,512]{1,0:T(8,128)(2,1)S(1)}, bf16[256,384]{1,0:T(8,128)(2,1)S(1)}, bf16[256,384]{1,0:T(8,128)(2,1)S(1)}, f32[384,1]{1,0:T(8,128)S(1)}) custom-call(bf16[384,4096]{1,0:T(8,128)(2,1)S(1)} %copy-done.1, f32[384,256]{1,0:T(8,128)S(1)} %get-tuple-element.61.ko_ref, ...), custom_call_target="tpu_custom_call" | custom-call | flops 3221225472 | bytes 9437184 | tf_op jit(solution)/shard_map/attention/pallas_call | solution.py:268
  83.1 3.2 %grad_part.7 = bf16[4,256,512]{2,1,0:T(8,128)(2,1)S(1)} custom-call(s32[16]{0:T(128)S(1)} %multiply_add_fusion.order_ref, bf16[384,8192]{1,0:T(8,128)(2,1)} %refs_1_.13, bf16[384,8192]{1,0:T(8,128)(2,1)} %refs_1_.13, bf16[384,8192]{1,0:T(8,128)(2,1)} %collective-permute-done.7.refs_4_.refs_5_.refs_6_.refs_7_.refs_2_.refs_3_, ...), custom_call_target="tpu_custom_call" | custom-call | flops 805306368 | bytes 3145728 | tf_op jit(solution)/shard_map/grad_part/pallas_call | solution.py:305
  86.7 3.2 %grad_part.6 = bf16[4,256,512]{2,1,0:T(8,128)(2,1)S(1)} custom-call(s32[16]{0:T(128)S(1)} %multiply_add_fusion.order_ref, bf16[384,8192]{1,0:T(8,128)(2,1)} %refs_1_.13, bf16[384,8192]{1,0:T(8,128)(2,1)} %refs_1_.13, bf16[384,8192]{1,0:T(8,128)(2,1)} %collective-permute-done.7.refs_4_.refs_5_.refs_6_.refs_7_.refs_2_.refs_3_, ...), custom_call_target="tpu_custom_call" | custom-call | flops 805306368 | bytes 3145728 | tf_op jit(solution)/shard_map/grad_part/pallas_call | solution.py:305
  91.2 3.2 %grad_part.5 = bf16[4,256,512]{2,1,0:T(8,128)(2,1)S(1)} custom-call(s32[16]{0:T(128)S(1)} %multiply_add_fusion.order_ref, bf16[384,8192]{1,0:T(8,128)(2,1)} %refs_1_.13, bf16[384,8192]{1,0:T(8,128)(2,1)} %refs_1_.13, bf16[384,8192]{1,0:T(8,128)(2,1)} %collective-permute-done.7.refs_4_.refs_5_.refs_6_.refs_7_.refs_2_.refs_3_, ...), custom_call_target="tpu_custom_call" | custom-call | flops 805306368 | bytes 3145728 | tf_op jit(solution)/shard_map/grad_part/pallas_call | solution.py:305
  95.1 11.9 %token_grad.1 = bf16[384,8192]{1,0:T(8,128)(2,1)} custom-call(s32[16]{0:T(128)S(1)} %fusion.10.place_ref, bf16[384,8192]{1,0:T(8,128)(2,1)} %refs_1_.13, bf16[384,512]{1,0:T(8,128)(2,1)S(1)} %get-tuple-element.67.dk_ref, bf16[4,512,256]{2,1,0:T(8,128)(2,1)S(1)} %pad_maximum_fusion.refs_8_.rest_0_, ...), custom_call_target="tpu_custom_call" | custom-call | flops 3221225472 | bytes 15728640 | tf_op jit(solution)/shard_map/token_grad/pallas_call | solution.py:355
  107.0 3.2 %grad_part.4 = bf16[4,256,512]{2,1,0:T(8,128)(2,1)S(1)} custom-call(s32[16]{0:T(128)S(1)} %multiply_add_fusion.order_ref, bf16[384,8192]{1,0:T(8,128)(2,1)} %refs_1_.13, bf16[384,8192]{1,0:T(8,128)(2,1)} %refs_1_.13, bf16[384,8192]{1,0:T(8,128)(2,1)} %collective-permute-done.7.refs_4_.refs_5_.refs_6_.refs_7_.refs_2_.refs_3_, ...), custom_call_target="tpu_custom_call" | custom-call | flops 805306368 | bytes 3145728 | tf_op jit(solution)/shard_map/grad_part/pallas_call | solution.py:305
  110.2 6.2 %collective-permute-done.18 = bf16[4,256,512]{2,1,0:T(8,128)(2,1)S(1)} collective-permute-done((bf16[4,256,512]{2,1,0:T(8,128)(2,1)S(1)}, bf16[4,256,512]{2,1,0:T(8,128)(2,1)S(1)}, u32[]{:S(2)}, u32[]{:S(2)}) %collective-permute-start.18) | collective-permute-done | bytes 1048608 | tf_op jit(solution)/shard_map/ppermute | solution.py:54
  118.6 3.3 %collective-permute-start.20 = (bf16[256,512]{1,0:T(8,128)(2,1)}, bf16[256,512]{1,0:T(8,128)(2,1)S(1)}, u32[]{:S(2)}, u32[]{:S(2)}) collective-permute-start(bf16[256,512]{1,0:T(8,128)(2,1)} %get-tuple-element.84), channel_id=1, source_target_pairs={{0,2},{1,3},{2,0},{3,1},{4,6},{5,7},{6,4},{7,5},{8,72},{9,73},{10,... | collective-permute-start | bytes 786440 | tf_op jit(solution)/shard_map/ppermute | solution.py:54
  121.9 2.7 %collective-permute-start.22 = (bf16[256,512]{1,0:T(8,128)(2,1)S(1)}, bf16[256,512]{1,0:T(8,128)(2,1)S(1)}, u32[]{:S(2)}, u32[]{:S(2)}) collective-permute-start(bf16[256,512]{1,0:T(8,128)(2,1)S(1)} %get-tuple-element.85), channel_id=1, source_target_pairs={{0,3},{1,0},{2,1},{3,2},{4,7},{5,4},{6,5},{7,6},{8,76},{9,77},{10,... | collective-permute-start | bytes 786440 | tf_op jit(solution)/shard_map/ppermute | solution.py:54
  124.6 1.6 %collective-permute-done.20 = bf16[256,512]{1,0:T(8,128)(2,1)S(1)} collective-permute-done((bf16[256,512]{1,0:T(8,128)(2,1)}, bf16[256,512]{1,0:T(8,128)(2,1)S(1)}, u32[]{:S(2)}, u32[]{:S(2)}) %collective-permute-start.20) | collective-permute-done | bytes 262176 | tf_op jit(solution)/shard_map/ppermute | solution.py:54
  126.1 2.8 %collective-permute-done.21 = bf16[256,512]{1,0:T(8,128)(2,1)S(1)} collective-permute-done((bf16[256,512]{1,0:T(8,128)(2,1)S(1)}, bf16[256,512]{1,0:T(8,128)(2,1)S(1)}, u32[]{:S(2)}, u32[]{:S(2)}) %collective-permute-start.21) | collective-permute-done | bytes 262176 | tf_op jit(solution)/shard_map/ppermute | solution.py:54
  131.3 2.5 %collective-permute-start.25 = (bf16[256,128]{1,0:T(8,128)(2,1)S(1)}, bf16[256,128]{1,0:T(8,128)(2,1)S(1)}, u32[]{:S(2)}, u32[]{:S(2)}) collective-permute-start(bf16[256,128]{1,0:T(8,128)(2,1)S(1)} %get-tuple-element.88), channel_id=1, source_target_pairs={{0,48},{1,49},{2,50},{3,51},{4,52},{5,53},{6,54},{7,55},{8,56},{9,... | collective-permute-start | bytes 196616 | tf_op jit(solution)/shard_map/ppermute | solution.py:54
  135.9 4.2 %collective-permute-start.26 = (f32[64,256]{0,1:T(8,128)S(1)}, f32[64,256]{0,1:T(8,128)S(1)}, u32[]{:S(2)}, u32[]{:S(2)}) collective-permute-start(f32[64,256]{0,1:T(8,128)S(1)} %get-tuple-element.97), channel_id=1, source_target_pairs={{0,8},{1,9},{2,10},{3,11},{4,12},{5,13},{6,14},{7,15},{8,0},{9,1},... | collective-permute-start | bytes 196616 | tf_op jit(solution)/shard_map/ppermute | solution.py:54
  (70 shorter events, 21.1 us)
Async XLA Ops:
  2.2 2.4 %collective-permute-start = (bf16[64,256]{1,0:T(8,128)(2,1)S(1)}, bf16[64,256]{1,0:T(8,128)(2,1)S(1)}, u32[]{:S(2)}, u32[]{:S(2)}) collective-permute-start(bf16[64,256]{1,0:T(8,128)(2,1)S(1)} %get-tuple-element.99), channel_id=1, source_target_pairs={{0,8},{1,9},{2,10},{3,11},{4,12},{5,13},{6,14},{7,15},{8,0},{9,1},... | collective-permute-start | bytes 98312 | tf_op jit(solution)/shard_map/ppermute | solution.py:54
  4.6 23.2 %collective-permute-start.7 = (bf16[384,8192]{1,0:T(8,128)(2,1)}, bf16[384,8192]{1,0:T(8,128)(2,1)}, u32[]{:S(2)}, u32[]{:S(2)}) collective-permute-start(bf16[384,8192]{1,0:T(8,128)(2,1)} %refs_1_.13), channel_id=1, source_target_pairs={{0,8},{1,9},{2,10},{3,11},{4,12},{5,13},{6,14},{7,15},{8,0},{9,1},... | collective-permute-start | bytes 18874376 | tf_op jit(solution)/shard_map/ppermute | solution.py:54
  5.0 4.0 %collective-permute-start.1 = (bf16[128,256]{1,0:T(8,128)(2,1)S(1)}, bf16[128,256]{1,0:T(8,128)(2,1)S(1)}, u32[]{:S(2)}, u32[]{:S(2)}) collective-permute-start(bf16[128,256]{1,0:T(8,128)(2,1)S(1)} %maximum_select_fusion.1), channel_id=1, source_target_pairs={{0,48},{1,49},{2,50},{3,51},{4,52},{5,53},{6,54},{7,55},{8,56},{9,... | collective-permute-start | bytes 196616 | tf_op jit(solution)/shard_map/ppermute | solution.py:54
  7.7 4.7 %collective-permute-start.2 = (bf16[128,256]{1,0:T(8,128)(2,1)S(1)}, bf16[128,256]{1,0:T(8,128)(2,1)S(1)}, u32[]{:S(2)}, u32[]{:S(2)}) collective-permute-start(bf16[128,256]{1,0:T(8,128)(2,1)S(1)} %maximum_select_fusion.1), channel_id=1, source_target_pairs={{0,32},{1,33},{2,34},{3,35},{4,36},{5,37},{6,38},{7,39},{8,40},{9,... | collective-permute-start | bytes 196616 | tf_op jit(solution)/shard_map/ppermute | solution.py:54
  8.2 6.0 %collective-permute-start.3 = (bf16[128,256]{1,0:T(8,128)(2,1)S(1)}, bf16[128,256]{1,0:T(8,128)(2,1)S(1)}, u32[]{:S(2)}, u32[]{:S(2)}) collective-permute-start(bf16[128,256]{1,0:T(8,128)(2,1)S(1)} %maximum_select_fusion.1), channel_id=1, source_target_pairs={{0,16},{1,17},{2,18},{3,19},{4,20},{5,21},{6,22},{7,23},{8,24},{9,... | collective-permute-start | bytes 196616 | tf_op jit(solution)/shard_map/ppermute | solution.py:54
  14.3 10.0 %collective-permute-start.4 = (bf16[512,256]{1,0:T(8,128)(2,1)S(1)}, bf16[512,256]{1,0:T(8,128)(2,1)S(1)}, u32[]{:S(2)}, u32[]{:S(2)}) collective-permute-start(bf16[512,256]{1,0:T(8,128)(2,1)S(1)} %get-tuple-element.91), channel_id=1, source_target_pairs={{0,3},{1,0},{2,1},{3,2},{4,7},{5,4},{6,5},{7,6},{8,76},{9,77},{10,... | collective-permute-start | bytes 786440 | tf_op jit(solution)/shard_map/ppermute | solution.py:54
  18.1 7.1 %collective-permute-start.5 = (bf16[512,256]{1,0:T(8,128)(2,1)S(1)}, bf16[512,256]{1,0:T(8,128)(2,1)S(1)}, u32[]{:S(2)}, u32[]{:S(2)}) collective-permute-start(bf16[512,256]{1,0:T(8,128)(2,1)S(1)} %get-tuple-element.91), channel_id=1, source_target_pairs={{0,2},{1,3},{2,0},{3,1},{4,6},{5,7},{6,4},{7,5},{8,72},{9,73},{10,... | collective-permute-start | bytes 786440 | tf_op jit(solution)/shard_map/ppermute | solution.py:54
  18.1 9.5 %collective-permute-start.6 = (bf16[512,256]{1,0:T(8,128)(2,1)S(1)}, bf16[512,256]{1,0:T(8,128)(2,1)S(1)}, u32[]{:S(2)}, u32[]{:S(2)}) collective-permute-start(bf16[512,256]{1,0:T(8,128)(2,1)S(1)} %get-tuple-element.91), channel_id=1, source_target_pairs={{0,1},{1,2},{2,3},{3,0},{4,5},{5,6},{6,7},{7,4},{8,12},{9,13},{10,... | collective-permute-start | bytes 786440 | tf_op jit(solution)/shard_map/ppermute | solution.py:54
  27.8 15.6 %collective-permute-start.10 = (bf16[4,512,256]{2,1,0:T(8,128)(2,1)S(1)}, bf16[4,512,256]{2,1,0:T(8,128)(2,1)S(1)}, u32[]{:S(2)}, u32[]{:S(2)}) collective-permute-start(bf16[4,512,256]{2,1,0:T(8,128)(2,1)S(1)} %pad_maximum_fusion.refs_8_.rest_0_), channel_id=1, source_target_pairs={{0,4},{1,5},{2,6},{3,7},{4,64},{5,65},{6,66},{7,67},{8,9},{9,10},{... | collective-permute-start | bytes 3145736 | tf_op jit(solution)/shard_map/ppermute | solution.py:54
  28.9 24.7 %collective-permute-start.8 = (bf16[4,512,256]{2,1,0:T(8,128)(2,1)S(1)}, bf16[4,512,256]{2,1,0:T(8,128)(2,1)S(1)}, u32[]{:S(2)}, u32[]{:S(2)}) collective-permute-start(bf16[4,512,256]{2,1,0:T(8,128)(2,1)S(1)} %pad_maximum_fusion.refs_8_.rest_0_), channel_id=1, source_target_pairs={{0,68},{1,69},{2,70},{3,71},{4,0},{5,1},{6,2},{7,3},{8,11},{9,8},{... | collective-permute-start | bytes 3145736 | tf_op jit(solution)/shard_map/ppermute | solution.py:54
  30.6 24.7 %collective-permute-start.9 = (bf16[4,512,256]{2,1,0:T(8,128)(2,1)S(1)}, bf16[4,512,256]{2,1,0:T(8,128)(2,1)S(1)}, u32[]{:S(2)}, u32[]{:S(2)}) collective-permute-start(bf16[4,512,256]{2,1,0:T(8,128)(2,1)S(1)} %pad_maximum_fusion.refs_8_.rest_0_), channel_id=1, source_target_pairs={{0,64},{1,65},{2,66},{3,67},{4,68},{5,69},{6,70},{7,71},{8,10},{9,... | collective-permute-start | bytes 3145736 | tf_op jit(solution)/shard_map/ppermute | solution.py:54
  32.0 49.6 %collective-permute-start.12 = (bf16[4,512,256]{2,1,0:T(8,128)(2,1)S(1)}, bf16[4,512,256]{2,1,0:T(8,128)(2,1)S(1)}, u32[]{:S(2)}, u32[]{:S(2)}) collective-permute-start(bf16[4,512,256]{2,1,0:T(8,128)(2,1)S(1)} %pad_maximum_fusion.refs_8_.rest_0_), channel_id=1, source_target_pairs={{0,8},{1,9},{2,10},{3,11},{4,12},{5,13},{6,14},{7,15},{8,0},{9,1},... | collective-permute-start | bytes 3145736 | tf_op jit(solution)/shard_map/ppermute | solution.py:54
  55.2 11.0 %copy-start.1 = (bf16[384,4096]{1,0:T(8,128)(2,1)S(1)}, bf16[384,4096]{1,0:T(8,128)(2,1)}, u32[]{:S(2)}) copy-start(bf16[384,4096]{1,0:T(8,128)(2,1)} %q_ref.1) | copy-start | bytes 9437188
  55.2 11.0 %copy-start.3 = (bf16[384,512]{1,0:T(8,128)(2,1)S(1)}, bf16[384,512]{1,0:T(8,128)(2,1)}, u32[]{:S(2)}) copy-start(bf16[384,512]{1,0:T(8,128)(2,1)} %v_ref.1) | copy-start | bytes 1179652
  55.2 26.3 %collective-permute-start.13 = (bf16[4,512,256]{2,1,0:T(8,128)(2,1)S(1)}, bf16[4,512,256]{2,1,0:T(8,128)(2,1)S(1)}, u32[]{:S(2)}, u32[]{:S(2)}) collective-permute-start(bf16[4,512,256]{2,1,0:T(8,128)(2,1)S(1)} %collective-permute-done.8.refs_8_.rest_1_), channel_id=1, source_target_pairs={{0,8},{1,9},{2,10},{3,11},{4,12},{5,13},{6,14},{7,15},{8,0},{9,1},... | collective-permute-start | bytes 3145736 | tf_op jit(solution)/shard_map/ppermute | solution.py:54
  58.7 22.9 %collective-permute-start.14 = (bf16[4,512,256]{2,1,0:T(8,128)(2,1)S(1)}, bf16[4,512,256]{2,1,0:T(8,128)(2,1)S(1)}, u32[]{:S(2)}, u32[]{:S(2)}) collective-permute-start(bf16[4,512,256]{2,1,0:T(8,128)(2,1)S(1)} %collective-permute-done.9.refs_9_.rest_2_), channel_id=1, source_target_pairs={{0,8},{1,9},{2,10},{3,11},{4,12},{5,13},{6,14},{7,15},{8,0},{9,1},... | collective-permute-start | bytes 3145736 | tf_op jit(solution)/shard_map/ppermute | solution.py:54
  58.7 22.8 %collective-permute-start.15 = (bf16[4,512,256]{2,1,0:T(8,128)(2,1)S(1)}, bf16[4,512,256]{2,1,0:T(8,128)(2,1)S(1)}, u32[]{:S(2)}, u32[]{:S(2)}) collective-permute-start(bf16[4,512,256]{2,1,0:T(8,128)(2,1)S(1)} %collective-permute-done.10.refs_8_.rest_3_), channel_id=1, source_target_pairs={{0,8},{1,9},{2,10},{3,11},{4,12},{5,13},{6,14},{7,15},{8,0},{9,1},... | collective-permute-start | bytes 3145736 | tf_op jit(solution)/shard_map/ppermute | solution.py:54
  64.2 2.0 %collective-permute-start.11 = (f32[384,256]{1,0:T(8,128)S(1)}, f32[384,256]{1,0:T(8,128)S(1)}, u32[]{:S(2)}, u32[]{:S(2)}) collective-permute-start(f32[384,256]{1,0:T(8,128)S(1)} %get-tuple-element.62), channel_id=1, source_target_pairs={{0,8},{1,9},{2,10},{3,11},{4,12},{5,13},{6,14},{7,15},{8,0},{9,1},... | collective-permute-start | bytes 1179656 | tf_op jit(solution)/shard_map/ppermute | solution.py:54
  81.5 4.8 %copy-start.4 = (bf16[4,512,256]{2,1,0:T(8,128)(2,1)}, bf16[4,512,256]{2,1,0:T(8,128)(2,1)S(1)}, u32[]{:S(2)}) copy-start(bf16[4,512,256]{2,1,0:T(8,128)(2,1)S(1)} %collective-permute-done.13.rest_5_) | copy-start | bytes 3145732
  81.6 4.8 %copy-start.5 = (bf16[4,512,256]{2,1,0:T(8,128)(2,1)}, bf16[4,512,256]{2,1,0:T(8,128)(2,1)S(1)}, u32[]{:S(2)}) copy-start(bf16[4,512,256]{2,1,0:T(8,128)(2,1)S(1)} %collective-permute-done.14.rest_6_) | copy-start | bytes 3145732
  81.6 4.8 %copy-start.6 = (bf16[4,512,256]{2,1,0:T(8,128)(2,1)}, bf16[4,512,256]{2,1,0:T(8,128)(2,1)S(1)}, u32[]{:S(2)}) copy-start(bf16[4,512,256]{2,1,0:T(8,128)(2,1)S(1)} %collective-permute-done.15.rest_7_) | copy-start | bytes 3145732
  81.6 1.5 %collective-permute-start.16 = (bf16[256,384]{1,0:T(8,128)(2,1)S(1)}, bf16[256,384]{1,0:T(8,128)(2,1)S(1)}, u32[]{:S(2)}, u32[]{:S(2)}) collective-permute-start(bf16[256,384]{1,0:T(8,128)(2,1)S(1)} %get-tuple-element.75), channel_id=1, source_target_pairs={{0,8},{1,9},{2,10},{3,11},{4,12},{5,13},{6,14},{7,15},{8,0},{9,1},... | collective-permute-start | bytes 589832 | tf_op jit(solution)/shard_map/ppermute | solution.py:54
  86.3 23.8 %collective-permute-start.19 = (bf16[4,256,512]{2,1,0:T(8,128)(2,1)S(1)}, bf16[4,256,512]{2,1,0:T(8,128)(2,1)S(1)}, u32[]{:S(2)}, u32[]{:S(2)}) collective-permute-start(bf16[4,256,512]{2,1,0:T(8,128)(2,1)S(1)} %grad_part.7), channel_id=1, source_target_pairs={{0,68},{1,69},{2,70},{3,71},{4,0},{5,1},{6,2},{7,3},{8,11},{9,8},{... | collective-permute-start | bytes 3145736 | tf_op jit(solution)/shard_map/ppermute | solution.py:54
  89.9 26.5 %collective-permute-start.18 = (bf16[4,256,512]{2,1,0:T(8,128)(2,1)S(1)}, bf16[4,256,512]{2,1,0:T(8,128)(2,1)S(1)}, u32[]{:S(2)}, u32[]{:S(2)}) collective-permute-start(bf16[4,256,512]{2,1,0:T(8,128)(2,1)S(1)} %grad_part.6), channel_id=1, source_target_pairs={{0,4},{1,5},{2,6},{3,7},{4,64},{5,65},{6,66},{7,67},{8,9},{9,10},{... | collective-permute-start | bytes 3145736 | tf_op jit(solution)/shard_map/ppermute | solution.py:54
  94.3 22.1 %collective-permute-start.17 = (bf16[4,256,512]{2,1,0:T(8,128)(2,1)S(1)}, bf16[4,256,512]{2,1,0:T(8,128)(2,1)S(1)}, u32[]{:S(2)}, u32[]{:S(2)}) collective-permute-start(bf16[4,256,512]{2,1,0:T(8,128)(2,1)S(1)} %grad_part.5), channel_id=1, source_target_pairs={{0,64},{1,65},{2,66},{3,67},{4,68},{5,69},{6,70},{7,71},{8,10},{9,... | collective-permute-start | bytes 3145736 | tf_op jit(solution)/shard_map/ppermute | solution.py:54
  118.6 7.6 %collective-permute-start.20 = (bf16[256,512]{1,0:T(8,128)(2,1)}, bf16[256,512]{1,0:T(8,128)(2,1)S(1)}, u32[]{:S(2)}, u32[]{:S(2)}) collective-permute-start(bf16[256,512]{1,0:T(8,128)(2,1)} %get-tuple-element.84), channel_id=1, source_target_pairs={{0,2},{1,3},{2,0},{3,1},{4,6},{5,7},{6,4},{7,5},{8,72},{9,73},{10,... | collective-permute-start | bytes 786440 | tf_op jit(solution)/shard_map/ppermute | solution.py:54
  121.9 7.1 %collective-permute-start.21 = (bf16[256,512]{1,0:T(8,128)(2,1)S(1)}, bf16[256,512]{1,0:T(8,128)(2,1)S(1)}, u32[]{:S(2)}, u32[]{:S(2)}) collective-permute-start(bf16[256,512]{1,0:T(8,128)(2,1)S(1)} %get-tuple-element.86), channel_id=1, source_target_pairs={{0,1},{1,2},{2,3},{3,0},{4,5},{5,6},{6,7},{7,4},{8,12},{9,13},{10,... | collective-permute-start | bytes 786440 | tf_op jit(solution)/shard_map/ppermute | solution.py:54
  121.9 7.1 %collective-permute-start.22 = (bf16[256,512]{1,0:T(8,128)(2,1)S(1)}, bf16[256,512]{1,0:T(8,128)(2,1)S(1)}, u32[]{:S(2)}, u32[]{:S(2)}) collective-permute-start(bf16[256,512]{1,0:T(8,128)(2,1)S(1)} %get-tuple-element.85), channel_id=1, source_target_pairs={{0,3},{1,0},{2,1},{3,2},{4,7},{5,4},{6,5},{7,6},{8,76},{9,77},{10,... | collective-permute-start | bytes 786440 | tf_op jit(solution)/shard_map/ppermute | solution.py:54
  130.3 4.7 %collective-permute-start.23 = (bf16[256,128]{1,0:T(8,128)(2,1)S(1)}, bf16[256,128]{1,0:T(8,128)(2,1)S(1)}, u32[]{:S(2)}, u32[]{:S(2)}) collective-permute-start(bf16[256,128]{1,0:T(8,128)(2,1)S(1)} %get-tuple-element.87), channel_id=1, source_target_pairs={{0,32},{1,33},{2,34},{3,35},{4,36},{5,37},{6,38},{7,39},{8,40},{9,... | collective-permute-start | bytes 196616 | tf_op jit(solution)/shard_map/ppermute | solution.py:54
  131.1 4.6 %collective-permute-start.24 = (bf16[256,128]{1,0:T(8,128)(2,1)S(1)}, bf16[256,128]{1,0:T(8,128)(2,1)S(1)}, u32[]{:S(2)}, u32[]{:S(2)}) collective-permute-start(bf16[256,128]{1,0:T(8,128)(2,1)S(1)} %get-tuple-element.89), channel_id=1, source_target_pairs={{0,16},{1,17},{2,18},{3,19},{4,20},{5,21},{6,22},{7,23},{8,24},{9,... | collective-permute-start | bytes 196616 | tf_op jit(solution)/shard_map/ppermute | solution.py:54
  131.3 4.4 %collective-permute-start.25 = (bf16[256,128]{1,0:T(8,128)(2,1)S(1)}, bf16[256,128]{1,0:T(8,128)(2,1)S(1)}, u32[]{:S(2)}, u32[]{:S(2)}) collective-permute-start(bf16[256,128]{1,0:T(8,128)(2,1)S(1)} %get-tuple-element.88), channel_id=1, source_target_pairs={{0,48},{1,49},{2,50},{3,51},{4,52},{5,53},{6,54},{7,55},{8,56},{9,... | collective-permute-start | bytes 196616 | tf_op jit(solution)/shard_map/ppermute | solution.py:54
  135.9 5.2 %collective-permute-start.26 = (f32[64,256]{0,1:T(8,128)S(1)}, f32[64,256]{0,1:T(8,128)S(1)}, u32[]{:S(2)}, u32[]{:S(2)}) collective-permute-start(f32[64,256]{0,1:T(8,128)S(1)} %get-tuple-element.97), channel_id=1, source_target_pairs={{0,8},{1,9},{2,10},{3,11},{4,12},{5,13},{6,14},{7,15},{8,0},{9,1},... | collective-permute-start | bytes 196616 | tf_op jit(solution)/shard_map/ppermute | solution.py:54
  (4 other events, 4.7 us)

commit v4 on v3

--- a/solution.py
+++ b/solution.py
@@ -16,7 +16,7 @@
 NT = (((1,), (1,)), ((), ()))
 BF16 = jnp.bfloat16
 VMEM_LIMIT = 48 * 1024 * 1024
-ATTENTION_LIMIT = 40 * 1024 * 1024
+ATTENTION_LIMIT = 52 * 1024 * 1024
 
 INDEX = np.arange(128).reshape(2, 4, 2, 2, 4)
 
@@ -55,7 +55,9 @@
 
 
 def collect(a, along):
-    two, right, left = (permute(a, along(d)) for d in (2, 1, -1))
+    two, right, left = lax.optimization_barrier(
+        tuple(permute(a, along(d)) for d in (2, 1, -1))
+    )
     return [a, left, two, right]
 
 
@@ -120,6 +122,7 @@
     cols = ws[0].shape[-1]
     first = acc is None
     n = len(ws)
+    by = rvs[1] - rvs[0] if n > 1 else 0
 
     def kernel(order_ref, *refs):
         tok_refs, w_refs = refs[:8], refs[8 : 8 + n]
@@ -149,7 +152,7 @@
                 add(w_refs[k][...], k == 0)
 
     tok = [
-        pl.BlockSpec((rows, BLK), lambda i, o, k=k: (0, o[(rvs[0] + i) * 4 + k])) for k in range(4)
+        pl.BlockSpec((rows, BLK), lambda i, o, k=k: (0, o[(rvs[0] + by * i) * 4 + k])) for k in range(4)
     ]
     whole = pl.BlockSpec((rows, cols), lambda i, o: (0, 0))
     wspec = pl.BlockSpec((4, BLK, cols), lambda i, o: (0, 0, 0))
@@ -412,14 +415,14 @@
     plane, tokens_now, tokens_sib, order, place = lax.optimization_barrier(
         (plane, tokens, tokens_sib, order, place)
     )
-    w_own = collect(plane, along_v)
+    w_own = [plane] + [permute(plane, along_v(d)) for d in (-1, 2, 1)]
 
     acc = keys_part(order, tokens, tokens_sib, w_own[:1], None, (0,))
     inv, bias = prepare(tokens_now, doc_ids)
-    w_own[3], inv, bias, *acc = lax.optimization_barrier((w_own[3], inv, bias, *acc))
-    acc = keys_part(order, tokens, tokens_sib, w_own[3:], acc, (3,))
-    w_own[1], w_own[2], *acc = lax.optimization_barrier((w_own[1], w_own[2], *acc))
-    keys_own, keys_sib = keys_part(order, tokens, tokens_sib, w_own[1:3], acc, (1, 2))
+    w_own[2], inv, bias, *acc = lax.optimization_barrier((w_own[2], inv, bias, *acc))
+    acc = keys_part(order, tokens, tokens_sib, w_own[2:3], acc, (2,))
+    w_own[3], w_own[1], *acc = lax.optimization_barrier((w_own[3], w_own[1], *acc))
+    keys_own, keys_sib = keys_part(order, tokens, tokens_sib, w_own[1::2], acc, (1, 3))
     keys_oth = permute(keys_sib, SWAP)
     w_sib = [permute(w, SWAP) for w in w_own]
 

time: 142 us -> 140 us (0.986)
  waiting for transfers between devices: 39.7 us -> 33.7 us
  starting transfers between devices: 38 us -> 42.5 us
  local copies, waits for them, and re-layouts: 4.72 us -> 2.84 us
    ppermute x27, waiting for transfers between devices: 39.7 us -> 33.7 us  [permute(): return lax.ppermute(a, AXES, perm)]
    ppermute x27, starting transfers between devices: 38 us -> 42.5 us  [permute(): return lax.ppermute(a, AXES, perm)]
    unnamed x19 -> x15, local copies, waits for them, and re-layouts: 4.37 us -> 2.48 us
  transfers between devices with their start and end apart: 27 -> 27, of which waited for: 17 -> 17; matrix products, arithmetic and copies ran while one was open for 0% -> 0% of each run, Pallas kernels for 36% -> 37%
where the time goes in v4:
time: 140 us; the launch traced here: 139 us
  Pallas kernels  55.2 us (39%)
  starting transfers between devices  42.5 us (30%)
  waiting for transfers between devices  33.7 us (24%)
  other arithmetic  4.34 us (3%)
  local copies, waits for them, and re-layouts  2.84 us (2%)
    ppermute x27, starting transfers between devices, permute(): return lax.ppermute(a, AXES, perm)  42.5 us
    ppermute x27, waiting for transfers between devices, permute(): return lax.ppermute(a, AXES, perm)  33.7 us
    pallas_call x1, Pallas kernels, attention(): pl.pallas_call(kernel, out_shape=(jax.ShapeDtypeStruct(queries.shape, BF1...  14.4 us
    pallas_call x4, Pallas kernels, grad_part(): pl.pallas_call(kernel, out_shape=jax.ShapeDtypeStruct((4, cols, BLK), BF1...  12.8 us
    pallas_call x1, Pallas kernels, token_grad(): pl.pallas_call(kernel, out_shape=jax.ShapeDtypeStruct(tokens.shape, BF16)...  11.9 us
    pallas_call x3, Pallas kernels, keys_part(): pl.pallas_call(kernel, out_shape=(out, out), grid_spec=pltpu.PrefetchScal...  11.8 us
    pallas_call x1, Pallas kernels, prepare(): pl.pallas_call(kernel, out_shape=(jax.ShapeDtypeStruct((rows, 1), F32), j...  4.32 us
  transfers between devices with their start and end apart: 27, of which 17 were waited for; matrix products, arithmetic and copies ran while one was open for 0% of the time, Pallas kernels for 37%

profile of v4, /device:TPU:1, one launch (start us, length us, event | category | flops | bytes accessed | tf_op | source)
XLA Modules:
  0.0 139.5 jit_solution(9553202248748233861)
XLA Ops:
  2.2 1.5 %collective-permute-start = (bf16[64,256]{1,0:T(8,128)(2,1)S(1)}, bf16[64,256]{1,0:T(8,128)(2,1)S(1)}, u32[]{:S(2)}, u32[]{:S(2)}) collective-permute-start(bf16[64,256]{1,0:T(8,128)(2,1)S(1)} %get-tuple-element.111), channel_id=1, source_target_pairs={{0,8},{1,9},{2,10},{3,11},{4,12},{5,13},{6,14},{7,15},{8,0},{9,1},... | collective-permute-start | bytes 98312 | tf_op jit(solution)/shard_map/ppermute | solution.py:54
  5.0 2.9 %collective-permute-start.1 = (bf16[128,256]{1,0:T(8,128)(2,1)S(1)}, bf16[128,256]{1,0:T(8,128)(2,1)S(1)}, u32[]{:S(2)}, u32[]{:S(2)}) collective-permute-start(bf16[128,256]{1,0:T(8,128)(2,1)S(1)} %maximum_select_fusion.1), channel_id=1, source_target_pairs={{0,32},{1,33},{2,34},{3,35},{4,36},{5,37},{6,38},{7,39},{8,40},{9,... | collective-permute-start | bytes 196616 | tf_op jit(solution)/shard_map/ppermute | solution.py:54
  8.3 2.4 %collective-permute-start.3 = (bf16[128,256]{1,0:T(8,128)(2,1)S(1)}, bf16[128,256]{1,0:T(8,128)(2,1)S(1)}, u32[]{:S(2)}, u32[]{:S(2)}) collective-permute-start(bf16[128,256]{1,0:T(8,128)(2,1)S(1)} %maximum_select_fusion.1), channel_id=1, source_target_pairs={{0,48},{1,49},{2,50},{3,51},{4,52},{5,53},{6,54},{7,55},{8,56},{9,... | collective-permute-start | bytes 196616 | tf_op jit(solution)/shard_map/ppermute | solution.py:54
  10.7 1.6 %collective-permute-done.2 = bf16[128,256]{1,0:T(8,128)(2,1)S(1)} collective-permute-done((bf16[128,256]{1,0:T(8,128)(2,1)S(1)}, bf16[128,256]{1,0:T(8,128)(2,1)S(1)}, u32[]{:S(2)}, u32[]{:S(2)}) %collective-permute-start.2) | collective-permute-done | bytes 65568 | tf_op jit(solution)/shard_map/ppermute | solution.py:54
  12.4 3.7 %collective-permute-start.4 = (bf16[512,256]{1,0:T(8,128)(2,1)S(1)}, bf16[512,256]{1,0:T(8,128)(2,1)S(1)}, u32[]{:S(2)}, u32[]{:S(2)}) collective-permute-start(bf16[512,256]{1,0:T(8,128)(2,1)S(1)} %get-tuple-element.103), channel_id=1, source_target_pairs={{0,2},{1,3},{2,0},{3,1},{4,6},{5,7},{6,4},{7,5},{8,72},{9,73},{10,... | collective-permute-start | bytes 786440 | tf_op jit(solution)/shard_map/ppermute | solution.py:54
  16.8 1.9 %collective-permute-start.6 = (bf16[512,256]{1,0:T(8,128)(2,1)S(1)}, bf16[512,256]{1,0:T(8,128)(2,1)S(1)}, u32[]{:S(2)}, u32[]{:S(2)}) collective-permute-start(bf16[512,256]{1,0:T(8,128)(2,1)S(1)} %get-tuple-element.103), channel_id=1, source_target_pairs={{0,3},{1,0},{2,1},{3,2},{4,7},{5,4},{6,5},{7,6},{8,76},{9,77},{10,... | collective-permute-start | bytes 786440 | tf_op jit(solution)/shard_map/ppermute | solution.py:54
  20.1 2.8 %collective-permute-done.5 = bf16[512,256]{1,0:T(8,128)(2,1)S(1)} collective-permute-done((bf16[512,256]{1,0:T(8,128)(2,1)S(1)}, bf16[512,256]{1,0:T(8,128)(2,1)S(1)}, u32[]{:S(2)}, u32[]{:S(2)}) %collective-permute-start.5) | collective-permute-done | bytes 262176 | tf_op jit(solution)/shard_map/ppermute | solution.py:54
  23.8 2.9 %collective-permute-start.10 = (bf16[4,512,256]{2,1,0:T(8,128)(2,1)S(1)}, bf16[4,512,256]{2,1,0:T(8,128)(2,1)S(1)}, u32[]{:S(2)}, u32[]{:S(2)}) collective-permute-start(bf16[4,512,256]{2,1,0:T(8,128)(2,1)S(1)} %pad_maximum_fusion.refs_8_.rest_0_), channel_id=1, source_target_pairs={{0,64},{1,65},{2,66},{3,67},{4,68},{5,69},{6,70},{7,71},{8,10},{9,... | collective-permute-start | bytes 3145736 | tf_op jit(solution)/shard_map/ppermute | solution.py:54
  27.2 2.2 %collective-permute-start.9 = (bf16[4,512,256]{2,1,0:T(8,128)(2,1)S(1)}, bf16[4,512,256]{2,1,0:T(8,128)(2,1)S(1)}, u32[]{:S(2)}, u32[]{:S(2)}) collective-permute-start(bf16[4,512,256]{2,1,0:T(8,128)(2,1)S(1)} %pad_maximum_fusion.refs_8_.rest_0_), channel_id=1, source_target_pairs={{0,68},{1,69},{2,70},{3,71},{4,0},{5,1},{6,2},{7,3},{8,11},{9,8},{... | collective-permute-start | bytes 3145736 | tf_op jit(solution)/shard_map/ppermute | solution.py:54
  29.4 3.0 %collective-permute-start.12 = (bf16[4,512,256]{2,1,0:T(8,128)(2,1)S(1)}, bf16[4,512,256]{2,1,0:T(8,128)(2,1)S(1)}, u32[]{:S(2)}, u32[]{:S(2)}) collective-permute-start(bf16[4,512,256]{2,1,0:T(8,128)(2,1)S(1)} %pad_maximum_fusion.refs_8_.rest_0_), channel_id=1, source_target_pairs={{0,8},{1,9},{2,10},{3,11},{4,12},{5,13},{6,14},{7,15},{8,0},{9,1},... | collective-permute-start | bytes 3145736 | tf_op jit(solution)/shard_map/ppermute | solution.py:54
  33.1 4.3 %prepare.1 = (f32[384,1]{1,0:T(8,128)S(1)}, f32[384,384]{1,0:T(8,128)S(1)}) custom-call(bf16[384,8192]{1,0:T(8,128)(2,1)} %refs_1_.13, s32[1,384]{1,0:T(1,128)S(1)} %copy-done), custom_call_target="tpu_custom_call" | custom-call | flops 9437184 | bytes 6291456 | tf_op jit(solution)/shard_map/prepare/pallas_call | solution.py:97
  37.4 3.4 %keys_part.3 = (f32[384,256]{1,0:T(8,128)S(1)}, f32[384,256]{1,0:T(8,128)S(1)}) custom-call(s32[16]{0:T(128)S(1)} %multiply_add_fusion.order_ref, bf16[384,8192]{1,0:T(8,128)(2,1)} %refs_1_.13, bf16[384,8192]{1,0:T(8,128)(2,1)} %refs_1_.13, bf16[384,8192]{1,0:T(8,128)(2,1)} %refs_1_.13, bf16[384,8192]{1,0:T(8,128)(2,1)} %refs_1_.13, ...), custom_call_target="tpu_custom_call" | custom-call | flops 805306368 | bytes 3145728 | tf_op jit(solution)/shard_map/keys_part/pallas_call | solution.py:160
  40.8 3.4 %keys_part.4 = (f32[384,256]{1,0:T(8,128)S(1)}, f32[384,256]{1,0:T(8,128)S(1)}) custom-call(s32[16]{0:T(128)S(1)} %multiply_add_fusion.order_ref, bf16[384,8192]{1,0:T(8,128)(2,1)} %refs_1_.13, bf16[384,8192]{1,0:T(8,128)(2,1)} %refs_1_.13, bf16[384,8192]{1,0:T(8,128)(2,1)} %refs_1_.13, bf16[384,8192]{1,0:T(8,128)(2,1)} %refs_1_.13, ...), custom_call_target="tpu_custom_call" | custom-call | flops 805306368 | bytes 3145728 | tf_op jit(solution)/shard_map/keys_part/pallas_call | solution.py:160
  44.2 6.3 %collective-permute-done.8.refs_9_.rest_3_ = bf16[4,512,256]{2,1,0:T(8,128)(2,1)S(1)} collective-permute-done((bf16[4,512,256]{2,1,0:T(8,128)(2,1)S(1)}, bf16[4,512,256]{2,1,0:T(8,128)(2,1)S(1)}, u32[]{:S(2)}, u32[]{:S(2)}) %collective-permute-start.8) | collective-permute-done | bytes 1048608 | tf_op jit(solution)/shard_map/ppermute | solution.py:54
  50.9 3.3 %collective-permute-start.13 = (bf16[4,512,256]{2,1,0:T(8,128)(2,1)S(1)}, bf16[4,512,256]{2,1,0:T(8,128)(2,1)S(1)}, u32[]{:S(2)}, u32[]{:S(2)}) collective-permute-start(bf16[4,512,256]{2,1,0:T(8,128)(2,1)S(1)} %collective-permute-done.9.refs_8_.rest_1_), channel_id=1, source_target_pairs={{0,8},{1,9},{2,10},{3,11},{4,12},{5,13},{6,14},{7,15},{8,0},{9,1},... | collective-permute-start | bytes 3145736 | tf_op jit(solution)/shard_map/ppermute | solution.py:54
  54.7 5.1 %keys_part.5 = (f32[384,256]{1,0:T(8,128)S(1)}, f32[384,256]{1,0:T(8,128)S(1)}) custom-call(s32[16]{0:T(128)S(1)} %multiply_add_fusion.order_ref, bf16[384,8192]{1,0:T(8,128)(2,1)} %refs_1_.13, bf16[384,8192]{1,0:T(8,128)(2,1)} %refs_1_.13, bf16[384,8192]{1,0:T(8,128)(2,1)} %refs_1_.13, bf16[384,8192]{1,0:T(8,128)(2,1)} %refs_1_.13, ...), custom_call_target="tpu_custom_call" | custom-call | flops 1610612736 | bytes 6291456 | tf_op jit(solution)/shard_map/keys_part/pallas_call | solution.py:160
  59.9 1.7 %collective-permute-done.11.kt_ref = f32[384,256]{1,0:T(8,128)S(1)} collective-permute-done((f32[384,256]{1,0:T(8,128)S(1)}, f32[384,256]{1,0:T(8,128)S(1)}, u32[]{:S(2)}, u32[]{:S(2)}) %collective-permute-start.11) | collective-permute-done | bytes 393248 | tf_op jit(solution)/shard_map/ppermute | solution.py:54
  61.6 14.4 %attention.1 = (bf16[384,4096]{1,0:T(8,128)(2,1)}, bf16[384,512]{1,0:T(8,128)(2,1)S(1)}, bf16[256,384]{1,0:T(8,128)(2,1)S(1)}, bf16[256,384]{1,0:T(8,128)(2,1)S(1)}, f32[384,1]{1,0:T(8,128)S(1)}) custom-call(bf16[384,4096]{1,0:T(8,128)(2,1)} %q_ref.1, f32[384,256]{1,0:T(8,128)S(1)} %get-tuple-element.73.ko_ref, ...), custom_call_target="tpu_custom_call" | custom-call | flops 3221225472 | bytes 9437184 | tf_op jit(solution)/shard_map/attention/pallas_call | solution.py:271
  77.8 3.2 %grad_part.7 = bf16[4,256,512]{2,1,0:T(8,128)(2,1)S(1)} custom-call(s32[16]{0:T(128)S(1)} %multiply_add_fusion.order_ref, bf16[384,8192]{1,0:T(8,128)(2,1)} %refs_1_.13, bf16[384,8192]{1,0:T(8,128)(2,1)} %refs_1_.13, bf16[384,8192]{1,0:T(8,128)(2,1)} %collective-permute-done.7.refs_4_.refs_5_.refs_6_.refs_7_.refs_2_.refs_3_, ...), custom_call_target="tpu_custom_call" | custom-call | flops 805306368 | bytes 3145728 | tf_op jit(solution)/shard_map/grad_part/pallas_call | solution.py:308
  81.0 2.7 %collective-permute-start.19 = (bf16[4,256,512]{2,1,0:T(8,128)(2,1)S(1)}, bf16[4,256,512]{2,1,0:T(8,128)(2,1)S(1)}, u32[]{:S(2)}, u32[]{:S(2)}) collective-permute-start(bf16[4,256,512]{2,1,0:T(8,128)(2,1)S(1)} %grad_part.7), channel_id=1, source_target_pairs={{0,68},{1,69},{2,70},{3,71},{4,0},{5,1},{6,2},{7,3},{8,11},{9,8},{... | collective-permute-start | bytes 3145736 | tf_op jit(solution)/shard_map/ppermute | solution.py:54
  83.7 3.2 %grad_part.6 = bf16[4,256,512]{2,1,0:T(8,128)(2,1)S(1)} custom-call(s32[16]{0:T(128)S(1)} %multiply_add_fusion.order_ref, bf16[384,8192]{1,0:T(8,128)(2,1)} %refs_1_.13, bf16[384,8192]{1,0:T(8,128)(2,1)} %refs_1_.13, bf16[384,8192]{1,0:T(8,128)(2,1)} %collective-permute-done.7.refs_4_.refs_5_.refs_6_.refs_7_.refs_2_.refs_3_, ...), custom_call_target="tpu_custom_call" | custom-call | flops 805306368 | bytes 3145728 | tf_op jit(solution)/shard_map/grad_part/pallas_call | solution.py:308
  87.1 3.2 %grad_part.5 = bf16[4,256,512]{2,1,0:T(8,128)(2,1)S(1)} custom-call(s32[16]{0:T(128)S(1)} %multiply_add_fusion.order_ref, bf16[384,8192]{1,0:T(8,128)(2,1)} %refs_1_.13, bf16[384,8192]{1,0:T(8,128)(2,1)} %refs_1_.13, bf16[384,8192]{1,0:T(8,128)(2,1)} %collective-permute-done.7.refs_4_.refs_5_.refs_6_.refs_7_.refs_2_.refs_3_, ...), custom_call_target="tpu_custom_call" | custom-call | flops 805306368 | bytes 3145728 | tf_op jit(solution)/shard_map/grad_part/pallas_call | solution.py:308
  91.5 11.9 %token_grad.1 = bf16[384,8192]{1,0:T(8,128)(2,1)} custom-call(s32[16]{0:T(128)S(1)} %fusion.10.place_ref, bf16[384,8192]{1,0:T(8,128)(2,1)} %refs_1_.13, bf16[384,512]{1,0:T(8,128)(2,1)S(1)} %get-tuple-element.79.dk_ref, bf16[4,512,256]{2,1,0:T(8,128)(2,1)S(1)} %pad_maximum_fusion.refs_8_.rest_0_, ...), custom_call_target="tpu_custom_call" | custom-call | flops 3221225472 | bytes 15728640 | tf_op jit(solution)/shard_map/token_grad/pallas_call | solution.py:358
  103.4 3.2 %grad_part.4 = bf16[4,256,512]{2,1,0:T(8,128)(2,1)S(1)} custom-call(s32[16]{0:T(128)S(1)} %multiply_add_fusion.order_ref, bf16[384,8192]{1,0:T(8,128)(2,1)} %refs_1_.13, bf16[384,8192]{1,0:T(8,128)(2,1)} %refs_1_.13, bf16[384,8192]{1,0:T(8,128)(2,1)} %collective-permute-done.7.refs_4_.refs_5_.refs_6_.refs_7_.refs_2_.refs_3_, ...), custom_call_target="tpu_custom_call" | custom-call | flops 805306368 | bytes 3145728 | tf_op jit(solution)/shard_map/grad_part/pallas_call | solution.py:308
  106.7 6.7 %collective-permute-done.18 = bf16[4,256,512]{2,1,0:T(8,128)(2,1)S(1)} collective-permute-done((bf16[4,256,512]{2,1,0:T(8,128)(2,1)S(1)}, bf16[4,256,512]{2,1,0:T(8,128)(2,1)S(1)}, u32[]{:S(2)}, u32[]{:S(2)}) %collective-permute-start.18) | collective-permute-done | bytes 1048608 | tf_op jit(solution)/shard_map/ppermute | solution.py:54
  115.6 1.5 %collective-permute-start.20 = (bf16[256,512]{1,0:T(8,128)(2,1)}, bf16[256,512]{1,0:T(8,128)(2,1)S(1)}, u32[]{:S(2)}, u32[]{:S(2)}) collective-permute-start(bf16[256,512]{1,0:T(8,128)(2,1)} %get-tuple-element.96), channel_id=1, source_target_pairs={{0,2},{1,3},{2,0},{3,1},{4,6},{5,7},{6,4},{7,5},{8,72},{9,73},{10,... | collective-permute-start | bytes 786440 | tf_op jit(solution)/shard_map/ppermute | solution.py:54
  118.2 1.6 %collective-permute-start.22 = (bf16[256,512]{1,0:T(8,128)(2,1)S(1)}, bf16[256,512]{1,0:T(8,128)(2,1)S(1)}, u32[]{:S(2)}, u32[]{:S(2)}) collective-permute-start(bf16[256,512]{1,0:T(8,128)(2,1)S(1)} %get-tuple-element.97), channel_id=1, source_target_pairs={{0,3},{1,0},{2,1},{3,2},{4,7},{5,4},{6,5},{7,6},{8,76},{9,77},{10,... | collective-permute-start | bytes 786440 | tf_op jit(solution)/shard_map/ppermute | solution.py:54
  119.7 3.1 %collective-permute-done.20 = bf16[256,512]{1,0:T(8,128)(2,1)S(1)} collective-permute-done((bf16[256,512]{1,0:T(8,128)(2,1)}, bf16[256,512]{1,0:T(8,128)(2,1)S(1)}, u32[]{:S(2)}, u32[]{:S(2)}) %collective-permute-start.20) | collective-permute-done | bytes 262176 | tf_op jit(solution)/shard_map/ppermute | solution.py:54
  122.8 2.8 %collective-permute-done.21 = bf16[256,512]{1,0:T(8,128)(2,1)S(1)} collective-permute-done((bf16[256,512]{1,0:T(8,128)(2,1)S(1)}, bf16[256,512]{1,0:T(8,128)(2,1)S(1)}, u32[]{:S(2)}, u32[]{:S(2)}) %collective-permute-start.21) | collective-permute-done | bytes 262176 | tf_op jit(solution)/shard_map/ppermute | solution.py:54
  128.2 2.4 %collective-permute-start.24 = (bf16[256,128]{1,0:T(8,128)(2,1)S(1)}, bf16[256,128]{1,0:T(8,128)(2,1)S(1)}, u32[]{:S(2)}, u32[]{:S(2)}) collective-permute-start(bf16[256,128]{1,0:T(8,128)(2,1)S(1)} %get-tuple-element.101), channel_id=1, source_target_pairs={{0,16},{1,17},{2,18},{3,19},{4,20},{5,21},{6,22},{7,23},{8,24},{9,... | collective-permute-start | bytes 196616 | tf_op jit(solution)/shard_map/ppermute | solution.py:54
  132.5 1.4 %collective-permute-done.25 = bf16[256,128]{1,0:T(8,128)(2,1)S(1)} collective-permute-done((bf16[256,128]{1,0:T(8,128)(2,1)S(1)}, bf16[256,128]{1,0:T(8,128)(2,1)S(1)}, u32[]{:S(2)}, u32[]{:S(2)}) %collective-permute-start.25) | collective-permute-done | bytes 65568 | tf_op jit(solution)/shard_map/ppermute | solution.py:54
  134.1 3.5 %collective-permute-start.26 = (f32[64,256]{0,1:T(8,128)S(1)}, f32[64,256]{0,1:T(8,128)S(1)}, u32[]{:S(2)}, u32[]{:S(2)}) collective-permute-start(f32[64,256]{0,1:T(8,128)S(1)} %get-tuple-element.109), channel_id=1, source_target_pairs={{0,8},{1,9},{2,10},{3,11},{4,12},{5,13},{6,14},{7,15},{8,0},{9,1},... | collective-permute-start | bytes 196616 | tf_op jit(solution)/shard_map/ppermute | solution.py:54
  (66 shorter events, 21.4 us)
Async XLA Ops:
  2.2 2.4 %collective-permute-start = (bf16[64,256]{1,0:T(8,128)(2,1)S(1)}, bf16[64,256]{1,0:T(8,128)(2,1)S(1)}, u32[]{:S(2)}, u32[]{:S(2)}) collective-permute-start(bf16[64,256]{1,0:T(8,128)(2,1)S(1)} %get-tuple-element.111), channel_id=1, source_target_pairs={{0,8},{1,9},{2,10},{3,11},{4,12},{5,13},{6,14},{7,15},{8,0},{9,1},... | collective-permute-start | bytes 98312 | tf_op jit(solution)/shard_map/ppermute | solution.py:54
  4.6 19.2 %collective-permute-start.7 = (bf16[384,8192]{1,0:T(8,128)(2,1)}, bf16[384,8192]{1,0:T(8,128)(2,1)}, u32[]{:S(2)}, u32[]{:S(2)}) collective-permute-start(bf16[384,8192]{1,0:T(8,128)(2,1)} %refs_1_.13), channel_id=1, source_target_pairs={{0,8},{1,9},{2,10},{3,11},{4,12},{5,13},{6,14},{7,15},{8,0},{9,1},... | collective-permute-start | bytes 18874376 | tf_op jit(solution)/shard_map/ppermute | solution.py:54
  5.0 5.7 %collective-permute-start.1 = (bf16[128,256]{1,0:T(8,128)(2,1)S(1)}, bf16[128,256]{1,0:T(8,128)(2,1)S(1)}, u32[]{:S(2)}, u32[]{:S(2)}) collective-permute-start(bf16[128,256]{1,0:T(8,128)(2,1)S(1)} %maximum_select_fusion.1), channel_id=1, source_target_pairs={{0,32},{1,33},{2,34},{3,35},{4,36},{5,37},{6,38},{7,39},{8,40},{9,... | collective-permute-start | bytes 196616 | tf_op jit(solution)/shard_map/ppermute | solution.py:54
  7.9 4.3 %collective-permute-start.2 = (bf16[128,256]{1,0:T(8,128)(2,1)S(1)}, bf16[128,256]{1,0:T(8,128)(2,1)S(1)}, u32[]{:S(2)}, u32[]{:S(2)}) collective-permute-start(bf16[128,256]{1,0:T(8,128)(2,1)S(1)} %maximum_select_fusion.1), channel_id=1, source_target_pairs={{0,16},{1,17},{2,18},{3,19},{4,20},{5,21},{6,22},{7,23},{8,24},{9,... | collective-permute-start | bytes 196616 | tf_op jit(solution)/shard_map/ppermute | solution.py:54
  8.3 4.0 %collective-permute-start.3 = (bf16[128,256]{1,0:T(8,128)(2,1)S(1)}, bf16[128,256]{1,0:T(8,128)(2,1)S(1)}, u32[]{:S(2)}, u32[]{:S(2)}) collective-permute-start(bf16[128,256]{1,0:T(8,128)(2,1)S(1)} %maximum_select_fusion.1), channel_id=1, source_target_pairs={{0,48},{1,49},{2,50},{3,51},{4,52},{5,53},{6,54},{7,55},{8,56},{9,... | collective-permute-start | bytes 196616 | tf_op jit(solution)/shard_map/ppermute | solution.py:54
  12.4 7.7 %collective-permute-start.4 = (bf16[512,256]{1,0:T(8,128)(2,1)S(1)}, bf16[512,256]{1,0:T(8,128)(2,1)S(1)}, u32[]{:S(2)}, u32[]{:S(2)}) collective-permute-start(bf16[512,256]{1,0:T(8,128)(2,1)S(1)} %get-tuple-element.103), channel_id=1, source_target_pairs={{0,2},{1,3},{2,0},{3,1},{4,6},{5,7},{6,4},{7,5},{8,72},{9,73},{10,... | collective-permute-start | bytes 786440 | tf_op jit(solution)/shard_map/ppermute | solution.py:54
  16.0 6.9 %collective-permute-start.5 = (bf16[512,256]{1,0:T(8,128)(2,1)S(1)}, bf16[512,256]{1,0:T(8,128)(2,1)S(1)}, u32[]{:S(2)}, u32[]{:S(2)}) collective-permute-start(bf16[512,256]{1,0:T(8,128)(2,1)S(1)} %get-tuple-element.103), channel_id=1, source_target_pairs={{0,1},{1,2},{2,3},{3,0},{4,5},{5,6},{6,7},{7,4},{8,12},{9,13},{10,... | collective-permute-start | bytes 786440 | tf_op jit(solution)/shard_map/ppermute | solution.py:54
  16.8 6.9 %collective-permute-start.6 = (bf16[512,256]{1,0:T(8,128)(2,1)S(1)}, bf16[512,256]{1,0:T(8,128)(2,1)S(1)}, u32[]{:S(2)}, u32[]{:S(2)}) collective-permute-start(bf16[512,256]{1,0:T(8,128)(2,1)S(1)} %get-tuple-element.103), channel_id=1, source_target_pairs={{0,3},{1,0},{2,1},{3,2},{4,7},{5,4},{6,5},{7,6},{8,76},{9,77},{10,... | collective-permute-start | bytes 786440 | tf_op jit(solution)/shard_map/ppermute | solution.py:54
  23.8 17.0 %collective-permute-start.10 = (bf16[4,512,256]{2,1,0:T(8,128)(2,1)S(1)}, bf16[4,512,256]{2,1,0:T(8,128)(2,1)S(1)}, u32[]{:S(2)}, u32[]{:S(2)}) collective-permute-start(bf16[4,512,256]{2,1,0:T(8,128)(2,1)S(1)} %pad_maximum_fusion.refs_8_.rest_0_), channel_id=1, source_target_pairs={{0,64},{1,65},{2,66},{3,67},{4,68},{5,69},{6,70},{7,71},{8,10},{9,... | collective-permute-start | bytes 3145736 | tf_op jit(solution)/shard_map/ppermute | solution.py:54
  26.7 23.9 %collective-permute-start.8 = (bf16[4,512,256]{2,1,0:T(8,128)(2,1)S(1)}, bf16[4,512,256]{2,1,0:T(8,128)(2,1)S(1)}, u32[]{:S(2)}, u32[]{:S(2)}) collective-permute-start(bf16[4,512,256]{2,1,0:T(8,128)(2,1)S(1)} %pad_maximum_fusion.refs_8_.rest_0_), channel_id=1, source_target_pairs={{0,4},{1,5},{2,6},{3,7},{4,64},{5,65},{6,66},{7,67},{8,9},{9,10},{... | collective-permute-start | bytes 3145736 | tf_op jit(solution)/shard_map/ppermute | solution.py:54
  27.2 23.8 %collective-permute-start.9 = (bf16[4,512,256]{2,1,0:T(8,128)(2,1)S(1)}, bf16[4,512,256]{2,1,0:T(8,128)(2,1)S(1)}, u32[]{:S(2)}, u32[]{:S(2)}) collective-permute-start(bf16[4,512,256]{2,1,0:T(8,128)(2,1)S(1)} %pad_maximum_fusion.refs_8_.rest_0_), channel_id=1, source_target_pairs={{0,68},{1,69},{2,70},{3,71},{4,0},{5,1},{6,2},{7,3},{8,11},{9,8},{... | collective-permute-start | bytes 3145736 | tf_op jit(solution)/shard_map/ppermute | solution.py:54
  29.4 46.6 %collective-permute-start.12 = (bf16[4,512,256]{2,1,0:T(8,128)(2,1)S(1)}, bf16[4,512,256]{2,1,0:T(8,128)(2,1)S(1)}, u32[]{:S(2)}, u32[]{:S(2)}) collective-permute-start(bf16[4,512,256]{2,1,0:T(8,128)(2,1)S(1)} %pad_maximum_fusion.refs_8_.rest_0_), channel_id=1, source_target_pairs={{0,8},{1,9},{2,10},{3,11},{4,12},{5,13},{6,14},{7,15},{8,0},{9,1},... | collective-permute-start | bytes 3145736 | tf_op jit(solution)/shard_map/ppermute | solution.py:54
  37.4 3.4 %copy-start.1 = (f32[384,384]{1,0:T(8,128)}, f32[384,384]{1,0:T(8,128)S(1)}, u32[]{:S(2)}) copy-start(f32[384,384]{1,0:T(8,128)S(1)} %get-tuple-element.76.bias) | copy-start | bytes 1769476
  50.9 25.1 %collective-permute-start.13 = (bf16[4,512,256]{2,1,0:T(8,128)(2,1)S(1)}, bf16[4,512,256]{2,1,0:T(8,128)(2,1)S(1)}, u32[]{:S(2)}, u32[]{:S(2)}) collective-permute-start(bf16[4,512,256]{2,1,0:T(8,128)(2,1)S(1)} %collective-permute-done.9.refs_8_.rest_1_), channel_id=1, source_target_pairs={{0,8},{1,9},{2,10},{3,11},{4,12},{5,13},{6,14},{7,15},{8,0},{9,1},... | collective-permute-start | bytes 3145736 | tf_op jit(solution)/shard_map/ppermute | solution.py:54
  54.2 21.8 %collective-permute-start.15 = (bf16[4,512,256]{2,1,0:T(8,128)(2,1)S(1)}, bf16[4,512,256]{2,1,0:T(8,128)(2,1)S(1)}, u32[]{:S(2)}, u32[]{:S(2)}) collective-permute-start(bf16[4,512,256]{2,1,0:T(8,128)(2,1)S(1)} %collective-permute-done.8.refs_9_.rest_3_), channel_id=1, source_target_pairs={{0,8},{1,9},{2,10},{3,11},{4,12},{5,13},{6,14},{7,15},{8,0},{9,1},... | collective-permute-start | bytes 3145736 | tf_op jit(solution)/shard_map/ppermute | solution.py:54
  54.2 21.8 %collective-permute-start.14 = (bf16[4,512,256]{2,1,0:T(8,128)(2,1)S(1)}, bf16[4,512,256]{2,1,0:T(8,128)(2,1)S(1)}, u32[]{:S(2)}, u32[]{:S(2)}) collective-permute-start(bf16[4,512,256]{2,1,0:T(8,128)(2,1)S(1)} %collective-permute-done.10.refs_8_.rest_2_), channel_id=1, source_target_pairs={{0,8},{1,9},{2,10},{3,11},{4,12},{5,13},{6,14},{7,15},{8,0},{9,1},... | collective-permute-start | bytes 3145736 | tf_op jit(solution)/shard_map/ppermute | solution.py:54
  59.8 1.8 %collective-permute-start.11 = (f32[384,256]{1,0:T(8,128)S(1)}, f32[384,256]{1,0:T(8,128)S(1)}, u32[]{:S(2)}, u32[]{:S(2)}) collective-permute-start(f32[384,256]{1,0:T(8,128)S(1)} %get-tuple-element.74), channel_id=1, source_target_pairs={{0,8},{1,9},{2,10},{3,11},{4,12},{5,13},{6,14},{7,15},{8,0},{9,1},... | collective-permute-start | bytes 1179656 | tf_op jit(solution)/shard_map/ppermute | solution.py:54
  76.0 5.0 %copy-start.2 = (bf16[4,512,256]{2,1,0:T(8,128)(2,1)}, bf16[4,512,256]{2,1,0:T(8,128)(2,1)S(1)}, u32[]{:S(2)}) copy-start(bf16[4,512,256]{2,1,0:T(8,128)(2,1)S(1)} %collective-permute-done.13.rest_5_) | copy-start | bytes 3145732
  76.0 4.9 %copy-start.3 = (bf16[4,512,256]{2,1,0:T(8,128)(2,1)}, bf16[4,512,256]{2,1,0:T(8,128)(2,1)S(1)}, u32[]{:S(2)}) copy-start(bf16[4,512,256]{2,1,0:T(8,128)(2,1)S(1)} %collective-permute-done.15.rest_7_) | copy-start | bytes 3145732
  76.0 4.9 %copy-start.4 = (bf16[4,512,256]{2,1,0:T(8,128)(2,1)}, bf16[4,512,256]{2,1,0:T(8,128)(2,1)S(1)}, u32[]{:S(2)}) copy-start(bf16[4,512,256]{2,1,0:T(8,128)(2,1)S(1)} %collective-permute-done.14.rest_6_) | copy-start | bytes 3145732
  76.1 1.7 %collective-permute-start.16 = (bf16[256,384]{1,0:T(8,128)(2,1)S(1)}, bf16[256,384]{1,0:T(8,128)(2,1)S(1)}, u32[]{:S(2)}, u32[]{:S(2)}) collective-permute-start(bf16[256,384]{1,0:T(8,128)(2,1)S(1)} %get-tuple-element.87), channel_id=1, source_target_pairs={{0,8},{1,9},{2,10},{3,11},{4,12},{5,13},{6,14},{7,15},{8,0},{9,1},... | collective-permute-start | bytes 589832 | tf_op jit(solution)/shard_map/ppermute | solution.py:54
  81.0 25.7 %collective-permute-start.19 = (bf16[4,256,512]{2,1,0:T(8,128)(2,1)S(1)}, bf16[4,256,512]{2,1,0:T(8,128)(2,1)S(1)}, u32[]{:S(2)}, u32[]{:S(2)}) collective-permute-start(bf16[4,256,512]{2,1,0:T(8,128)(2,1)S(1)} %grad_part.7), channel_id=1, source_target_pairs={{0,68},{1,69},{2,70},{3,71},{4,0},{5,1},{6,2},{7,3},{8,11},{9,8},{... | collective-permute-start | bytes 3145736 | tf_op jit(solution)/shard_map/ppermute | solution.py:54
  87.0 26.5 %collective-permute-start.18 = (bf16[4,256,512]{2,1,0:T(8,128)(2,1)S(1)}, bf16[4,256,512]{2,1,0:T(8,128)(2,1)S(1)}, u32[]{:S(2)}, u32[]{:S(2)}) collective-permute-start(bf16[4,256,512]{2,1,0:T(8,128)(2,1)S(1)} %grad_part.6), channel_id=1, source_target_pairs={{0,4},{1,5},{2,6},{3,7},{4,64},{5,65},{6,66},{7,67},{8,9},{9,10},{... | collective-permute-start | bytes 3145736 | tf_op jit(solution)/shard_map/ppermute | solution.py:54
  90.3 23.2 %collective-permute-start.17 = (bf16[4,256,512]{2,1,0:T(8,128)(2,1)S(1)}, bf16[4,256,512]{2,1,0:T(8,128)(2,1)S(1)}, u32[]{:S(2)}, u32[]{:S(2)}) collective-permute-start(bf16[4,256,512]{2,1,0:T(8,128)(2,1)S(1)} %grad_part.5), channel_id=1, source_target_pairs={{0,64},{1,65},{2,66},{3,67},{4,68},{5,69},{6,70},{7,71},{8,10},{9,... | collective-permute-start | bytes 3145736 | tf_op jit(solution)/shard_map/ppermute | solution.py:54
  114.4 1.1 copy-start.6
  115.6 7.3 %collective-permute-start.20 = (bf16[256,512]{1,0:T(8,128)(2,1)}, bf16[256,512]{1,0:T(8,128)(2,1)S(1)}, u32[]{:S(2)}, u32[]{:S(2)}) collective-permute-start(bf16[256,512]{1,0:T(8,128)(2,1)} %get-tuple-element.96), channel_id=1, source_target_pairs={{0,2},{1,3},{2,0},{3,1},{4,6},{5,7},{6,4},{7,5},{8,72},{9,73},{10,... | collective-permute-start | bytes 786440 | tf_op jit(solution)/shard_map/ppermute | solution.py:54
  117.1 8.5 %collective-permute-start.21 = (bf16[256,512]{1,0:T(8,128)(2,1)S(1)}, bf16[256,512]{1,0:T(8,128)(2,1)S(1)}, u32[]{:S(2)}, u32[]{:S(2)}) collective-permute-start(bf16[256,512]{1,0:T(8,128)(2,1)S(1)} %get-tuple-element.98), channel_id=1, source_target_pairs={{0,1},{1,2},{2,3},{3,0},{4,5},{5,6},{6,7},{7,4},{8,12},{9,13},{10,... | collective-permute-start | bytes 786440 | tf_op jit(solution)/shard_map/ppermute | solution.py:54
  118.2 7.4 %collective-permute-start.22 = (bf16[256,512]{1,0:T(8,128)(2,1)S(1)}, bf16[256,512]{1,0:T(8,128)(2,1)S(1)}, u32[]{:S(2)}, u32[]{:S(2)}) collective-permute-start(bf16[256,512]{1,0:T(8,128)(2,1)S(1)} %get-tuple-element.97), channel_id=1, source_target_pairs={{0,3},{1,0},{2,1},{3,2},{4,7},{5,4},{6,5},{7,6},{8,76},{9,77},{10,... | collective-permute-start | bytes 786440 | tf_op jit(solution)/shard_map/ppermute | solution.py:54
  126.9 4.7 %collective-permute-start.23 = (bf16[256,128]{1,0:T(8,128)(2,1)S(1)}, bf16[256,128]{1,0:T(8,128)(2,1)S(1)}, u32[]{:S(2)}, u32[]{:S(2)}) collective-permute-start(bf16[256,128]{1,0:T(8,128)(2,1)S(1)} %get-tuple-element.99), channel_id=1, source_target_pairs={{0,32},{1,33},{2,34},{3,35},{4,36},{5,37},{6,38},{7,39},{8,40},{9,... | collective-permute-start | bytes 196616 | tf_op jit(solution)/shard_map/ppermute | solution.py:54
  128.2 4.3 %collective-permute-start.24 = (bf16[256,128]{1,0:T(8,128)(2,1)S(1)}, bf16[256,128]{1,0:T(8,128)(2,1)S(1)}, u32[]{:S(2)}, u32[]{:S(2)}) collective-permute-start(bf16[256,128]{1,0:T(8,128)(2,1)S(1)} %get-tuple-element.101), channel_id=1, source_target_pairs={{0,16},{1,17},{2,18},{3,19},{4,20},{5,21},{6,22},{7,23},{8,24},{9,... | collective-permute-start | bytes 196616 | tf_op jit(solution)/shard_map/ppermute | solution.py:54
  130.6 3.4 %collective-permute-start.25 = (bf16[256,128]{1,0:T(8,128)(2,1)S(1)}, bf16[256,128]{1,0:T(8,128)(2,1)S(1)}, u32[]{:S(2)}, u32[]{:S(2)}) collective-permute-start(bf16[256,128]{1,0:T(8,128)(2,1)S(1)} %get-tuple-element.100), channel_id=1, source_target_pairs={{0,48},{1,49},{2,50},{3,51},{4,52},{5,53},{6,54},{7,55},{8,56},{9,... | collective-permute-start | bytes 196616 | tf_op jit(solution)/shard_map/ppermute | solution.py:54
  134.1 4.5 %collective-permute-start.26 = (f32[64,256]{0,1:T(8,128)S(1)}, f32[64,256]{0,1:T(8,128)S(1)}, u32[]{:S(2)}, u32[]{:S(2)}) collective-permute-start(f32[64,256]{0,1:T(8,128)S(1)} %get-tuple-element.109), channel_id=1, source_target_pairs={{0,8},{1,9},{2,10},{3,11},{4,12},{5,13},{6,14},{7,15},{8,0},{9,1},... | collective-permute-start | bytes 196616 | tf_op jit(solution)/shard_map/ppermute | solution.py:54
  (2 other events, 1.7 us)

commit v5 on v4

--- a/solution.py
+++ b/solution.py
@@ -437,7 +437,10 @@
         parts[r] = grad_part(order, tokens, tokens_sib, dkw_own, dkw_sib, r)
     arrived = distribute(parts, along_v)
     grad_tokens = token_grad(place, tokens, dk, w_own, w_sib, inv, ms)
-    grad_tokens, parts[0], *arrived = lax.optimization_barrier((grad_tokens, parts[0], *arrived))
+    two, right, left = arrived
+    grad_tokens, own, two = lax.optimization_barrier((grad_tokens, parts[0], two))
+    early = own.astype(F32) + two.astype(F32)
+    early, right, left = lax.optimization_barrier((early, right, left))
 
     def total(own, others):
         s = own.astype(F32)
@@ -445,7 +448,7 @@
             s = s + o.astype(F32)
         return s
 
-    chunk = [total(parts[0][r], [a[r] for a in arrived]) for r in range(4)]
+    chunk = [total(early[r], [right[r], left[r]]) for r in range(4)]
     arrived = distribute([c.astype(BF16) for c in chunk], along_u)
     line = total(chunk[0], arrived)
     by_x = [lax.dynamic_slice_in_dim(line, ((x + r) % 4) * HD, HD, 1) for r in range(4)]

time: 140 us -> 134 us (0.957)
  waiting for transfers between devices: 33.7 us -> 28.9 us
    ppermute x27, waiting for transfers between devices: 33.7 us -> 28.9 us  [permute(): return lax.ppermute(a, AXES, perm)]
  transfers between devices with their start and end apart: 27 -> 27, of which waited for: 17 -> 16; matrix products, arithmetic and copies ran while one was open for 0% -> 1% of each run, Pallas kernels for 37% -> 39%
where the time goes in v5:
time: 134 us
  Pallas kernels  55.1 us (41%)
  starting transfers between devices  42.2 us (31%)
  waiting for transfers between devices  28.9 us (22%)
  other arithmetic  4.59 us (3%)
  local copies, waits for them, and re-layouts  2.16 us (2%)
    ppermute x27, starting transfers between devices, permute(): return lax.ppermute(a, AXES, perm)  42.2 us
    ppermute x27, waiting for transfers between devices, permute(): return lax.ppermute(a, AXES, perm)  28.9 us
    pallas_call x1, Pallas kernels, attention(): pl.pallas_call(kernel, out_shape=(jax.ShapeDtypeStruct(queries.shape, BF1...  14.3 us
    pallas_call x4, Pallas kernels, grad_part(): pl.pallas_call(kernel, out_shape=jax.ShapeDtypeStruct((4, cols, BLK), BF1...  12.7 us
    pallas_call x1, Pallas kernels, token_grad(): pl.pallas_call(kernel, out_shape=jax.ShapeDtypeStruct(tokens.shape, BF16)...  11.9 us
    pallas_call x3, Pallas kernels, keys_part(): pl.pallas_call(kernel, out_shape=(out, out), grid_spec=pltpu.PrefetchScal...  11.8 us
    pallas_call x1, Pallas kernels, prepare(): pl.pallas_call(kernel, out_shape=(jax.ShapeDtypeStruct((rows, 1), F32), j...  4.32 us
  transfers between devices with their start and end apart: 27, of which 16 were waited for; matrix products, arithmetic and copies ran while one was open for 1% of the time, Pallas kernels for 39%

profile of v5, /device:TPU:1, one launch (start us, length us, event | category | flops | bytes accessed | tf_op | source)
XLA Modules:
  0.0 133.8 jit_solution(195946293007523843)
XLA Ops:
  2.2 1.5 %collective-permute-start = (bf16[64,256]{1,0:T(8,128)(2,1)S(1)}, bf16[64,256]{1,0:T(8,128)(2,1)S(1)}, u32[]{:S(2)}, u32[]{:S(2)}) collective-permute-start(bf16[64,256]{1,0:T(8,128)(2,1)S(1)} %get-tuple-element.113), channel_id=1, source_target_pairs={{0,8},{1,9},{2,10},{3,11},{4,12},{5,13},{6,14},{7,15},{8,0},{9,1},... | collective-permute-start | bytes 98312 | tf_op jit(solution)/shard_map/ppermute | solution.py:54
  5.0 2.9 %collective-permute-start.1 = (bf16[128,256]{1,0:T(8,128)(2,1)S(1)}, bf16[128,256]{1,0:T(8,128)(2,1)S(1)}, u32[]{:S(2)}, u32[]{:S(2)}) collective-permute-start(bf16[128,256]{1,0:T(8,128)(2,1)S(1)} %maximum_select_fusion.1), channel_id=1, source_target_pairs={{0,32},{1,33},{2,34},{3,35},{4,36},{5,37},{6,38},{7,39},{8,40},{9,... | collective-permute-start | bytes 196616 | tf_op jit(solution)/shard_map/ppermute | solution.py:54
  8.3 2.4 %collective-permute-start.3 = (bf16[128,256]{1,0:T(8,128)(2,1)S(1)}, bf16[128,256]{1,0:T(8,128)(2,1)S(1)}, u32[]{:S(2)}, u32[]{:S(2)}) collective-permute-start(bf16[128,256]{1,0:T(8,128)(2,1)S(1)} %maximum_select_fusion.1), channel_id=1, source_target_pairs={{0,48},{1,49},{2,50},{3,51},{4,52},{5,53},{6,54},{7,55},{8,56},{9,... | collective-permute-start | bytes 196616 | tf_op jit(solution)/shard_map/ppermute | solution.py:54
  10.7 1.6 %collective-permute-done.2 = bf16[128,256]{1,0:T(8,128)(2,1)S(1)} collective-permute-done((bf16[128,256]{1,0:T(8,128)(2,1)S(1)}, bf16[128,256]{1,0:T(8,128)(2,1)S(1)}, u32[]{:S(2)}, u32[]{:S(2)}) %collective-permute-start.2) | collective-permute-done | bytes 65568 | tf_op jit(solution)/shard_map/ppermute | solution.py:54
  12.4 3.7 %collective-permute-start.4 = (bf16[512,256]{1,0:T(8,128)(2,1)S(1)}, bf16[512,256]{1,0:T(8,128)(2,1)S(1)}, u32[]{:S(2)}, u32[]{:S(2)}) collective-permute-start(bf16[512,256]{1,0:T(8,128)(2,1)S(1)} %get-tuple-element.105), channel_id=1, source_target_pairs={{0,2},{1,3},{2,0},{3,1},{4,6},{5,7},{6,4},{7,5},{8,72},{9,73},{10,... | collective-permute-start | bytes 786440 | tf_op jit(solution)/shard_map/ppermute | solution.py:54
  16.8 1.9 %collective-permute-start.6 = (bf16[512,256]{1,0:T(8,128)(2,1)S(1)}, bf16[512,256]{1,0:T(8,128)(2,1)S(1)}, u32[]{:S(2)}, u32[]{:S(2)}) collective-permute-start(bf16[512,256]{1,0:T(8,128)(2,1)S(1)} %get-tuple-element.105), channel_id=1, source_target_pairs={{0,3},{1,0},{2,1},{3,2},{4,7},{5,4},{6,5},{7,6},{8,76},{9,77},{10,... | collective-permute-start | bytes 786440 | tf_op jit(solution)/shard_map/ppermute | solution.py:54
  20.1 2.8 %collective-permute-done.5 = bf16[512,256]{1,0:T(8,128)(2,1)S(1)} collective-permute-done((bf16[512,256]{1,0:T(8,128)(2,1)S(1)}, bf16[512,256]{1,0:T(8,128)(2,1)S(1)}, u32[]{:S(2)}, u32[]{:S(2)}) %collective-permute-start.5) | collective-permute-done | bytes 262176 | tf_op jit(solution)/shard_map/ppermute | solution.py:54
  23.8 2.9 %collective-permute-start.10 = (bf16[4,512,256]{2,1,0:T(8,128)(2,1)S(1)}, bf16[4,512,256]{2,1,0:T(8,128)(2,1)S(1)}, u32[]{:S(2)}, u32[]{:S(2)}) collective-permute-start(bf16[4,512,256]{2,1,0:T(8,128)(2,1)S(1)} %pad_maximum_fusion.refs_8_.rest_0_), channel_id=1, source_target_pairs={{0,64},{1,65},{2,66},{3,67},{4,68},{5,69},{6,70},{7,71},{8,10},{9,... | collective-permute-start | bytes 3145736 | tf_op jit(solution)/shard_map/ppermute | solution.py:54
  27.2 2.2 %collective-permute-start.9 = (bf16[4,512,256]{2,1,0:T(8,128)(2,1)S(1)}, bf16[4,512,256]{2,1,0:T(8,128)(2,1)S(1)}, u32[]{:S(2)}, u32[]{:S(2)}) collective-permute-start(bf16[4,512,256]{2,1,0:T(8,128)(2,1)S(1)} %pad_maximum_fusion.refs_8_.rest_0_), channel_id=1, source_target_pairs={{0,68},{1,69},{2,70},{3,71},{4,0},{5,1},{6,2},{7,3},{8,11},{9,8},{... | collective-permute-start | bytes 3145736 | tf_op jit(solution)/shard_map/ppermute | solution.py:54
  29.4 3.0 %collective-permute-start.12 = (bf16[4,512,256]{2,1,0:T(8,128)(2,1)S(1)}, bf16[4,512,256]{2,1,0:T(8,128)(2,1)S(1)}, u32[]{:S(2)}, u32[]{:S(2)}) collective-permute-start(bf16[4,512,256]{2,1,0:T(8,128)(2,1)S(1)} %pad_maximum_fusion.refs_8_.rest_0_), channel_id=1, source_target_pairs={{0,8},{1,9},{2,10},{3,11},{4,12},{5,13},{6,14},{7,15},{8,0},{9,1},... | collective-permute-start | bytes 3145736 | tf_op jit(solution)/shard_map/ppermute | solution.py:54
  32.4 4.3 %prepare.1 = (f32[384,1]{1,0:T(8,128)S(1)}, f32[384,384]{1,0:T(8,128)S(1)}) custom-call(bf16[384,8192]{1,0:T(8,128)(2,1)} %refs_1_.13, s32[1,384]{1,0:T(1,128)S(1)} %copy-done), custom_call_target="tpu_custom_call" | custom-call | flops 9437184 | bytes 6291456 | tf_op jit(solution)/shard_map/prepare/pallas_call | solution.py:97
  36.8 3.4 %keys_part.3 = (f32[384,256]{1,0:T(8,128)S(1)}, f32[384,256]{1,0:T(8,128)S(1)}) custom-call(s32[16]{0:T(128)S(1)} %multiply_add_fusion.order_ref, bf16[384,8192]{1,0:T(8,128)(2,1)} %refs_1_.13, bf16[384,8192]{1,0:T(8,128)(2,1)} %refs_1_.13, bf16[384,8192]{1,0:T(8,128)(2,1)} %refs_1_.13, bf16[384,8192]{1,0:T(8,128)(2,1)} %refs_1_.13, ...), custom_call_target="tpu_custom_call" | custom-call | flops 805306368 | bytes 3145728 | tf_op jit(solution)/shard_map/keys_part/pallas_call | solution.py:160
  40.2 3.4 %keys_part.4 = (f32[384,256]{1,0:T(8,128)S(1)}, f32[384,256]{1,0:T(8,128)S(1)}) custom-call(s32[16]{0:T(128)S(1)} %multiply_add_fusion.order_ref, bf16[384,8192]{1,0:T(8,128)(2,1)} %refs_1_.13, bf16[384,8192]{1,0:T(8,128)(2,1)} %refs_1_.13, bf16[384,8192]{1,0:T(8,128)(2,1)} %refs_1_.13, bf16[384,8192]{1,0:T(8,128)(2,1)} %refs_1_.13, ...), custom_call_target="tpu_custom_call" | custom-call | flops 805306368 | bytes 3145728 | tf_op jit(solution)/shard_map/keys_part/pallas_call | solution.py:160
  43.5 7.0 %collective-permute-done.8.refs_9_.rest_3_ = bf16[4,512,256]{2,1,0:T(8,128)(2,1)S(1)} collective-permute-done((bf16[4,512,256]{2,1,0:T(8,128)(2,1)S(1)}, bf16[4,512,256]{2,1,0:T(8,128)(2,1)S(1)}, u32[]{:S(2)}, u32[]{:S(2)}) %collective-permute-start.8) | collective-permute-done | bytes 1048608 | tf_op jit(solution)/shard_map/ppermute | solution.py:54
  50.9 3.3 %collective-permute-start.13 = (bf16[4,512,256]{2,1,0:T(8,128)(2,1)S(1)}, bf16[4,512,256]{2,1,0:T(8,128)(2,1)S(1)}, u32[]{:S(2)}, u32[]{:S(2)}) collective-permute-start(bf16[4,512,256]{2,1,0:T(8,128)(2,1)S(1)} %collective-permute-done.9.refs_8_.rest_1_), channel_id=1, source_target_pairs={{0,8},{1,9},{2,10},{3,11},{4,12},{5,13},{6,14},{7,15},{8,0},{9,1},... | collective-permute-start | bytes 3145736 | tf_op jit(solution)/shard_map/ppermute | solution.py:54
  54.8 5.1 %keys_part.5 = (f32[384,256]{1,0:T(8,128)S(1)}, f32[384,256]{1,0:T(8,128)S(1)}) custom-call(s32[16]{0:T(128)S(1)} %multiply_add_fusion.order_ref, bf16[384,8192]{1,0:T(8,128)(2,1)} %refs_1_.13, bf16[384,8192]{1,0:T(8,128)(2,1)} %refs_1_.13, bf16[384,8192]{1,0:T(8,128)(2,1)} %refs_1_.13, bf16[384,8192]{1,0:T(8,128)(2,1)} %refs_1_.13, ...), custom_call_target="tpu_custom_call" | custom-call | flops 1610612736 | bytes 6291456 | tf_op jit(solution)/shard_map/keys_part/pallas_call | solution.py:160
  59.9 1.7 %collective-permute-done.11.kt_ref = f32[384,256]{1,0:T(8,128)S(1)} collective-permute-done((f32[384,256]{1,0:T(8,128)S(1)}, f32[384,256]{1,0:T(8,128)S(1)}, u32[]{:S(2)}, u32[]{:S(2)}) %collective-permute-start.11) | collective-permute-done | bytes 393248 | tf_op jit(solution)/shard_map/ppermute | solution.py:54
  61.7 14.3 %attention.1 = (bf16[384,4096]{1,0:T(8,128)(2,1)}, bf16[384,512]{1,0:T(8,128)(2,1)S(1)}, bf16[256,384]{1,0:T(8,128)(2,1)S(1)}, bf16[256,384]{1,0:T(8,128)(2,1)S(1)}, f32[384,1]{1,0:T(8,128)S(1)}) custom-call(bf16[384,4096]{1,0:T(8,128)(2,1)} %q_ref.1, f32[384,256]{1,0:T(8,128)S(1)} %get-tuple-element.74.ko_ref, ...), custom_call_target="tpu_custom_call" | custom-call | flops 3221225472 | bytes 9437184 | tf_op jit(solution)/shard_map/attention/pallas_call | solution.py:271
  77.8 3.2 %grad_part.5 = bf16[4,256,512]{2,1,0:T(8,128)(2,1)S(1)} custom-call(s32[16]{0:T(128)S(1)} %multiply_add_fusion.order_ref, bf16[384,8192]{1,0:T(8,128)(2,1)} %refs_1_.13, bf16[384,8192]{1,0:T(8,128)(2,1)} %refs_1_.13, bf16[384,8192]{1,0:T(8,128)(2,1)} %collective-permute-done.7.refs_4_.refs_5_.refs_6_.refs_7_.refs_2_.refs_3_, ...), custom_call_target="tpu_custom_call" | custom-call | flops 805306368 | bytes 3145728 | tf_op jit(solution)/shard_map/grad_part/pallas_call | solution.py:308
  81.0 1.8 %collective-permute-start.17 = (bf16[4,256,512]{2,1,0:T(8,128)(2,1)S(1)}, bf16[4,256,512]{2,1,0:T(8,128)(2,1)S(1)}, u32[]{:S(2)}, u32[]{:S(2)}) collective-permute-start(bf16[4,256,512]{2,1,0:T(8,128)(2,1)S(1)} %grad_part.5), channel_id=1, source_target_pairs={{0,64},{1,65},{2,66},{3,67},{4,68},{5,69},{6,70},{7,71},{8,10},{9,... | collective-permute-start | bytes 3145736 | tf_op jit(solution)/shard_map/ppermute | solution.py:54
  82.8 3.2 %grad_part.7 = bf16[4,256,512]{2,1,0:T(8,128)(2,1)S(1)} custom-call(s32[16]{0:T(128)S(1)} %multiply_add_fusion.order_ref, bf16[384,8192]{1,0:T(8,128)(2,1)} %refs_1_.13, bf16[384,8192]{1,0:T(8,128)(2,1)} %refs_1_.13, bf16[384,8192]{1,0:T(8,128)(2,1)} %collective-permute-done.7.refs_4_.refs_5_.refs_6_.refs_7_.refs_2_.refs_3_, ...), custom_call_target="tpu_custom_call" | custom-call | flops 805306368 | bytes 3145728 | tf_op jit(solution)/shard_map/grad_part/pallas_call | solution.py:308
  86.0 1.8 %collective-permute-start.19 = (bf16[4,256,512]{2,1,0:T(8,128)(2,1)S(1)}, bf16[4,256,512]{2,1,0:T(8,128)(2,1)S(1)}, u32[]{:S(2)}, u32[]{:S(2)}) collective-permute-start(bf16[4,256,512]{2,1,0:T(8,128)(2,1)S(1)} %grad_part.7), channel_id=1, source_target_pairs={{0,68},{1,69},{2,70},{3,71},{4,0},{5,1},{6,2},{7,3},{8,11},{9,8},{... | collective-permute-start | bytes 3145736 | tf_op jit(solution)/shard_map/ppermute | solution.py:54
  87.8 3.2 %grad_part.6 = bf16[4,256,512]{2,1,0:T(8,128)(2,1)S(1)} custom-call(s32[16]{0:T(128)S(1)} %multiply_add_fusion.order_ref, bf16[384,8192]{1,0:T(8,128)(2,1)} %refs_1_.13, bf16[384,8192]{1,0:T(8,128)(2,1)} %refs_1_.13, bf16[384,8192]{1,0:T(8,128)(2,1)} %collective-permute-done.7.refs_4_.refs_5_.refs_6_.refs_7_.refs_2_.refs_3_, ...), custom_call_target="tpu_custom_call" | custom-call | flops 805306368 | bytes 3145728 | tf_op jit(solution)/shard_map/grad_part/pallas_call | solution.py:308
  91.1 11.9 %token_grad.1 = bf16[384,8192]{1,0:T(8,128)(2,1)} custom-call(s32[16]{0:T(128)S(1)} %fusion.10.place_ref, bf16[384,8192]{1,0:T(8,128)(2,1)} %refs_1_.13, bf16[384,512]{1,0:T(8,128)(2,1)S(1)} %get-tuple-element.80.dk_ref, bf16[4,512,256]{2,1,0:T(8,128)(2,1)S(1)} %pad_maximum_fusion.refs_8_.rest_0_, ...), custom_call_target="tpu_custom_call" | custom-call | flops 3221225472 | bytes 15728640 | tf_op jit(solution)/shard_map/token_grad/pallas_call | solution.py:358
  102.9 3.2 %grad_part.4 = bf16[4,256,512]{2,1,0:T(8,128)(2,1)S(1)} custom-call(s32[16]{0:T(128)S(1)} %multiply_add_fusion.order_ref, bf16[384,8192]{1,0:T(8,128)(2,1)} %refs_1_.13, bf16[384,8192]{1,0:T(8,128)(2,1)} %refs_1_.13, bf16[384,8192]{1,0:T(8,128)(2,1)} %collective-permute-done.7.refs_4_.refs_5_.refs_6_.refs_7_.refs_2_.refs_3_, ...), custom_call_target="tpu_custom_call" | custom-call | flops 805306368 | bytes 3145728 | tf_op jit(solution)/shard_map/grad_part/pallas_call | solution.py:308
  106.4 1.7 %collective-permute-done.19 = bf16[4,256,512]{2,1,0:T(8,128)(2,1)S(1)} collective-permute-done((bf16[4,256,512]{2,1,0:T(8,128)(2,1)S(1)}, bf16[4,256,512]{2,1,0:T(8,128)(2,1)S(1)}, u32[]{:S(2)}, u32[]{:S(2)}) %collective-permute-start.19) | collective-permute-done | bytes 1048608 | tf_op jit(solution)/shard_map/ppermute | solution.py:54
  110.2 1.8 %collective-permute-start.20 = (bf16[256,512]{1,0:T(8,128)(2,1)}, bf16[256,512]{1,0:T(8,128)(2,1)S(1)}, u32[]{:S(2)}, u32[]{:S(2)}) collective-permute-start(bf16[256,512]{1,0:T(8,128)(2,1)} %get-tuple-element.98), channel_id=1, source_target_pairs={{0,2},{1,3},{2,0},{3,1},{4,6},{5,7},{6,4},{7,5},{8,72},{9,73},{10,... | collective-permute-start | bytes 786440 | tf_op jit(solution)/shard_map/ppermute | solution.py:54
  113.1 1.6 %collective-permute-start.22 = (bf16[256,512]{1,0:T(8,128)(2,1)S(1)}, bf16[256,512]{1,0:T(8,128)(2,1)S(1)}, u32[]{:S(2)}, u32[]{:S(2)}) collective-permute-start(bf16[256,512]{1,0:T(8,128)(2,1)S(1)} %get-tuple-element.99), channel_id=1, source_target_pairs={{0,3},{1,0},{2,1},{3,2},{4,7},{5,4},{6,5},{7,6},{8,76},{9,77},{10,... | collective-permute-start | bytes 786440 | tf_op jit(solution)/shard_map/ppermute | solution.py:54
  114.7 2.8 %collective-permute-done.20 = bf16[256,512]{1,0:T(8,128)(2,1)S(1)} collective-permute-done((bf16[256,512]{1,0:T(8,128)(2,1)}, bf16[256,512]{1,0:T(8,128)(2,1)S(1)}, u32[]{:S(2)}, u32[]{:S(2)}) %collective-permute-start.20) | collective-permute-done | bytes 262176 | tf_op jit(solution)/shard_map/ppermute | solution.py:54
  117.4 2.8 %collective-permute-done.21 = bf16[256,512]{1,0:T(8,128)(2,1)S(1)} collective-permute-done((bf16[256,512]{1,0:T(8,128)(2,1)S(1)}, bf16[256,512]{1,0:T(8,128)(2,1)S(1)}, u32[]{:S(2)}, u32[]{:S(2)}) %collective-permute-start.21) | collective-permute-done | bytes 262176 | tf_op jit(solution)/shard_map/ppermute | solution.py:54
  122.8 2.3 %collective-permute-start.24 = (bf16[256,128]{1,0:T(8,128)(2,1)S(1)}, bf16[256,128]{1,0:T(8,128)(2,1)S(1)}, u32[]{:S(2)}, u32[]{:S(2)}) collective-permute-start(bf16[256,128]{1,0:T(8,128)(2,1)S(1)} %get-tuple-element.103), channel_id=1, source_target_pairs={{0,16},{1,17},{2,18},{3,19},{4,20},{5,21},{6,22},{7,23},{8,24},{9,... | collective-permute-start | bytes 196616 | tf_op jit(solution)/shard_map/ppermute | solution.py:54
  128.8 3.3 %collective-permute-start.26 = (f32[64,256]{0,1:T(8,128)S(1)}, f32[64,256]{0,1:T(8,128)S(1)}, u32[]{:S(2)}, u32[]{:S(2)}) collective-permute-start(f32[64,256]{0,1:T(8,128)S(1)} %get-tuple-element.111), channel_id=1, source_target_pairs={{0,8},{1,9},{2,10},{3,11},{4,12},{5,13},{6,14},{7,15},{8,0},{9,1},... | collective-permute-start | bytes 196616 | tf_op jit(solution)/shard_map/ppermute | solution.py:54
  (67 shorter events, 21.0 us)
Async XLA Ops:
  0.6 31.8 %copy-start = (s32[1,384]{1,0:T(1,128)S(1)}, s32[1,384]{1,0:T(1,128)}, u32[]{:S(2)}) copy-start(s32[1,384]{1,0:T(1,128)} %doc_ref.1) | copy-start | bytes 4612
  2.2 2.4 %collective-permute-start = (bf16[64,256]{1,0:T(8,128)(2,1)S(1)}, bf16[64,256]{1,0:T(8,128)(2,1)S(1)}, u32[]{:S(2)}, u32[]{:S(2)}) collective-permute-start(bf16[64,256]{1,0:T(8,128)(2,1)S(1)} %get-tuple-element.113), channel_id=1, source_target_pairs={{0,8},{1,9},{2,10},{3,11},{4,12},{5,13},{6,14},{7,15},{8,0},{9,1},... | collective-permute-start | bytes 98312 | tf_op jit(solution)/shard_map/ppermute | solution.py:54
  4.6 19.2 %collective-permute-start.7 = (bf16[384,8192]{1,0:T(8,128)(2,1)}, bf16[384,8192]{1,0:T(8,128)(2,1)}, u32[]{:S(2)}, u32[]{:S(2)}) collective-permute-start(bf16[384,8192]{1,0:T(8,128)(2,1)} %refs_1_.13), channel_id=1, source_target_pairs={{0,8},{1,9},{2,10},{3,11},{4,12},{5,13},{6,14},{7,15},{8,0},{9,1},... | collective-permute-start | bytes 18874376 | tf_op jit(solution)/shard_map/ppermute | solution.py:54
  5.0 5.7 %collective-permute-start.1 = (bf16[128,256]{1,0:T(8,128)(2,1)S(1)}, bf16[128,256]{1,0:T(8,128)(2,1)S(1)}, u32[]{:S(2)}, u32[]{:S(2)}) collective-permute-start(bf16[128,256]{1,0:T(8,128)(2,1)S(1)} %maximum_select_fusion.1), channel_id=1, source_target_pairs={{0,32},{1,33},{2,34},{3,35},{4,36},{5,37},{6,38},{7,39},{8,40},{9,... | collective-permute-start | bytes 196616 | tf_op jit(solution)/shard_map/ppermute | solution.py:54
  8.0 4.3 %collective-permute-start.2 = (bf16[128,256]{1,0:T(8,128)(2,1)S(1)}, bf16[128,256]{1,0:T(8,128)(2,1)S(1)}, u32[]{:S(2)}, u32[]{:S(2)}) collective-permute-start(bf16[128,256]{1,0:T(8,128)(2,1)S(1)} %maximum_select_fusion.1), channel_id=1, source_target_pairs={{0,16},{1,17},{2,18},{3,19},{4,20},{5,21},{6,22},{7,23},{8,24},{9,... | collective-permute-start | bytes 196616 | tf_op jit(solution)/shard_map/ppermute | solution.py:54
  8.3 4.0 %collective-permute-start.3 = (bf16[128,256]{1,0:T(8,128)(2,1)S(1)}, bf16[128,256]{1,0:T(8,128)(2,1)S(1)}, u32[]{:S(2)}, u32[]{:S(2)}) collective-permute-start(bf16[128,256]{1,0:T(8,128)(2,1)S(1)} %maximum_select_fusion.1), channel_id=1, source_target_pairs={{0,48},{1,49},{2,50},{3,51},{4,52},{5,53},{6,54},{7,55},{8,56},{9,... | collective-permute-start | bytes 196616 | tf_op jit(solution)/shard_map/ppermute | solution.py:54
  12.4 7.7 %collective-permute-start.4 = (bf16[512,256]{1,0:T(8,128)(2,1)S(1)}, bf16[512,256]{1,0:T(8,128)(2,1)S(1)}, u32[]{:S(2)}, u32[]{:S(2)}) collective-permute-start(bf16[512,256]{1,0:T(8,128)(2,1)S(1)} %get-tuple-element.105), channel_id=1, source_target_pairs={{0,2},{1,3},{2,0},{3,1},{4,6},{5,7},{6,4},{7,5},{8,72},{9,73},{10,... | collective-permute-start | bytes 786440 | tf_op jit(solution)/shard_map/ppermute | solution.py:54
  16.1 6.9 %collective-permute-start.5 = (bf16[512,256]{1,0:T(8,128)(2,1)S(1)}, bf16[512,256]{1,0:T(8,128)(2,1)S(1)}, u32[]{:S(2)}, u32[]{:S(2)}) collective-permute-start(bf16[512,256]{1,0:T(8,128)(2,1)S(1)} %get-tuple-element.105), channel_id=1, source_target_pairs={{0,1},{1,2},{2,3},{3,0},{4,5},{5,6},{6,7},{7,4},{8,12},{9,13},{10,... | collective-permute-start | bytes 786440 | tf_op jit(solution)/shard_map/ppermute | solution.py:54
  16.8 6.9 %collective-permute-start.6 = (bf16[512,256]{1,0:T(8,128)(2,1)S(1)}, bf16[512,256]{1,0:T(8,128)(2,1)S(1)}, u32[]{:S(2)}, u32[]{:S(2)}) collective-permute-start(bf16[512,256]{1,0:T(8,128)(2,1)S(1)} %get-tuple-element.105), channel_id=1, source_target_pairs={{0,3},{1,0},{2,1},{3,2},{4,7},{5,4},{6,5},{7,6},{8,76},{9,77},{10,... | collective-permute-start | bytes 786440 | tf_op jit(solution)/shard_map/ppermute | solution.py:54
  23.8 16.4 %collective-permute-start.10 = (bf16[4,512,256]{2,1,0:T(8,128)(2,1)S(1)}, bf16[4,512,256]{2,1,0:T(8,128)(2,1)S(1)}, u32[]{:S(2)}, u32[]{:S(2)}) collective-permute-start(bf16[4,512,256]{2,1,0:T(8,128)(2,1)S(1)} %pad_maximum_fusion.refs_8_.rest_0_), channel_id=1, source_target_pairs={{0,64},{1,65},{2,66},{3,67},{4,68},{5,69},{6,70},{7,71},{8,10},{9,... | collective-permute-start | bytes 3145736 | tf_op jit(solution)/shard_map/ppermute | solution.py:54
  26.7 23.9 %collective-permute-start.8 = (bf16[4,512,256]{2,1,0:T(8,128)(2,1)S(1)}, bf16[4,512,256]{2,1,0:T(8,128)(2,1)S(1)}, u32[]{:S(2)}, u32[]{:S(2)}) collective-permute-start(bf16[4,512,256]{2,1,0:T(8,128)(2,1)S(1)} %pad_maximum_fusion.refs_8_.rest_0_), channel_id=1, source_target_pairs={{0,4},{1,5},{2,6},{3,7},{4,64},{5,65},{6,66},{7,67},{8,9},{9,10},{... | collective-permute-start | bytes 3145736 | tf_op jit(solution)/shard_map/ppermute | solution.py:54
  27.2 23.8 %collective-permute-start.9 = (bf16[4,512,256]{2,1,0:T(8,128)(2,1)S(1)}, bf16[4,512,256]{2,1,0:T(8,128)(2,1)S(1)}, u32[]{:S(2)}, u32[]{:S(2)}) collective-permute-start(bf16[4,512,256]{2,1,0:T(8,128)(2,1)S(1)} %pad_maximum_fusion.refs_8_.rest_0_), channel_id=1, source_target_pairs={{0,68},{1,69},{2,70},{3,71},{4,0},{5,1},{6,2},{7,3},{8,11},{9,8},{... | collective-permute-start | bytes 3145736 | tf_op jit(solution)/shard_map/ppermute | solution.py:54
  29.4 46.6 %collective-permute-start.12 = (bf16[4,512,256]{2,1,0:T(8,128)(2,1)S(1)}, bf16[4,512,256]{2,1,0:T(8,128)(2,1)S(1)}, u32[]{:S(2)}, u32[]{:S(2)}) collective-permute-start(bf16[4,512,256]{2,1,0:T(8,128)(2,1)S(1)} %pad_maximum_fusion.refs_8_.rest_0_), channel_id=1, source_target_pairs={{0,8},{1,9},{2,10},{3,11},{4,12},{5,13},{6,14},{7,15},{8,0},{9,1},... | collective-permute-start | bytes 3145736 | tf_op jit(solution)/shard_map/ppermute | solution.py:54
  36.7 3.4 %copy-start.1 = (f32[384,384]{1,0:T(8,128)}, f32[384,384]{1,0:T(8,128)S(1)}, u32[]{:S(2)}) copy-start(f32[384,384]{1,0:T(8,128)S(1)} %get-tuple-element.77.bias) | copy-start | bytes 1769476
  50.9 25.1 %collective-permute-start.13 = (bf16[4,512,256]{2,1,0:T(8,128)(2,1)S(1)}, bf16[4,512,256]{2,1,0:T(8,128)(2,1)S(1)}, u32[]{:S(2)}, u32[]{:S(2)}) collective-permute-start(bf16[4,512,256]{2,1,0:T(8,128)(2,1)S(1)} %collective-permute-done.9.refs_8_.rest_1_), channel_id=1, source_target_pairs={{0,8},{1,9},{2,10},{3,11},{4,12},{5,13},{6,14},{7,15},{8,0},{9,1},... | collective-permute-start | bytes 3145736 | tf_op jit(solution)/shard_map/ppermute | solution.py:54
  54.2 21.8 %collective-permute-start.15 = (bf16[4,512,256]{2,1,0:T(8,128)(2,1)S(1)}, bf16[4,512,256]{2,1,0:T(8,128)(2,1)S(1)}, u32[]{:S(2)}, u32[]{:S(2)}) collective-permute-start(bf16[4,512,256]{2,1,0:T(8,128)(2,1)S(1)} %collective-permute-done.8.refs_9_.rest_3_), channel_id=1, source_target_pairs={{0,8},{1,9},{2,10},{3,11},{4,12},{5,13},{6,14},{7,15},{8,0},{9,1},... | collective-permute-start | bytes 3145736 | tf_op jit(solution)/shard_map/ppermute | solution.py:54
  54.2 21.8 %collective-permute-start.14 = (bf16[4,512,256]{2,1,0:T(8,128)(2,1)S(1)}, bf16[4,512,256]{2,1,0:T(8,128)(2,1)S(1)}, u32[]{:S(2)}, u32[]{:S(2)}) collective-permute-start(bf16[4,512,256]{2,1,0:T(8,128)(2,1)S(1)} %collective-permute-done.10.refs_8_.rest_2_), channel_id=1, source_target_pairs={{0,8},{1,9},{2,10},{3,11},{4,12},{5,13},{6,14},{7,15},{8,0},{9,1},... | collective-permute-start | bytes 3145736 | tf_op jit(solution)/shard_map/ppermute | solution.py:54
  59.9 1.8 %collective-permute-start.11 = (f32[384,256]{1,0:T(8,128)S(1)}, f32[384,256]{1,0:T(8,128)S(1)}, u32[]{:S(2)}, u32[]{:S(2)}) collective-permute-start(f32[384,256]{1,0:T(8,128)S(1)} %get-tuple-element.75), channel_id=1, source_target_pairs={{0,8},{1,9},{2,10},{3,11},{4,12},{5,13},{6,14},{7,15},{8,0},{9,1},... | collective-permute-start | bytes 1179656 | tf_op jit(solution)/shard_map/ppermute | solution.py:54
  76.0 4.9 %copy-start.2 = (bf16[4,512,256]{2,1,0:T(8,128)(2,1)}, bf16[4,512,256]{2,1,0:T(8,128)(2,1)S(1)}, u32[]{:S(2)}) copy-start(bf16[4,512,256]{2,1,0:T(8,128)(2,1)S(1)} %collective-permute-done.13.rest_5_) | copy-start | bytes 3145732
  76.0 4.9 %copy-start.3 = (bf16[4,512,256]{2,1,0:T(8,128)(2,1)}, bf16[4,512,256]{2,1,0:T(8,128)(2,1)S(1)}, u32[]{:S(2)}) copy-start(bf16[4,512,256]{2,1,0:T(8,128)(2,1)S(1)} %collective-permute-done.15.rest_7_) | copy-start | bytes 3145732
  76.0 4.9 %copy-start.4 = (bf16[4,512,256]{2,1,0:T(8,128)(2,1)}, bf16[4,512,256]{2,1,0:T(8,128)(2,1)S(1)}, u32[]{:S(2)}) copy-start(bf16[4,512,256]{2,1,0:T(8,128)(2,1)S(1)} %collective-permute-done.14.rest_6_) | copy-start | bytes 3145732
  76.1 1.7 %collective-permute-start.16 = (bf16[256,384]{1,0:T(8,128)(2,1)S(1)}, bf16[256,384]{1,0:T(8,128)(2,1)S(1)}, u32[]{:S(2)}, u32[]{:S(2)}) collective-permute-start(bf16[256,384]{1,0:T(8,128)(2,1)S(1)} %get-tuple-element.88), channel_id=1, source_target_pairs={{0,8},{1,9},{2,10},{3,11},{4,12},{5,13},{6,14},{7,15},{8,0},{9,1},... | collective-permute-start | bytes 589832 | tf_op jit(solution)/shard_map/ppermute | solution.py:54
  81.0 25.2 %collective-permute-start.17 = (bf16[4,256,512]{2,1,0:T(8,128)(2,1)S(1)}, bf16[4,256,512]{2,1,0:T(8,128)(2,1)S(1)}, u32[]{:S(2)}, u32[]{:S(2)}) collective-permute-start(bf16[4,256,512]{2,1,0:T(8,128)(2,1)S(1)} %grad_part.5), channel_id=1, source_target_pairs={{0,64},{1,65},{2,66},{3,67},{4,68},{5,69},{6,70},{7,71},{8,10},{9,... | collective-permute-start | bytes 3145736 | tf_op jit(solution)/shard_map/ppermute | solution.py:54
  86.0 22.1 %collective-permute-start.19 = (bf16[4,256,512]{2,1,0:T(8,128)(2,1)S(1)}, bf16[4,256,512]{2,1,0:T(8,128)(2,1)S(1)}, u32[]{:S(2)}, u32[]{:S(2)}) collective-permute-start(bf16[4,256,512]{2,1,0:T(8,128)(2,1)S(1)} %grad_part.7), channel_id=1, source_target_pairs={{0,68},{1,69},{2,70},{3,71},{4,0},{5,1},{6,2},{7,3},{8,11},{9,8},{... | collective-permute-start | bytes 3145736 | tf_op jit(solution)/shard_map/ppermute | solution.py:54
  91.0 17.1 %collective-permute-start.18 = (bf16[4,256,512]{2,1,0:T(8,128)(2,1)S(1)}, bf16[4,256,512]{2,1,0:T(8,128)(2,1)S(1)}, u32[]{:S(2)}, u32[]{:S(2)}) collective-permute-start(bf16[4,256,512]{2,1,0:T(8,128)(2,1)S(1)} %grad_part.6), channel_id=1, source_target_pairs={{0,4},{1,5},{2,6},{3,7},{4,64},{5,65},{6,66},{7,67},{8,9},{9,10},{... | collective-permute-start | bytes 3145736 | tf_op jit(solution)/shard_map/ppermute | solution.py:54
  110.2 7.2 %collective-permute-start.20 = (bf16[256,512]{1,0:T(8,128)(2,1)}, bf16[256,512]{1,0:T(8,128)(2,1)S(1)}, u32[]{:S(2)}, u32[]{:S(2)}) collective-permute-start(bf16[256,512]{1,0:T(8,128)(2,1)} %get-tuple-element.98), channel_id=1, source_target_pairs={{0,2},{1,3},{2,0},{3,1},{4,6},{5,7},{6,4},{7,5},{8,72},{9,73},{10,... | collective-permute-start | bytes 786440 | tf_op jit(solution)/shard_map/ppermute | solution.py:54
  112.0 8.2 %collective-permute-start.21 = (bf16[256,512]{1,0:T(8,128)(2,1)S(1)}, bf16[256,512]{1,0:T(8,128)(2,1)S(1)}, u32[]{:S(2)}, u32[]{:S(2)}) collective-permute-start(bf16[256,512]{1,0:T(8,128)(2,1)S(1)} %get-tuple-element.100), channel_id=1, source_target_pairs={{0,1},{1,2},{2,3},{3,0},{4,5},{5,6},{6,7},{7,4},{8,12},{9,13},{10,... | collective-permute-start | bytes 786440 | tf_op jit(solution)/shard_map/ppermute | solution.py:54
  113.1 7.1 %collective-permute-start.22 = (bf16[256,512]{1,0:T(8,128)(2,1)S(1)}, bf16[256,512]{1,0:T(8,128)(2,1)S(1)}, u32[]{:S(2)}, u32[]{:S(2)}) collective-permute-start(bf16[256,512]{1,0:T(8,128)(2,1)S(1)} %get-tuple-element.99), channel_id=1, source_target_pairs={{0,3},{1,0},{2,1},{3,2},{4,7},{5,4},{6,5},{7,6},{8,76},{9,77},{10,... | collective-permute-start | bytes 786440 | tf_op jit(solution)/shard_map/ppermute | solution.py:54
  121.6 4.7 %collective-permute-start.23 = (bf16[256,128]{1,0:T(8,128)(2,1)S(1)}, bf16[256,128]{1,0:T(8,128)(2,1)S(1)}, u32[]{:S(2)}, u32[]{:S(2)}) collective-permute-start(bf16[256,128]{1,0:T(8,128)(2,1)S(1)} %get-tuple-element.101), channel_id=1, source_target_pairs={{0,32},{1,33},{2,34},{3,35},{4,36},{5,37},{6,38},{7,39},{8,40},{9,... | collective-permute-start | bytes 196616 | tf_op jit(solution)/shard_map/ppermute | solution.py:54
  122.8 4.3 %collective-permute-start.24 = (bf16[256,128]{1,0:T(8,128)(2,1)S(1)}, bf16[256,128]{1,0:T(8,128)(2,1)S(1)}, u32[]{:S(2)}, u32[]{:S(2)}) collective-permute-start(bf16[256,128]{1,0:T(8,128)(2,1)S(1)} %get-tuple-element.103), channel_id=1, source_target_pairs={{0,16},{1,17},{2,18},{3,19},{4,20},{5,21},{6,22},{7,23},{8,24},{9,... | collective-permute-start | bytes 196616 | tf_op jit(solution)/shard_map/ppermute | solution.py:54
  125.2 3.4 %collective-permute-start.25 = (bf16[256,128]{1,0:T(8,128)(2,1)S(1)}, bf16[256,128]{1,0:T(8,128)(2,1)S(1)}, u32[]{:S(2)}, u32[]{:S(2)}) collective-permute-start(bf16[256,128]{1,0:T(8,128)(2,1)S(1)} %get-tuple-element.102), channel_id=1, source_target_pairs={{0,48},{1,49},{2,50},{3,51},{4,52},{5,53},{6,54},{7,55},{8,56},{9,... | collective-permute-start | bytes 196616 | tf_op jit(solution)/shard_map/ppermute | solution.py:54
  128.8 4.3 %collective-permute-start.26 = (f32[64,256]{0,1:T(8,128)S(1)}, f32[64,256]{0,1:T(8,128)S(1)}, u32[]{:S(2)}, u32[]{:S(2)}) collective-permute-start(f32[64,256]{0,1:T(8,128)S(1)} %get-tuple-element.111), channel_id=1, source_target_pairs={{0,8},{1,9},{2,10},{3,11},{4,12},{5,13},{6,14},{7,15},{8,0},{9,1},... | collective-permute-start | bytes 196616 | tf_op jit(solution)/shard_map/ppermute | solution.py:54
  (2 other events, 2.1 us)
